TPU v7x, 128 devices: a whole 4x4x4 slice. The times are simulated.
128 devices in a mesh: dp: 16 (over z, x_hi, core), ctx: 8 (over x_lo, y).
Axes of the slice: x: 4 (x_hi: 2, x_lo: 2; x = x_hi * 2 + x_lo), y: 4, z: 4, core: 2. Of those that a mesh axis runs over, the one named last changes fastest.
Arguments:
- queries: bfloat16 [16, 1024, 2048], P('dp', 'ctx'), may hold values from -5 to 5
- keys: bfloat16 [16, 1024, 2048], P('dp', 'ctx'), may hold values from -5 to 5
- values: bfloat16 [16, 1024, 2048], P('dp', 'ctx'), may hold values from -12 to 12
- out_weight: bfloat16 [2048, 2048], P(('dp', 'ctx')), may hold values from -0.5 to 0.5
- cotangent: bfloat16 [16, 1024, 2048], P('dp', 'ctx'), may hold values from -6 to 6
- rand_blocks: int32 [16, 16, 16, 3], P('dp', 'ctx'), may hold values from 0 to 15
- glob_blocks: int32 [16, 2], P('dp'), may hold values from 0 to 15
Outputs:
- mixed: bfloat16 [16, 1024, 2048], P('dp', 'ctx')
- grad_queries: bfloat16 [16, 1024, 2048], P('dp', 'ctx')
- grad_keys: bfloat16 [16, 1024, 2048], P('dp', 'ctx')
- grad_values: bfloat16 [16, 1024, 2048], P('dp', 'ctx')
- grad_weight: float32 [2048, 2048], P(('dp', 'ctx'))
Inputs may be any that keep to these rules, and one draw needn't show every extreme that they name: `glob_blocks`: each entry names a block of the document.
All inputs are finite; a program needn't handle non-finite values.
Results may differ from a plain program's by a relative error of at most 0.015.
Values may be sent and summed in bfloat16 or wider, within the bound.
No kernel may reach another device: no remote copies, remote signals or barrier semaphores. Data moves between devices by JAX's collectives and lax.ppermute only.
A program may use at most 128 MiB of HBM per device.

v0:
```python
import math

import jax
import jax.numpy as jnp
from jax import lax
from jax.sharding import PartitionSpec as P

HS = 128
BLK = 64
WIN = 1


masked_score = -1e30


def block_lists(rand_rows, glob_row, block_count):
    head_count = rand_rows.shape[0]
    width = 2 * WIN + 1
    offsets = jnp.arange(-WIN, WIN + 1, dtype=jnp.int32)
    window = jnp.arange(block_count, dtype=jnp.int32)[:, None] + offsets[None, :]
    inside = (window >= 0) & (window < block_count)
    window = jnp.clip(window, 0, block_count - 1)
    lists = jnp.concatenate(
        [
            jnp.broadcast_to(window, (head_count, block_count, width)),
            jnp.broadcast_to(glob_row[None, None, :], (head_count, block_count, glob_row.shape[0])),
            rand_rows,
        ],
        axis=-1,
    )
    in_range = jnp.concatenate(
        [
            jnp.broadcast_to(inside, (head_count, block_count, width)),
            jnp.ones((head_count, block_count, lists.shape[-1] - width), dtype=jnp.bool_),
        ],
        axis=-1,
    )
    positions = jnp.arange(lists.shape[-1], dtype=jnp.int32)
    earlier = positions[None, :] < positions[:, None]
    matching = lists[..., :, None] == lists[..., None, :]
    repeated = jnp.any(matching & earlier & in_range[..., None, :], axis=-1)
    return (lists, in_range & jnp.logical_not(repeated))


def head_pass(query_blocks, key_blocks, value_blocks, cot_blocks, lists, live_entries):
    scale = 1.0 / math.sqrt(HS)
    key_sets = key_blocks[lists]
    value_sets = value_blocks[lists]
    live_mask = live_entries[:, None, :, None]
    scores = (
        jnp.einsum("nqd,nekd->nqek", query_blocks, key_sets, preferred_element_type=jnp.float32)
        * scale
    )
    scores = jnp.where(live_mask, scores, masked_score)
    row_max = jnp.max(scores, axis=(2, 3), keepdims=True)
    unnormed = jnp.where(live_mask, jnp.exp(scores - row_max), 0.0)
    probs = unnormed / jnp.sum(unnormed, axis=(2, 3), keepdims=True)
    probs_low = probs.astype(jnp.bfloat16)
    attended = jnp.einsum(
        "nqek,nekd->nqd", probs_low, value_sets, preferred_element_type=jnp.float32
    ).astype(jnp.bfloat16)
    delta = jnp.sum(cot_blocks.astype(jnp.float32) * attended.astype(jnp.float32), axis=-1)
    prob_grad = jnp.einsum(
        "nqd,nekd->nqek", cot_blocks, value_sets, preferred_element_type=jnp.float32
    )
    score_grad = (probs * (prob_grad - delta[:, :, None, None])).astype(jnp.bfloat16)
    query_grad = (
        jnp.einsum("nqek,nekd->nqd", score_grad, key_sets, preferred_element_type=jnp.float32)
        * scale
    )
    key_terms = (
        jnp.einsum("nqek,nqd->nekd", score_grad, query_blocks, preferred_element_type=jnp.float32)
        * scale
    )
    value_terms = jnp.einsum(
        "nqek,nqd->nekd", probs_low, cot_blocks, preferred_element_type=jnp.float32
    )
    flat_lists = lists.reshape(-1)
    block_count = key_blocks.shape[0]
    key_grad = jax.ops.segment_sum(
        key_terms.reshape(flat_lists.shape[0], -1), flat_lists, num_segments=block_count
    )
    value_grad = jax.ops.segment_sum(
        value_terms.reshape(flat_lists.shape[0], -1), flat_lists, num_segments=block_count
    )
    return (
        attended,
        query_grad.astype(jnp.bfloat16),
        key_grad.reshape(key_blocks.shape).astype(jnp.bfloat16),
        value_grad.reshape(value_blocks.shape).astype(jnp.bfloat16),
    )


def on_device(queries, keys, values, out_weight, cotangent, rand_blocks, glob_blocks):
    cot_rows = cotangent[0]
    full_weight = lax.all_gather(out_weight, ("dp", "ctx"), axis=0, tiled=True)
    head_cot = jnp.dot(cot_rows, full_weight, preferred_element_type=jnp.float32)
    head_cot = head_cot.astype(jnp.bfloat16)[None]
    query_heads, key_heads, value_heads, cot_heads = (
        lax.all_to_all(queries, "ctx", split_axis=2, concat_axis=1, tiled=True),
        lax.all_to_all(keys, "ctx", split_axis=2, concat_axis=1, tiled=True),
        lax.all_to_all(values, "ctx", split_axis=2, concat_axis=1, tiled=True),
        lax.all_to_all(head_cot, "ctx", split_axis=2, concat_axis=1, tiled=True),
    )
    head_count = rand_blocks.shape[1]
    block_count = rand_blocks.shape[2]
    group_len = query_heads.shape[1]

    def split(heads_layout):
        return heads_layout[0].reshape(block_count, BLK, head_count, HS).transpose(2, 0, 1, 3)

    def join(blocks):
        return blocks.transpose(1, 2, 0, 3).reshape(1, group_len, head_count * HS)

    lists, live_entries = block_lists(rand_blocks[0], glob_blocks[0], block_count)

    def per_head(parts):
        return head_pass(*parts)

    attended, query_grad, key_grad, value_grad = lax.map(
        per_head,
        (
            split(query_heads),
            split(key_heads),
            split(value_heads),
            split(cot_heads),
            lists,
            live_entries,
        ),
    )
    attended_heads = join(attended)
    attended_tok, grad_queries, grad_keys, grad_values = (
        lax.all_to_all(attended_heads, "ctx", split_axis=1, concat_axis=2, tiled=True),
        lax.all_to_all(join(query_grad), "ctx", split_axis=1, concat_axis=2, tiled=True),
        lax.all_to_all(join(key_grad), "ctx", split_axis=1, concat_axis=2, tiled=True),
        lax.all_to_all(join(value_grad), "ctx", split_axis=1, concat_axis=2, tiled=True),
    )
    token_rows = attended_tok[0]
    mixed = jnp.dot(token_rows, full_weight.T, preferred_element_type=jnp.float32)
    mixed = mixed.astype(jnp.bfloat16)[None]
    total_tokens = lax.axis_size("dp") * lax.axis_size("ctx") * cot_rows.shape[0]
    grad_scale = 1.0 / math.sqrt(total_tokens)
    term = lax.dot_general(
        cot_rows, token_rows, (((0,), (0,)), ((), ())), preferred_element_type=jnp.float32
    )
    grad_weight = lax.psum_scatter(
        term * grad_scale, ("dp", "ctx"), scatter_dimension=0, tiled=True
    )
    return (mixed, grad_queries, grad_keys, grad_values, grad_weight)


def solution(mesh):
    return jax.shard_map(
        on_device,
        mesh=mesh,
        in_specs=(
            P("dp", "ctx", None),
            P("dp", "ctx", None),
            P("dp", "ctx", None),
            P(("dp", "ctx"), None),
            P("dp", "ctx", None),
            P("dp", "ctx", None, None),
            P("dp", None),
        ),
        out_specs=(
            P("dp", "ctx", None),
            P("dp", "ctx", None),
            P("dp", "ctx", None),
            P("dp", "ctx", None),
            P(("dp", "ctx"), None),
        ),
        check_vma=False,
    )
```

profile of v0, /device:TPU:0, one launch (start us, length us, event | category | flops | bytes accessed | tf_op | source)
XLA Modules:
  0.0 1173.2 jit_solution(4008736325638047405)
XLA Ops:
  7.9 2.4 copy.160
  10.8 11.4 reduce
  23.1 5.5 all-to-all-start
  29.4 11.4 reduce.1
  41.8 5.9 all-to-all-start.1
  47.7 2.4 copy.164
  50.0 11.4 reduce.2
  62.6 5.7 all-to-all-start.2
  68.3 257.8 %all-gather.2.cloned.1.call-done = bf16[2048,2048]{1,0:T(8,128)(2,1)} async-done(((bf16[16,2048]{1,0:T(8,128)(2,1)}), bf16[2048,2048]{1,0:T(8,128)(2,1)}) %all-gather.2.cloned.1.call-update) | async-done | bytes 8388624 | tf_op jit(solution)/shard_map/all_gather | solution.py:96
  326.1 4.6 fusion.33
  331.5 11.4 reduce.3
  343.9 8.4 all-to-all-start.3
  355.8 0.9 copy.169
  356.8 2.2 reshape.175
  360.4 1.7 all-to-all-done.3
  363.9 85.9 %while.16 = (s32[]{:T(128)}, bf16[2,16,64,128]{3,2,1,0:T(8,128)(2,1)}, bf16[2,16,64,128]{3,2,1,0:T(8,128)(2,1)}, bf16[2,16,64,128]{3,2,1,0:T(8,128)(2,1)}, bf16[...) while((s32[]{:T(128)}, ...), condition=%wide.region_7.8_spmd, body=%wide.region_1.7_spmd.sunk | while | flops 824310144 | bytes 95252584 | solution.py:120
  368.3 1.0 dynamic-slice_bitcast_fusion.6
  369.3 1.0 dynamic-slice_bitcast_fusion.8
  370.3 1.0 gather_fusion.1
  371.2 2.2 gather_fusion
  374.3 1.3 fusion.83
  375.6 1.8 bitcast_dynamic-update-slice_fusion.5
  378.4 1.7 multiply_convert_fusion.2
  380.1 1.5 fusion.84
  381.7 2.8 convolution_bitcast_fusion.4
  384.4 9.7 scatter_custom_fusion.10
  394.3 3.6 multiply_bitcast_fusion.3
  397.8 9.7 scatter_custom_fusion.11
  409.1 1.0 dynamic-slice_bitcast_fusion.6
  410.1 1.0 dynamic-slice_bitcast_fusion.8
  411.1 1.0 gather_fusion.1
  412.0 2.2 gather_fusion
  415.1 1.3 fusion.83
  416.4 1.8 bitcast_dynamic-update-slice_fusion.5
  419.3 1.7 multiply_convert_fusion.2
  421.0 1.5 fusion.84
  422.5 2.8 convolution_bitcast_fusion.4
  425.3 9.7 scatter_custom_fusion.10
  435.1 3.6 multiply_bitcast_fusion.3
  438.7 9.7 scatter_custom_fusion.11
  449.9 1.6 copy.173
  451.7 3.7 reduce.4
  455.6 15.3 %all_to_all.129 = bf16[8,2,16384]{2,1,0:T(2,128)(2,1)S(1)} all-to-all(bf16[8,2,16384]{2,1,0:T(2,128)(2,1)S(1)} %reshape.178), channel_id=1, replica_groups=mesh['dp'=16,'ctx'=8] {'ctx'}, dimensions={0} | all-to-all | bytes 1048576 | tf_op jit(solution)/shard_map/all_to_all | solution.py:133
  471.8 8.0 multiply_bitcast_fusion.1
  479.8 17.6 %copy.196 = f32[2048,2048]{1,0:T(8,128)} copy(f32[2048,2048]{0,1:T(8,128)} %multiply_bitcast_fusion.1) | data formatting | bytes 33554432
  497.4 1.0 copy-done.9
  499.3 3.7 reduce.7
  503.9 3.7 all-to-all-start.7
  507.6 1.6 copy.176
  509.5 3.7 reduce.5
  514.1 3.5 all-to-all-done.7
  517.6 3.6 all-to-all-start.5
  521.3 2.4 copy.179
  523.7 3.6 reshape.161
  527.2 4.5 reduce.6
  531.7 2.0 reshape.182
  533.7 6.0 all-to-all-start.6
  540.6 1.0 copy.187
  542.5 1.0 copy.185
  543.5 6.4 all-to-all-done.6
  549.9 2.2 reshape.183
  552.5 1.0 copy.186
  553.5 7.1 fusion.34
  560.7 605.4 %reduce-scatter.4.cloned.1.call-done = f32[16,2048]{1,0:T(8,128)} async-done(((f32[2048,2048]{1,0:T(8,128)}), f32[16,2048]{1,0:T(8,128)}) %reduce-scatter.4.cloned.1.call-update) | async-done | bytes 131088
  (150 shorter events, 26.6 us)
Async XLA Ops:
  7.2 319.0 %copy-start = (bf16[1,128,2048]{2,1,0:T(8,128)(2,1)S(1)}, bf16[1,128,2048]{2,1,0:T(8,128)(2,1)}, u32[]{:S(2)}) copy-start(bf16[1,128,2048]{2,1,0:T(8,128)(2,1)} %param.13) | copy-start | bytes 1572868
  7.2 21.4 %copy-start.6 = (bf16[1,128,2048]{2,1,0:T(8,128)(2,1)S(1)}, bf16[1,128,2048]{2,1,0:T(8,128)(2,1)}, u32[]{:S(2)}) copy-start(bf16[1,128,2048]{2,1,0:T(8,128)(2,1)} %param.10) | copy-start | bytes 1572868
  7.2 318.9 %all-gather.2.cloned.1.call-start = ((), (), s32[]{:S(2)}) async-start(), calls=%async_computation.9 | async-start | bytes 8454144 | tf_op jit(solution)/shard_map/all_gather | solution.py:96
  23.1 18.6 %all-to-all-start = ((bf16[8,2,16384]{2,1,0:T(2,128)(2,1)}), bf16[8,2,16384]{2,1,0:T(2,128)(2,1)S(1)}, u32[]{:S(2)}, u32[]{:S(2)}) async-start(bf16[8,2,16384]{2,1,0:T(2,128)(2,1)} %reshape.170), calls=%async_computation | async-start | bytes 1048576 | tf_op jit(solution)/shard_map/all_to_all | solution.py:100
  29.4 33.0 %copy-start.15 = (s32[1,2]{1,0:T(1,128)S(1)}, s32[1,2]{1,0:T(1,128)}, u32[]{:S(2)}) copy-start(s32[1,2]{1,0:T(1,128)} %param.15) | copy-start | bytes 28
  29.4 33.2 %copy-start.14 = (s32[1,2,16,3]{2,1,3,0:T(2,128)S(1)}, s32[1,2,16,3]{2,1,3,0:T(2,128)}, u32[]{:S(2)}) copy-start(s32[1,2,16,3]{2,1,3,0:T(2,128)} %param.14) | copy-start | bytes 1156
  41.8 20.9 %all-to-all-start.1 = ((bf16[8,2,16384]{2,1,0:T(2,128)(2,1)}), bf16[8,2,16384]{2,1,0:T(2,128)(2,1)S(1)}, u32[]{:S(2)}, u32[]{:S(2)}) async-start(bf16[8,2,16384]{2,1,0:T(2,128)(2,1)} %reshape.172), calls=%async_computation.1 | async-start | bytes 1048576 | tf_op jit(solution)/shard_map/all_to_all | solution.py:101
  62.6 281.3 %all-to-all-start.2 = ((bf16[8,2,16384]{2,1,0:T(2,128)(2,1)}), bf16[8,2,16384]{2,1,0:T(2,128)(2,1)}, u32[]{:S(2)}, u32[]{:S(2)}) async-start(bf16[8,2,16384]{2,1,0:T(2,128)(2,1)} %reshape.174), calls=%async_computation.2 | async-start | bytes 1048576 | tf_op jit(solution)/shard_map/all_to_all | solution.py:102
  343.9 18.2 %all-to-all-start.3 = ((bf16[8,2,16384]{2,1,0:T(2,128)(2,1)}), bf16[8,2,16384]{2,1,0:T(2,128)(2,1)S(1)}, u32[]{:S(2)}, u32[]{:S(2)}) async-start(bf16[8,2,16384]{2,1,0:T(2,128)(2,1)} %reshape.176), calls=%async_computation.3 | async-start | bytes 1048576 | tf_op jit(solution)/shard_map/all_to_all | solution.py:103
  352.3 813.8 %reduce-scatter.4.cloned.1.call-start = ((), (), s32[]{:S(2)}) async-start(), calls=%async_computation.10 | async-start | bytes 16908288
  371.2 2.2 copy-start.4
  373.4 2.2 copy-start.3
  373.4 2.2 copy-start.12
  375.6 2.6 copy-start.5
  377.4 0.8 copy-start.13
  380.1 1.5 copy-start.1
  384.4 9.8 copy-start.2
  397.8 9.8 copy-start.7
  397.8 9.8 copy-start.10
  407.7 0.8 copy-start.8
  407.7 1.0 copy-start.11
  412.0 2.2 copy-start.4
  414.2 2.2 copy-start.3
  414.2 2.2 copy-start.12
  416.4 2.6 copy-start.5
  418.2 0.8 copy-start.13
  420.9 1.5 copy-start.1
  425.2 9.8 copy-start.2
  438.7 9.8 copy-start.7
  438.7 9.8 copy-start.10
  448.5 0.8 copy-start.8
  448.5 1.0 copy-start.11
  497.4 1.0 copy-start.9
  503.9 13.7 %all-to-all-start.7 = ((bf16[8,2,16384]{2,1,0:T(2,128)(2,1)}), bf16[8,2,16384]{2,1,0:T(2,128)(2,1)S(1)}, u32[]{:S(2)}, u32[]{:S(2)}) async-start(bf16[8,2,16384]{2,1,0:T(2,128)(2,1)} %reshape.184), calls=%async_computation.7 | async-start | bytes 1048576 | tf_op jit(solution)/shard_map/all_to_all | solution.py:136
  517.6 16.1 %all-to-all-start.5 = ((bf16[8,2,16384]{2,1,0:T(2,128)(2,1)}), bf16[8,2,16384]{2,1,0:T(2,128)(2,1)S(1)}, u32[]{:S(2)}, u32[]{:S(2)}) async-start(bf16[8,2,16384]{2,1,0:T(2,128)(2,1)} %reshape.180), calls=%async_computation.5 | async-start | bytes 1048576 | tf_op jit(solution)/shard_map/all_to_all | solution.py:134
  533.7 16.2 %all-to-all-start.6 = ((bf16[8,2,16384]{2,1,0:T(2,128)(2,1)}), bf16[8,2,16384]{2,1,0:T(2,128)(2,1)}, u32[]{:S(2)}, u32[]{:S(2)}) async-start(bf16[8,2,16384]{2,1,0:T(2,128)(2,1)} %reshape.182), calls=%async_computation.6 | async-start | bytes 1048576 | tf_op jit(solution)/shard_map/all_to_all | solution.py:135
Sparse Core Ops, SparseCore 0:
  9.7 316.3 all-gather.1
  497.6 668.4 reduce-scatter.3
where the time goes:
time: 1180 us; the launch traced here: 1170 us
  waiting for transfers between devices  876 us (74%)
  other arithmetic  104 us (9%)
  local copies, waits for them, and re-layouts  75.7 us (6%)
  matrix products  44.2 us (4%)
  starting transfers between devices  39.2 us (3%)
  blocking collectives  15.3 us (1%)
  between operations  14.7 us (1%)
    unnamed x3, waiting for transfers between devices  606 us
    all_gather x1, waiting for transfers between devices, on_device(): full_weight = lax.all_gather(out_weight, ('dp', 'ctx'), axis=0, tiled=True)  258 us
    unnamed x8, other arithmetic  61.4 us
    unnamed x42, local copies, waits for them, and re-layouts  43.4 us
  transfers between devices with their start and end apart: 9, of which 5 were waited for; matrix products, arithmetic and copies ran while one was open for 9% of the time, Pallas kernels for 0%

commit v1 on v0

v1 whole, which is shorter than its diff:
```python
import math

import jax
import jax.numpy as jnp
from jax import lax
from jax.experimental import pallas as pl
from jax.experimental.pallas import tpu as pltpu
from jax.sharding import Mesh
from jax.sharding import PartitionSpec as P

HS = 128
BLK = 64
NB = 16
LEN = 1024
HD = 2048
SCALE = 1.0 / math.sqrt(HS)
LOG2E = math.log2(math.e)
MASKED = -1e30
CTX = ("xl", "y")
DP = ("z", "xh", "core")
BF = jnp.bfloat16
F32 = jnp.float32
NT = (((1,), (1,)), ((), ()))
NN = (((1,), (0,)), ((), ()))
TN = (((0,), (0,)), ((), ()))


def dot(a, b, dims=NN):
    return lax.dot_general(a, b, dims, preferred_element_type=F32)


def params(mib=48):
    return pltpu.CompilerParams(vmem_limit_bytes=mib * 2**20)


def pack_kernel(q_ref, k_ref, v_ref, out_ref):
    out_ref[0, 0] = q_ref[...]
    out_ref[0, 1] = k_ref[...]
    out_ref[0, 2] = v_ref[...]


def pack_heads(q, k, v):
    spec = pl.BlockSpec((128, 256), lambda c: (0, c))
    return pl.pallas_call(
        pack_kernel,
        grid=(8,),
        in_specs=[spec] * 3,
        out_specs=pl.BlockSpec((1, 3, 128, 256), lambda c: (c, 0, 0, 0)),
        out_shape=jax.ShapeDtypeStruct((8, 3, 128, 256), BF),
        cost_estimate=pl.CostEstimate(flops=0, bytes_accessed=3 * 2**20, transcendentals=0),
        name="pack_heads",
    )(q, k, v)


def halves_kernel(cot_ref, out_ref):
    low = lax.broadcasted_iota(jnp.int32, (128, 128), 1) < 64
    for pair in range(8):
        a = cot_ref[:, 256 * pair : 256 * pair + 128].astype(F32)
        b = cot_ref[:, 256 * pair + 128 : 256 * pair + 256].astype(F32)
        first = jnp.where(low, a, pltpu.roll(b, 64, 1)).astype(BF)
        second = jnp.where(low, pltpu.roll(a, 64, 1), b).astype(BF)
        for y in range(4):
            out_ref[y, :, 128 * pair : 128 * pair + 128] = first
            out_ref[4 + y, :, 128 * pair : 128 * pair + 128] = second


def cot_halves(cot):
    return pl.pallas_call(
        halves_kernel,
        out_shape=jax.ShapeDtypeStruct((8, 128, 1024), BF),
        in_specs=[pl.BlockSpec(memory_space=pltpu.VMEM)],
        out_specs=pl.BlockSpec(memory_space=pltpu.VMEM),
        compiler_params=params(),
        cost_estimate=pl.CostEstimate(flops=0, bytes_accessed=5 * 2**19, transcendentals=0),
        name="cot_halves",
    )(cot)


def live_bias(rand, glob):
    kb = jnp.arange(NB, dtype=jnp.int32)[:, None]
    qb = jnp.arange(NB, dtype=jnp.int32)[None, :]
    live = (jnp.abs(kb - qb) <= 1) | jnp.any(kb[:, :, None] == glob[None, None, :], axis=-1)
    by_rand = jnp.any(rand.transpose(0, 2, 1)[:, :, None, :] == kb[None, None], axis=1)
    bias = jnp.where(live[None] | by_rand, 0.0, MASKED).astype(F32)
    return jnp.repeat(bias, BLK, axis=2)


TILE = 256


def scores_at(k, q, bias):
    s = dot(k, q, NT).reshape(NB, BLK, TILE)
    return s * (SCALE * LOG2E) + bias[:, None, :]


def forward_kernel(qkv_ref, bias_ref, o_ref, stat_ref):
    k = qkv_ref[:, 1].reshape(LEN, HS)
    v_t = qkv_ref[:, 2].reshape(LEN, HS).T
    for t in range(LEN // TILE):
        tok = slice(TILE * t, TILE * t + TILE)
        q = qkv_ref[2 * t : 2 * t + 2, 0].reshape(TILE, HS)
        s = scores_at(k, q, bias_ref[0, :, tok])
        top = jnp.max(s, axis=(0, 1), keepdims=True)
        p = jnp.exp2(s - top)
        total = jnp.sum(p, axis=(0, 1), keepdims=True)
        p_low = (p * (1.0 / total)).astype(BF).reshape(LEN, TILE)
        o_t = dot(v_t, p_low)
        o_ref[tok, :] = o_t.T.astype(BF)
        stat_ref[0, :, tok] = (top + jnp.log2(total))[0]


def forward(qkv, bias):
    return pl.pallas_call(
        forward_kernel,
        grid=(2,),
        in_specs=[
            pl.BlockSpec((8, 3, 128, HS), lambda h: (0, 0, 0, h)),
            pl.BlockSpec((1, NB, LEN), lambda h: (h, 0, 0)),
        ],
        out_specs=[
            pl.BlockSpec((LEN, HS), lambda h: (0, h)),
            pl.BlockSpec((1, 1, LEN), lambda h: (h, 0, 0)),
        ],
        out_shape=[
            jax.ShapeDtypeStruct((LEN, 2 * HS), BF),
            jax.ShapeDtypeStruct((2, 1, LEN), F32),
        ],
        compiler_params=params(),
        cost_estimate=pl.CostEstimate(flops=4 * 2**30, bytes_accessed=2**21, transcendentals=2**21),
        name="attention_forward",
    )(qkv, bias)


def backward_kernel(qkv_ref, bias_ref, stat_ref, o_ref, keep_ref, recv_ref, out_ref, dk_ref, dv_ref):
    k = qkv_ref[:, 1].reshape(LEN, HS)
    v = qkv_ref[:, 2].reshape(LEN, HS)
    k_t = k.T
    for t in range(LEN // TILE):
        tok = slice(TILE * t, TILE * t + TILE)
        q = qkv_ref[2 * t : 2 * t + 2, 0].reshape(TILE, HS)
        do = (keep_ref[tok, :] + recv_ref[tok, :].astype(F32)).astype(BF)
        delta = jnp.sum((do.astype(F32) * o_ref[tok, :].astype(F32)).T, axis=0, keepdims=True)
        p = jnp.exp2(scores_at(k, q, bias_ref[0, :, tok] - stat_ref[0, :, tok]))
        p = p.reshape(LEN, TILE)
        dp = dot(v, do, NT)
        ds = (p * (dp - delta)).astype(BF)
        dq = dot(k_t, ds).T * SCALE
        out_ref[2 * t : 2 * t + 2, 0] = dq.astype(BF).reshape(2, 128, HS)
        dk = dot(ds, q)
        dv = dot(p.astype(BF), do)
        if t == 0:
            dk_ref[...] = dk
            dv_ref[...] = dv
        else:
            dk_ref[...] += dk
            dv_ref[...] += dv
    out_ref[:, 1] = (dk_ref[...] * SCALE).astype(BF).reshape(8, 128, HS)
    out_ref[:, 2] = dv_ref[...].astype(BF).reshape(8, 128, HS)


def backward(qkv, bias, stat, attended, keep, recv):
    wide = pl.BlockSpec((LEN, HS), lambda h: (0, h))
    heads = pl.BlockSpec((8, 3, 128, HS), lambda h: (0, 0, 0, h))
    return pl.pallas_call(
        backward_kernel,
        grid=(2,),
        in_specs=[
            heads,
            pl.BlockSpec((1, NB, LEN), lambda h: (h, 0, 0)),
            pl.BlockSpec((1, 1, LEN), lambda h: (h, 0, 0)),
            wide,
            wide,
            wide,
        ],
        out_specs=heads,
        out_shape=jax.ShapeDtypeStruct((8, 3, 128, 2 * HS), BF),
        scratch_shapes=[pltpu.VMEM((LEN, HS), F32), pltpu.VMEM((LEN, HS), F32)],
        compiler_params=params(),
        cost_estimate=pl.CostEstimate(flops=8 * 2**30, bytes_accessed=2**22, transcendentals=2**21),
        name="attention_backward",
    )(qkv, bias, stat, attended, keep, recv)


def unpack_kernel(in_ref, q_ref, k_ref, v_ref):
    q_ref[...] = in_ref[0, 0]
    k_ref[...] = in_ref[0, 1]
    v_ref[...] = in_ref[0, 2]


def unpack_heads(grads):
    spec = pl.BlockSpec((128, 256), lambda c: (0, c))
    return pl.pallas_call(
        unpack_kernel,
        grid=(8,),
        in_specs=[pl.BlockSpec((1, 3, 128, 256), lambda c: (c, 0, 0, 0))],
        out_specs=[spec] * 3,
        out_shape=[jax.ShapeDtypeStruct((128, HD), BF)] * 3,
        cost_estimate=pl.CostEstimate(flops=0, bytes_accessed=3 * 2**20, transcendentals=0),
        name="unpack_heads",
    )(grads)


def mixed_kernel(in_ref, out_ref):
    low = lax.broadcasted_iota(jnp.int32, (128, 128), 1) < 64
    for pair in range(8):
        cols = slice(128 * pair, 128 * pair + 128)
        first = sum(in_ref[y, :, cols].astype(F32) for y in range(4))
        second = sum(in_ref[4 + y, :, cols].astype(F32) for y in range(4))
        a = jnp.where(low, first, pltpu.roll(second, 64, 1))
        b = jnp.where(low, pltpu.roll(first, 64, 1), second)
        out_ref[:, 256 * pair : 256 * pair + 128] = a.astype(BF)
        out_ref[:, 256 * pair + 128 : 256 * pair + 256] = b.astype(BF)


def finish_mixed(parts):
    return pl.pallas_call(
        mixed_kernel,
        out_shape=jax.ShapeDtypeStruct((128, HD), BF),
        in_specs=[pl.BlockSpec(memory_space=pltpu.VMEM)],
        out_specs=pl.BlockSpec(memory_space=pltpu.VMEM),
        compiler_params=params(),
        cost_estimate=pl.CostEstimate(flops=0, bytes_accessed=5 * 2**19, transcendentals=0),
        name="finish_mixed",
    )(parts)


def ring(size, step):
    return [(i, (i + step) % size) for i in range(size)]


def swap(array):
    return lax.ppermute(array, "xl", ring(2, 1))


def gather_weight(own):
    parts = lax.all_to_all(own, "y", 0, 0, tiled=True).reshape(64, 512)
    core = lax.axis_index("core")
    other = lax.ppermute(parts, "core", ring(2, 1))
    pair = jnp.where(core == 0, jnp.stack([parts, other]), jnp.stack([other, parts]))
    xh = lax.axis_index("xh")
    other = lax.ppermute(pair, "xh", ring(2, 1))
    quad = jnp.where(xh == 0, jnp.stack([pair, other]), jnp.stack([other, pair]))
    z = lax.axis_index("z")
    rel = jnp.stack([quad] + [lax.ppermute(quad, "z", ring(4, step)) for step in (1, 2, 3)])
    at = (z - jnp.arange(4)) % 4
    full = jnp.zeros_like(rel)
    for step in range(4):
        full = lax.dynamic_update_index_in_dim(full, rel[step], at[step], 0)
    return full.reshape(1024, 512)


def on_device(queries, keys, values, out_weight, cotangent, rand_blocks, glob_blocks):
    xl = lax.axis_index("xl")
    sides = out_weight.reshape(16, 2, 1024)
    sides = jnp.where(xl == 0, sides, sides[:, ::-1])
    own = sides.reshape(16, 2, 4, 256).transpose(2, 0, 1, 3).reshape(4, 16, 512)

    qkv = lax.all_to_all(pack_heads(queries[0], keys[0], values[0]), CTX, 0, 0, tiled=True)
    weight = gather_weight(own)
    cot = lax.all_to_all(cot_halves(cotangent[0]), CTX, 0, 0, tiled=True).reshape(LEN, 1024)

    bias = live_bias(rand_blocks[0], glob_blocks[0])
    attended, stat = forward(qkv, bias)
    keep = dot(cot, weight[:, :256])
    recv = swap(dot(cot, weight[:, 256:]).astype(BF))
    other = swap(attended)
    grads = backward(qkv, bias, stat, attended, keep, recv)
    grads = lax.all_to_all(grads, CTX, 0, 0, tiled=True)

    pair = jnp.concatenate([attended, other], axis=1)
    part = dot(pair, weight, NT).astype(BF).reshape(8, 128, 1024)
    part = lax.all_to_all(part, CTX, 0, 0, tiled=True)

    block = dot(cot, pair, TN).astype(BF).reshape(16, 64, 512)
    block = lax.all_to_all(block, DP, 0, 0, tiled=True)
    total_tokens = lax.axis_size(DP) * lax.axis_size(CTX) * cotangent.shape[1]
    rows = jnp.sum(block.astype(F32), axis=0) * (1.0 / math.sqrt(total_tokens))
    rows = lax.all_to_all(rows.reshape(4, 16, 512), "y", 0, 0, tiled=True)
    rows = rows.reshape(4, 16, 2, 256).transpose(1, 2, 0, 3)
    rows = jnp.where(xl == 0, rows, rows[:, ::-1]).reshape(16, HD)

    grad_q, grad_k, grad_v = unpack_heads(grads)
    mixed = finish_mixed(part)
    return (mixed[None], grad_q[None], grad_k[None], grad_v[None], rows)


def solution(mesh):
    fine = Mesh(mesh.devices.reshape(4, 2, 2, 2, 4), ("z", "xh", "core", "xl", "y"))
    tokens = P(DP, CTX, None)
    return jax.shard_map(
        on_device,
        mesh=fine,
        in_specs=(tokens, tokens, tokens, P(DP + CTX, None), tokens, P(DP, CTX, None, None), P(DP, None)),
        out_specs=(tokens, tokens, tokens, tokens, P(DP + CTX, None)),
        check_vma=False,
    )
```

time: 1180 us -> 199 us (0.17)
  waiting for transfers between devices: 876 us -> 86.8 us
  other arithmetic: 104 us -> 2.45 us
  local copies, waits for them, and re-layouts: 75.7 us -> 11.8 us
  matrix products: 44.2 us -> 13.7 us
  Pallas kernels: 0 us -> 28.6 us
  blocking collectives: 15.3 us -> 0 us
    unnamed x3 -> x0, waiting for transfers between devices: 606 us -> none
    all_gather x1 -> x0, waiting for transfers between devices: 258 us -> none  [on_device(): full_weight = lax.all_gather(out_weight, ('dp', 'ctx'), axis=0, tiled=True)]
    unnamed x8 -> x0, other arithmetic: 61.4 us -> none
    all_to_all x7, waiting for transfers between devices: 11.6 us -> 63.9 us  [the longest x1 19.4 us: on_device(): part = lax.all_to_all(part, CTX, 0, 0, tiled=True)]
    unnamed x42 -> x17, local copies, waits for them, and re-layouts: 43.4 us -> 3.31 us
    scatter-add x4 -> x0, other arithmetic: 38.8 us -> none  [the longest x2 19.5 us: head_pass(): jax.ops.segment_sum(value_terms.reshape(flat_lists.shape[0], -1), flat_li...]
    dot_general x15 -> x4, matrix products: 44.2 us -> 13.7 us  [dot(): return lax.dot_general(a, b, dims, preferred_element_type=F32)]
    pallas_call x0 -> x6, Pallas kernels: none -> 28.6 us  [the longest x1 7.53 us: backward(): pl.pallas_call(backward_kernel, grid=(2,), in_specs=[heads, pl.BlockSpec(...]
  transfers between devices with their start and end apart: 9 -> 14, of which waited for: 5 -> 9; matrix products, arithmetic and copies ran while one was open for 9% -> 12% of each run, Pallas kernels for 0% -> 14%
where the time goes in v1:
time: 199 us; the launch traced here: 197 us
  waiting for transfers between devices  86.8 us (44%)
  starting transfers between devices  45.3 us (23%)
  Pallas kernels  28.6 us (14%)
  matrix products  13.7 us (7%)
  local copies, waits for them, and re-layouts  11.8 us (6%)
  between operations  8.66 us (4%)
  other arithmetic  2.45 us (1%)
    all_to_all x1, waiting for transfers between devices, on_device(): part = lax.all_to_all(part, CTX, 0, 0, tiled=True)  19.4 us
    all_to_all x1, waiting for transfers between devices, on_device(): lax.all_to_all(pack_heads(queries[0], keys[0], values[0]), CTX, 0, 0, til...  17.7 us
    all_to_all x1, waiting for transfers between devices, on_device(): grads = lax.all_to_all(grads, CTX, 0, 0, tiled=True)  16.3 us
    ppermute x1, waiting for transfers between devices, gather_weight(): other = lax.ppermute(pair, 'xh', ring(2, 1))  15.9 us
    dot_general x4, matrix products, dot(): return lax.dot_general(a, b, dims, preferred_element_type=F32)  13.7 us
    all_to_all x1, waiting for transfers between devices, on_device(): block = lax.all_to_all(block, DP, 0, 0, tiled=True)  10 us
    pallas_call x1, Pallas kernels, backward(): pl.pallas_call(backward_kernel, grid=(2,), in_specs=[heads, pl.BlockSpec(...  7.53 us
    pallas_call x1, Pallas kernels, forward(): pl.pallas_call(forward_kernel, grid=(2,), in_specs=[pl.BlockSpec((8, 3, 1...  7.15 us
  transfers between devices with their start and end apart: 14, of which 9 were waited for; matrix products, arithmetic and copies ran while one was open for 12% of the time, Pallas kernels for 14%

profile of v1, /device:TPU:0, one launch (start us, length us, event | category | flops | bytes accessed | tf_op | source)
XLA Modules:
  0.0 197.3 jit_solution(9390420055813933739)
XLA Ops:
  0.6 0.8 copy.39
  1.5 0.1 copy.30
  1.6 0.7 reshape.292
  2.3 4.5 %all-to-all-start.1 = ((bf16[4,16,512]{2,1,0:T(8,128)(2,1)}), bf16[4,16,512]{2,1,0:T(8,128)(2,1)S(1)}, u32[]{:S(2)}, u32[]{:S(2)}) async-start(bf16[4,16,512]{2,1,0:T(8,128)(2,1)} %reshape.292), calls=%async_computation.1 | async-start | bytes 131072 | tf_op jit(solution)/shard_map/all_to_all | solution.py:236
  6.8 5.3 %pack_heads.1 = bf16[8,3,128,256]{3,2,1,0:T(8,128)(2,1)} custom-call(bf16[128,2048]{1,0:T(8,128)(2,1)} %bitcast.76, bf16[128,2048]{1,0:T(8,128)(2,1)} %bitcast.77, bf16[128,2048]{1,0:T(8,128)(2,1)} %bitcast.78), custom_call_target="tpu_custom_call" | custom-call | bytes 3145728 | tf_op jit(solution)/shard_map/pack_heads/pallas_call | solution.py:44
  12.2 0.3 all-to-all-done.1
  12.5 5.6 %all-to-all-start = ((bf16[8,3,128,256]{3,2,1,0:T(8,128)(2,1)}), bf16[8,3,128,256]{3,2,1,0:T(8,128)(2,1)S(1)}, u32[]{:S(2)}, u32[]{:S(2)}) async-start(bf16[8,3,128,256]{3,2,1,0:T(8,128)(2,1)} %pack_heads.1), calls=%async_computation | async-start | bytes 3145728 | tf_op jit(solution)/shard_map/all_to_all | solution.py:258
  18.0 0.0 copy-start.7
  18.1 1.9 cot_halves.1
  20.0 0.0 copy-done.6
  20.0 0.1 compare_reduce_fusion
  20.1 0.1 fusion.6
  20.2 17.7 %all-to-all-done.qkv_ref = bf16[8,3,128,256]{3,2,1,0:T(8,128)(2,1)S(1)} async-done(((bf16[8,3,128,256]{3,2,1,0:T(8,128)(2,1)}), bf16[8,3,128,256]{3,2,1,0:T(8,128)(2,1)S(1)}, u32[]{:S(2)}, u32[]{:S(2)}) %all-to-all-start) | async-done | bytes 1572896 | tf_op jit(solution)/shard_map/all_to_all | solution.py:258
  37.9 4.3 %all-to-all-start.3 = ((bf16[8,128,1024]{2,1,0:T(8,128)(2,1)}), bf16[8,128,1024]{2,1,0:T(8,128)(2,1)}, u32[]{:S(2)}, u32[]{:S(2)}) async-start(bf16[8,128,1024]{2,1,0:T(8,128)(2,1)} %cot_halves.1), calls=%async_computation.3 | async-start | bytes 4194304 | tf_op jit(solution)/shard_map/all_to_all | solution.py:260
  42.3 0.1 collective-permute-start.1
  42.4 1.2 collective-permute-done.1
  43.6 2.8 %collective-permute-start.2 = (bf16[2,64,512]{2,1,0:T(8,128)(2,1)S(1)}, bf16[2,64,512]{2,1,0:T(8,128)(2,1)S(1)}, u32[]{:S(2)}, u32[]{:S(2)}) collective-permute-start(bf16[2,64,512]{2,1,0:T(8,128)(2,1)S(1)} %maximum_select_fusion.3), channel_id=1, source_target_pairs={{0,16},{16,0},{1,17},{17,1},{2,18},{18,2},{3,19},{19,3},{4,20},{20... | collective-permute-start | bytes 393224 | tf_op jit(solution)/shard_map/ppermute | solution.py:241
  46.4 0.6 fusion.8
  52.2 0.1 broadcast_in_dim.43
  52.3 0.1 reshape.289.bias_ref
  55.1 15.9 %collective-permute-done.2 = bf16[2,64,512]{2,1,0:T(8,128)(2,1)S(1)} collective-permute-done((bf16[2,64,512]{2,1,0:T(8,128)(2,1)S(1)}, bf16[2,64,512]{2,1,0:T(8,128)(2,1)S(1)}, u32[]{:S(2)}, u32[]{:S(2)}) %collective-permute-start.2) | collective-permute-done | bytes 131104 | tf_op jit(solution)/shard_map/ppermute | solution.py:241
  71.0 2.0 %collective-permute-start.3 = (bf16[2,2,64,512]{3,2,1,0:T(8,128)(2,1)S(1)}, bf16[2,2,64,512]{3,2,1,0:T(8,128)(2,1)S(1)}, u32[]{:S(2)}, u32[]{:S(2)}) collective-permute-start(bf16[2,2,64,512]{3,2,1,0:T(8,128)(2,1)S(1)} %maximum_select_fusion.1), channel_id=1, source_target_pairs={{0,32},{32,64},{64,96},{96,0},{1,33},{33,65},{65,97},{97,1},{2,34}... | collective-permute-start | bytes 786440 | tf_op jit(solution)/shard_map/ppermute | solution.py:244
  73.0 7.1 %attention_forward.1 = (bf16[1024,256]{1,0:T(8,128)(2,1)S(1)}, f32[2,1,1024]{2,1,0:T(1,128)S(1)}) custom-call(bf16[8,3,128,256]{3,2,1,0:T(8,128)(2,1)S(1)} %all-to-all-done.qkv_ref, f32[2,16,1024]{2,1,0:T(8,128)S(1)} %reshape.289.bias_ref), custom_call_target="tpu_custom_call" | custom-call | flops 4294967296 | bytes 2097152 | tf_op jit(solution)/shard_map/attention_forward/pallas_call | solution.py:113
  80.1 1.2 collective-permute-start
  81.3 3.7 %collective-permute-start.4 = (bf16[2,2,64,512]{3,2,1,0:T(8,128)(2,1)S(1)}, bf16[2,2,64,512]{3,2,1,0:T(8,128)(2,1)S(1)}, u32[]{:S(2)}, u32[]{:S(2)}) collective-permute-start(bf16[2,2,64,512]{3,2,1,0:T(8,128)(2,1)S(1)} %maximum_select_fusion.1), channel_id=1, source_target_pairs={{0,64},{32,96},{64,0},{96,32},{1,65},{33,97},{65,1},{97,33},{2,66}... | collective-permute-start | bytes 786440 | tf_op jit(solution)/shard_map/ppermute | solution.py:244
  85.0 1.0 collective-permute-start.5
  86.0 0.1 broadcast_in_dim.44
  86.1 0.1 fusion.4
  86.2 0.0 collective-permute-done.3
  86.2 0.9 constant_dynamic-update-slice_fusion.1
  87.2 5.7 %collective-permute-done = bf16[1024,256]{1,0:T(8,128)(2,1)S(1)} collective-permute-done((bf16[1024,256]{1,0:T(8,128)(2,1)S(1)}, bf16[1024,256]{1,0:T(8,128)(2,1)S(1)}, u32[]{:S(2)}, u32[]{:S(2)}) %collective-permute-start) | collective-permute-done | bytes 524320 | tf_op jit(solution)/shard_map/ppermute | solution.py:232
  92.9 0.9 constant_dynamic-update-slice_fusion
  93.7 0.0 all-to-all-done.3
  93.7 4.2 %fusion = bf16[1024,512]{0,1:T(8,128)(2,1)} fusion(bf16[1024,512]{1,0:T(8,128)(2,1)} %constant_dynamic-update-slice_fusion, bf16[1024,1024]{1,0:T(8,128)(2,1)} %bitcast.26), kind=kOutput, calls=%fused_computation.4 | convolution fusion | flops 1074266112 | bytes 4194304 | tf_op jit(solution)/shard_map/dot_general | solution.py:29
  97.9 2.3 %copy.33 = bf16[1024,512]{1,0:T(8,128)(2,1)} copy(bf16[1024,512]{0,1:T(8,128)(2,1)} %fusion) | data formatting | bytes 2097152 | tf_op jit(solution)/shard_map/convert_element_type | solution.py:274
  100.1 5.5 %all-to-all-start.5 = ((bf16[16,64,512]{2,1,0:T(8,128)(2,1)}), bf16[16,64,512]{2,1,0:T(8,128)(2,1)}, u32[]{:S(2)}, u32[]{:S(2)}) async-start(bf16[16,64,512]{2,1,0:T(8,128)(2,1)} %bitcast.60), calls=%async_computation.5 | async-start | bytes 2097152 | tf_op jit(solution)/shard_map/all_to_all | solution.py:275
  105.7 0.0 collective-permute-done.4
  105.7 0.7 bitcast_dynamic-update-slice_fusion.1
  106.4 0.0 collective-permute-done.5
  106.4 0.7 bitcast_dynamic-update-slice_fusion
  107.2 2.5 %fusion.1 = bf16[1024,256]{1,0:T(8,128)(2,1)S(1)} fusion(bf16[1024,1024]{1,0:T(8,128)(2,1)} %bitcast.26, bf16[1024,512]{1,0:T(8,128)(2,1)} %bitcast.63), kind=kOutput, calls=%fused_computation.6 | convolution fusion | flops 537133056 | bytes 3145728 | tf_op jit(solution)/shard_map/dot_general | solution.py:29
  109.6 1.2 collective-permute-start.6
  110.9 3.3 %convolution_bitcast_fusion.keep_ref = f32[1024,256]{1,0:T(8,128)} fusion(bf16[1024,1024]{1,0:T(8,128)(2,1)} %bitcast.26, bf16[1024,512]{1,0:T(8,128)(2,1)S(1)} %bitcast.64), kind=kOutput, calls=%fused_computation.3 | convolution fusion | flops 536870912 | bytes 3670016 | tf_op jit(solution)/shard_map/dot_general | solution.py:29
  114.1 10.0 %all-to-all-done.5 = bf16[16,64,512]{2,1,0:T(8,128)(2,1)} async-done(((bf16[16,64,512]{2,1,0:T(8,128)(2,1)}), bf16[16,64,512]{2,1,0:T(8,128)(2,1)}, u32[]{:S(2)}, u32[]{:S(2)}) %all-to-all-start.5) | async-done | bytes 1048608 | tf_op jit(solution)/shard_map/all_to_all | solution.py:275
  124.2 1.4 convert_reduce_fusion
  125.6 0.7 broadcast_multiply_fusion
  126.2 4.3 %all-to-all-start.6 = ((f32[4,16,512]{2,1,0:T(8,128)}), f32[4,16,512]{2,1,0:T(8,128)S(1)}, u32[]{:S(2)}, u32[]{:S(2)}) async-start(f32[4,16,512]{2,1,0:T(8,128)} %bitcast.34), calls=%async_computation.6 | async-start | bytes 262144 | tf_op jit(solution)/shard_map/all_to_all | solution.py:278
  130.5 0.2 collective-permute-done.6.recv_ref
  130.7 1.2 copy-done.1
  131.9 7.5 %attention_backward.1 = bf16[8,3,128,256]{3,2,1,0:T(8,128)(2,1)} custom-call(bf16[8,3,128,256]{3,2,1,0:T(8,128)(2,1)S(1)} %all-to-all-done.qkv_ref, f32[2,16,1024]{2,1,0:T(8,128)S(1)} %reshape.289.bias_ref, f32[2,1,1024]{2,1,0:T(1,128)S(1)} %get-tuple-element.11.stat_ref, bf16[1024,256]{1,0:T(8,128)(2,1)S(1)} %get-tuple-element.10.o_ref, ...), custom_call_target="tpu_custom_call" | custom-call | flops 8589934592 | bytes 4194304 | tf_op jit(solution)/shard_map/attention_backward/pallas_call | solution.py:164
  139.5 0.0 all-to-all-done.6
  139.5 5.4 %all-to-all-start.4 = ((bf16[8,3,128,256]{3,2,1,0:T(8,128)(2,1)}), bf16[8,3,128,256]{3,2,1,0:T(8,128)(2,1)S(1)}, u32[]{:S(2)}, u32[]{:S(2)}) async-start(bf16[8,3,128,256]{3,2,1,0:T(8,128)(2,1)} %attention_backward.1), calls=%async_computation.4 | async-start | bytes 3145728 | tf_op jit(solution)/shard_map/all_to_all | solution.py:268
  144.9 3.8 %convolution_convert_fusion = bf16[1024,1024]{1,0:T(8,128)(2,1)} fusion(bf16[1024,512]{1,0:T(8,128)(2,1)} %constant_dynamic-update-slice_fusion, bf16[1024,512]{1,0:T(8,128)(2,1)S(1)} %bitcast.65), kind=kOutput, calls=%fused_computation.1 | convolution fusion | flops 1074790400 | bytes 4194304 | tf_op jit(solution)/shard_map/dot_general | solution.py:29
  148.7 16.3 %all-to-all-done.4.in_ref = bf16[8,3,128,256]{3,2,1,0:T(8,128)(2,1)S(1)} async-done(((bf16[8,3,128,256]{3,2,1,0:T(8,128)(2,1)}), bf16[8,3,128,256]{3,2,1,0:T(8,128)(2,1)S(1)}, u32[]{:S(2)}, u32[]{:S(2)}) %all-to-all-start.4) | async-done | bytes 1572896 | tf_op jit(solution)/shard_map/all_to_all | solution.py:268
  165.0 1.1 copy-done.2
  166.2 3.6 %all-to-all-start.2 = ((bf16[8,128,1024]{2,1,0:T(8,128)(2,1)}), bf16[8,128,1024]{2,1,0:T(8,128)(2,1)S(1)}, u32[]{:S(2)}, u32[]{:S(2)}) async-start(bf16[8,128,1024]{2,1,0:T(8,128)(2,1)} %bitcast.61), calls=%async_computation.2 | async-start | bytes 4194304 | tf_op jit(solution)/shard_map/all_to_all | solution.py:272
  169.8 0.1 reshape.298
  169.9 0.4 rev.7
  170.3 0.1 broadcast_select_fusion
  170.4 0.1 copy.34
  170.5 0.7 reshape.299
  171.2 5.4 %unpack_heads.1 = (bf16[128,2048]{1,0:T(8,128)(2,1)}, bf16[128,2048]{1,0:T(8,128)(2,1)}, bf16[128,2048]{1,0:T(8,128)(2,1)}) custom-call(bf16[8,3,128,256]{3,2,1,0:T(8,128)(2,1)} %copy-done.2), custom_call_target="tpu_custom_call" | custom-call | bytes 3145728 | tf_op jit(solution)/shard_map/unpack_heads/pallas_call | solution.py:192
  176.6 19.4 %all-to-all-done.2.in_ref = bf16[8,128,1024]{2,1,0:T(8,128)(2,1)S(1)} async-done(((bf16[8,128,1024]{2,1,0:T(8,128)(2,1)}), bf16[8,128,1024]{2,1,0:T(8,128)(2,1)S(1)}, u32[]{:S(2)}, u32[]{:S(2)}) %all-to-all-start.2) | async-done | bytes 2097184 | tf_op jit(solution)/shard_map/all_to_all | solution.py:272
  196.0 1.3 finish_mixed.1
  (23 shorter events, 0.2 us)
Async XLA Ops:
  2.3 10.2 %all-to-all-start.1 = ((bf16[4,16,512]{2,1,0:T(8,128)(2,1)}), bf16[4,16,512]{2,1,0:T(8,128)(2,1)S(1)}, u32[]{:S(2)}, u32[]{:S(2)}) async-start(bf16[4,16,512]{2,1,0:T(8,128)(2,1)} %reshape.292), calls=%async_computation.1 | async-start | bytes 131072 | tf_op jit(solution)/shard_map/all_to_all | solution.py:236
  12.2 5.9 %copy-start = (bf16[1,128,2048]{2,1,0:T(8,128)(2,1)S(1)}, bf16[1,128,2048]{2,1,0:T(8,128)(2,1)}, u32[]{:S(2)}) copy-start(bf16[1,128,2048]{2,1,0:T(8,128)(2,1)} %param.11) | copy-start | bytes 1572868
  12.5 25.4 %all-to-all-start = ((bf16[8,3,128,256]{3,2,1,0:T(8,128)(2,1)}), bf16[8,3,128,256]{3,2,1,0:T(8,128)(2,1)S(1)}, u32[]{:S(2)}, u32[]{:S(2)}) async-start(bf16[8,3,128,256]{3,2,1,0:T(8,128)(2,1)} %pack_heads.1), calls=%async_computation | async-start | bytes 3145728 | tf_op jit(solution)/shard_map/all_to_all | solution.py:258
  18.0 1.9 copy-start.6
  18.0 2.0 copy-start.7
  37.9 55.8 %all-to-all-start.3 = ((bf16[8,128,1024]{2,1,0:T(8,128)(2,1)}), bf16[8,128,1024]{2,1,0:T(8,128)(2,1)}, u32[]{:S(2)}, u32[]{:S(2)}) async-start(bf16[8,128,1024]{2,1,0:T(8,128)(2,1)} %cot_halves.1), calls=%async_computation.3 | async-start | bytes 4194304 | tf_op jit(solution)/shard_map/all_to_all | solution.py:260
  42.3 1.3 collective-permute-start.1
  43.6 27.4 %collective-permute-start.2 = (bf16[2,64,512]{2,1,0:T(8,128)(2,1)S(1)}, bf16[2,64,512]{2,1,0:T(8,128)(2,1)S(1)}, u32[]{:S(2)}, u32[]{:S(2)}) collective-permute-start(bf16[2,64,512]{2,1,0:T(8,128)(2,1)S(1)} %maximum_select_fusion.3), channel_id=1, source_target_pairs={{0,16},{16,0},{1,17},{17,1},{2,18},{18,2},{3,19},{19,3},{4,20},{20... | collective-permute-start | bytes 393224 | tf_op jit(solution)/shard_map/ppermute | solution.py:241
  71.0 15.2 %collective-permute-start.3 = (bf16[2,2,64,512]{3,2,1,0:T(8,128)(2,1)S(1)}, bf16[2,2,64,512]{3,2,1,0:T(8,128)(2,1)S(1)}, u32[]{:S(2)}, u32[]{:S(2)}) collective-permute-start(bf16[2,2,64,512]{3,2,1,0:T(8,128)(2,1)S(1)} %maximum_select_fusion.1), channel_id=1, source_target_pairs={{0,32},{32,64},{64,96},{96,0},{1,33},{33,65},{65,97},{97,1},{2,34}... | collective-permute-start | bytes 786440 | tf_op jit(solution)/shard_map/ppermute | solution.py:244
  80.1 12.7 %collective-permute-start = (bf16[1024,256]{1,0:T(8,128)(2,1)S(1)}, bf16[1024,256]{1,0:T(8,128)(2,1)S(1)}, u32[]{:S(2)}, u32[]{:S(2)}) collective-permute-start(bf16[1024,256]{1,0:T(8,128)(2,1)S(1)} %get-tuple-element.10.o_ref), channel_id=1, source_target_pairs={{0,4},{4,0},{1,5},{5,1},{2,6},{6,2},{3,7},{7,3},{8,12},{12,8},{9,1... | collective-permute-start | bytes 1572872 | tf_op jit(solution)/shard_map/ppermute | solution.py:232
  81.3 24.3 %collective-permute-start.4 = (bf16[2,2,64,512]{3,2,1,0:T(8,128)(2,1)S(1)}, bf16[2,2,64,512]{3,2,1,0:T(8,128)(2,1)S(1)}, u32[]{:S(2)}, u32[]{:S(2)}) collective-permute-start(bf16[2,2,64,512]{3,2,1,0:T(8,128)(2,1)S(1)} %maximum_select_fusion.1), channel_id=1, source_target_pairs={{0,64},{32,96},{64,0},{96,32},{1,65},{33,97},{65,1},{97,33},{2,66}... | collective-permute-start | bytes 786440 | tf_op jit(solution)/shard_map/ppermute | solution.py:244
  85.0 21.4 %collective-permute-start.5 = (bf16[2,2,64,512]{3,2,1,0:T(8,128)(2,1)S(1)}, bf16[2,2,64,512]{3,2,1,0:T(8,128)(2,1)S(1)}, u32[]{:S(2)}, u32[]{:S(2)}) collective-permute-start(bf16[2,2,64,512]{3,2,1,0:T(8,128)(2,1)S(1)} %maximum_select_fusion.1), channel_id=1, source_target_pairs={{0,96},{32,0},{64,32},{96,64},{1,97},{33,1},{65,33},{97,65},{2,98}... | collective-permute-start | bytes 786440 | tf_op jit(solution)/shard_map/ppermute | solution.py:244
  86.2 6.6 %copy-start.3 = (bf16[4,2,2,64,512]{4,3,2,1,0:T(8,128)(2,1)}, bf16[4,2,2,64,512]{4,3,2,1,0:T(8,128)(2,1)S(1)}, u32[]{:S(2)}) copy-start(bf16[4,2,2,64,512]{4,3,2,1,0:T(8,128)(2,1)S(1)} %bitcast_dynamic-update-slice_fusion.2) | copy-start | bytes 3145732
  100.1 24.1 %all-to-all-start.5 = ((bf16[16,64,512]{2,1,0:T(8,128)(2,1)}), bf16[16,64,512]{2,1,0:T(8,128)(2,1)}, u32[]{:S(2)}, u32[]{:S(2)}) async-start(bf16[16,64,512]{2,1,0:T(8,128)(2,1)} %bitcast.60), calls=%async_computation.5 | async-start | bytes 2097152 | tf_op jit(solution)/shard_map/all_to_all | solution.py:275
  107.2 3.7 %copy-start.4 = (bf16[4,2,2,64,512]{4,3,2,1,0:T(8,128)(2,1)S(1)}, bf16[4,2,2,64,512]{4,3,2,1,0:T(8,128)(2,1)}, u32[]{:S(2)}) copy-start(bf16[4,2,2,64,512]{4,3,2,1,0:T(8,128)(2,1)} %bitcast_dynamic-update-slice_fusion) | copy-start | bytes 3145732
  109.6 21.1 %collective-permute-start.6 = (bf16[1024,256]{1,0:T(8,128)(2,1)S(1)}, bf16[1024,256]{1,0:T(8,128)(2,1)S(1)}, u32[]{:S(2)}, u32[]{:S(2)}) collective-permute-start(bf16[1024,256]{1,0:T(8,128)(2,1)S(1)} %fusion.1), channel_id=1, source_target_pairs={{0,4},{4,0},{1,5},{5,1},{2,6},{6,2},{3,7},{7,3},{8,12},{12,8},{9,1... | collective-permute-start | bytes 1572872 | tf_op jit(solution)/shard_map/ppermute | solution.py:232
  126.2 13.2 %all-to-all-start.6 = ((f32[4,16,512]{2,1,0:T(8,128)}), f32[4,16,512]{2,1,0:T(8,128)S(1)}, u32[]{:S(2)}, u32[]{:S(2)}) async-start(f32[4,16,512]{2,1,0:T(8,128)} %bitcast.34), calls=%async_computation.6 | async-start | bytes 262144 | tf_op jit(solution)/shard_map/all_to_all | solution.py:278
  130.7 1.2 copy-start.1
  139.5 5.4 %copy-start.5 = (bf16[4,2,2,64,512]{4,3,2,1,0:T(8,128)(2,1)S(1)}, bf16[4,2,2,64,512]{4,3,2,1,0:T(8,128)(2,1)}, u32[]{:S(2)}) copy-start(bf16[4,2,2,64,512]{4,3,2,1,0:T(8,128)(2,1)} %bitcast_dynamic-update-slice_fusion) | copy-start | bytes 3145732
  139.5 25.6 %all-to-all-start.4 = ((bf16[8,3,128,256]{3,2,1,0:T(8,128)(2,1)}), bf16[8,3,128,256]{3,2,1,0:T(8,128)(2,1)S(1)}, u32[]{:S(2)}, u32[]{:S(2)}) async-start(bf16[8,3,128,256]{3,2,1,0:T(8,128)(2,1)} %attention_backward.1), calls=%async_computation.4 | async-start | bytes 3145728 | tf_op jit(solution)/shard_map/all_to_all | solution.py:268
  165.0 1.1 copy-start.2
  166.2 29.9 %all-to-all-start.2 = ((bf16[8,128,1024]{2,1,0:T(8,128)(2,1)}), bf16[8,128,1024]{2,1,0:T(8,128)(2,1)S(1)}, u32[]{:S(2)}, u32[]{:S(2)}) async-start(bf16[8,128,1024]{2,1,0:T(8,128)(2,1)} %bitcast.61), calls=%async_computation.2 | async-start | bytes 4194304 | tf_op jit(solution)/shard_map/all_to_all | solution.py:272

commit v2 on v1

v2 whole, which is shorter than its diff:
```python
import functools
import math

import jax
import jax.numpy as jnp
from jax import lax
from jax.experimental import pallas as pl
from jax.experimental.pallas import tpu as pltpu
from jax.sharding import Mesh
from jax.sharding import PartitionSpec as P

HS = 128
BLK = 64
NB = 16
LEN = 1024
HD = 2048
SCALE = 1.0 / math.sqrt(HS)
LOG2E = math.log2(math.e)
MASKED = -1e30
CTX = ("xl", "y")
DP = ("z", "xh", "core")
BF = jnp.bfloat16
F32 = jnp.float32
NT = (((1,), (1,)), ((), ()))
NN = (((1,), (0,)), ((), ()))
TN = (((0,), (0,)), ((), ()))


def dot(a, b, dims=NN):
    return lax.dot_general(a, b, dims, preferred_element_type=F32)


def params(mib=48):
    return pltpu.CompilerParams(vmem_limit_bytes=mib * 2**20)


VMEM = pl.BlockSpec(memory_space=pltpu.VMEM)
SMEM = pl.BlockSpec(memory_space=pltpu.SMEM)


def whole(body, name, outs, *args, scalars=0, scratch=(), flops=0):
    one = isinstance(outs[0][0], int)
    made = [jax.ShapeDtypeStruct(*o) for o in ([outs] if one else outs)]
    moved = sum(math.prod(x.shape) * x.dtype.itemsize for x in args)
    moved += sum(math.prod(x.shape) * x.dtype.itemsize for x in made)
    given = pl.pallas_call(
        body,
        in_specs=[SMEM] * scalars + [VMEM] * (len(args) - scalars),
        out_specs=[VMEM] * len(made),
        out_shape=made,
        scratch_shapes=list(scratch),
        compiler_params=params(),
        cost_estimate=pl.CostEstimate(flops=flops, bytes_accessed=moved, transcendentals=0),
        name=name,
    )(*args)
    return given[0] if one else given


def ring(size, step):
    return [(i, (i + step) % size) for i in range(size)]


def swap(array, axis="xl"):
    return lax.ppermute(array, axis, ring(2, 1))


def pack_kernel(q_ref, k_ref, v_ref, out_ref):
    for c in range(8):
        cols = slice(256 * c, 256 * c + 256)
        out_ref[c, 0] = q_ref[:, cols]
        out_ref[c, 1] = k_ref[:, cols]
        out_ref[c, 2] = v_ref[:, cols]


def pack_heads(q, k, v):
    return whole(pack_kernel, "pack_heads", ((8, 3, 128, 256), BF), q, k, v)


def halves_kernel(at_ref, cot_ref, own_ref, other_ref):
    low = lax.broadcasted_iota(jnp.int32, (128, 128), 1) < 64
    mine = at_ref[3] == 0
    for pair in range(8):
        a = cot_ref[:, 256 * pair : 256 * pair + 128].astype(F32)
        b = cot_ref[:, 256 * pair + 128 : 256 * pair + 256].astype(F32)
        first = jnp.where(low, a, pltpu.roll(b, 64, 1))
        second = jnp.where(low, pltpu.roll(a, 64, 1), b)
        cols = slice(128 * pair, 128 * pair + 128)
        own_ref[:, cols] = jnp.where(mine, first, second).astype(BF)
        other_ref[:, cols] = jnp.where(mine, second, first).astype(BF)


def cot_halves(at, cot):
    half = ((128, 1024), BF)
    return whole(halves_kernel, "cot_halves", (half, half), at, cot, scalars=1)


def copies_kernel(at_ref, own_ref, recv_ref, out_ref):
    xl = at_ref[3]
    for y in range(4):
        out_ref[y, xl] = own_ref[...]
        out_ref[y, 1 - xl] = recv_ref[...]


def cot_copies(at, own, recv):
    return whole(copies_kernel, "cot_copies", ((4, 2, 128, 1024), BF), at, own, recv, scalars=1)


def weight_kernel(at_ref, *refs):
    z, xh, core, y = at_ref[0], at_ref[1], at_ref[2], at_ref[4]
    out_ref = refs[-1]
    for step in range(4):
        for h in range(2):
            for k in range(2):
                for b in range(4):
                    zs, ys = lax.rem(z - step + 4, 4), lax.rem(y - b + 4, 4)
                    hs, ks = lax.rem(xh + h, 2), lax.rem(core + k, 2)
                    row = pl.multiple_of(64 * (4 * zs + 2 * hs + ks) + 16 * ys, 16)
                    out_ref[pl.ds(row, 16), :] = refs[step][h, k, b]


def gather_weight(at, own):
    y = at[4]
    parts = [lax.dynamic_index_in_dim(own, y, 0, False)]
    for step in (1, 2, 3):
        piece = lax.dynamic_index_in_dim(own, (y + step) % 4, 0, False)
        parts.append(lax.ppermute(piece, "y", ring(4, step)))
    rows = jnp.stack(parts)
    pair = jnp.stack([rows, swap(rows, "core")])
    quad = jnp.stack([pair, swap(pair, "xh")])
    far = [lax.ppermute(quad, "z", ring(4, step)) for step in (1, 2, 3)]
    return whole(weight_kernel, "place_weight", ((1024, 512), BF), at, quad, *far, scalars=1)


def head_cot_kernel(cot_ref, w_ref, keep_ref, send_ref):
    for y in range(4):
        rows = cot_ref[y].reshape(256, 1024)
        part = dot(rows, w_ref[...])
        for xl in range(2):
            at = slice(128 * (4 * xl + y), 128 * (4 * xl + y) + 128)
            keep_ref[at, :] = part[128 * xl : 128 * xl + 128, :256]
            send_ref[at, :] = part[128 * xl : 128 * xl + 128, 256:].astype(BF)


def head_cot_parts(cot, weight):
    return whole(
        head_cot_kernel, "head_cot", (((LEN, 256), F32), ((LEN, 256), BF)), cot, weight, flops=2**30
    )


def mixed_part_kernel(own_ref, other_ref, w_ref, out_ref):
    for y in range(4):
        for xl in range(2):
            at = slice(128 * (4 * xl + y), 128 * (4 * xl + y) + 128)
            part = dot(own_ref[at, :], w_ref[:, :256], NT) + dot(other_ref[at, :], w_ref[:, 256:], NT)
            out_ref[y, xl] = part.astype(BF)


def mixed_parts(own, other, weight):
    return whole(
        mixed_part_kernel, "mixed_part", ((4, 2, 128, 1024), BF), own, other, weight, flops=2**30
    )


def mixed_sum_kernel(at_ref, in_ref, keep_ref, send_ref):
    xl = at_ref[3]
    keep_ref[...] = sum(in_ref[y, xl].astype(F32) for y in range(4)).astype(BF)
    send_ref[...] = sum(in_ref[y, 1 - xl].astype(F32) for y in range(4)).astype(BF)


def mixed_sum(at, parts):
    half = ((128, 1024), BF)
    return whole(mixed_sum_kernel, "mixed_sum", (half, half), at, parts, scalars=1)


def mixed_join_kernel(at_ref, own_ref, recv_ref, out_ref):
    low = lax.broadcasted_iota(jnp.int32, (128, 128), 1) < 64
    mine = at_ref[3] == 0
    for pair in range(8):
        cols = slice(128 * pair, 128 * pair + 128)
        own, recv = own_ref[:, cols].astype(F32), recv_ref[:, cols].astype(F32)
        first = jnp.where(mine, own, recv)
        second = jnp.where(mine, recv, own)
        out_ref[:, 256 * pair : 256 * pair + 128] = jnp.where(low, first, pltpu.roll(second, 64, 1)).astype(BF)
        out_ref[:, 256 * pair + 128 : 256 * pair + 256] = jnp.where(low, pltpu.roll(first, 64, 1), second).astype(BF)


def mixed_join(at, own, recv):
    return whole(mixed_join_kernel, "mixed_join", ((128, HD), BF), at, own, recv, scalars=1)


def weight_grad_kernel(at_ref, cot_ref, own_ref, other_ref, keep_ref, send_ref, pair_ref, sum_ref):
    core = at_ref[2]
    for y in range(4):
        for xl in range(2):
            at = slice(128 * (4 * xl + y), 128 * (4 * xl + y) + 128)
            to = slice(128 * (2 * y + xl), 128 * (2 * y + xl) + 128)
            pair_ref[to, :256] = own_ref[at, :]
            pair_ref[to, 256:] = other_ref[at, :]
    sum_ref[...] = dot(cot_ref[...].reshape(LEN, 1024), pair_ref[...], TN).reshape(16, 64, 512)
    for d in range(8):
        keep_ref[d] = sum_ref[2 * d + core]
        send_ref[d] = sum_ref[2 * d + 1 - core].astype(BF)


def add_xh_kernel(at_ref, keep_ref, recv_ref, out_ref, send_ref):
    xh = at_ref[1]
    for z in range(4):
        out_ref[z] = keep_ref[2 * z + xh] + recv_ref[2 * z + xh].astype(F32)
        send_ref[z] = (keep_ref[2 * z + 1 - xh] + recv_ref[2 * z + 1 - xh].astype(F32)).astype(BF)


def add_z_kernel(at_ref, keep_ref, recv_ref, out_ref, *send_refs):
    z = at_ref[0]
    out_ref[...] = keep_ref[z] + recv_ref[z].astype(F32)
    for step, ref in enumerate(send_refs, 1):
        to = lax.rem(z + step, 4)
        ref[...] = (keep_ref[to] + recv_ref[to].astype(F32)).astype(BF)


def add_y_kernel(scale, at_ref, own_ref, a_ref, b_ref, c_ref, sum_ref, out_ref, *send_refs):
    y = at_ref[4]
    sum_ref[...] = (own_ref[...] + a_ref[...].astype(F32) + b_ref[...].astype(F32) + c_ref[...].astype(F32)) * scale
    for step, ref in enumerate((out_ref, *send_refs)):
        ref[...] = sum_ref[pl.ds(pl.multiple_of(16 * lax.rem(y + step, 4), 16), 16), :]


def rows_kernel(at_ref, *refs):
    xl, y = at_ref[3], at_ref[4]
    out_ref = refs[-1]
    for step in range(4):
        for side in range(2):
            col = 1024 * lax.rem(xl + side, 2) + 256 * lax.rem(y - step + 4, 4)
            out_ref[:, pl.ds(pl.multiple_of(col, 256), 256)] = refs[step][:, 256 * side : 256 * side + 256]


def weight_grad(at, cot, own, other, scale):
    keep, send = whole(
        weight_grad_kernel,
        "weight_grad",
        (((8, 64, 512), F32), ((8, 64, 512), BF)),
        at,
        cot,
        own,
        other,
        scalars=1,
        scratch=(pltpu.VMEM((LEN, 512), BF), pltpu.VMEM((16, 64, 512), F32)),
        flops=2**30,
    )
    keep, send = whole(
        add_xh_kernel,
        "add_core",
        (((4, 64, 512), F32), ((4, 64, 512), BF)),
        at,
        keep,
        swap(send, "core"),
        scalars=1,
    )
    piece = ((64, 512), BF)
    keep, *sends = whole(
        add_z_kernel,
        "add_xh",
        (((64, 512), F32), piece, piece, piece),
        at,
        keep,
        swap(send, "xh"),
        scalars=1,
    )
    got = [lax.ppermute(send, "z", ring(4, step)) for step, send in enumerate(sends, 1)]
    piece = ((16, 512), F32)
    total, *pieces = whole(
        functools.partial(add_y_kernel, scale),
        "add_z",
        (((64, 512), F32), piece, piece, piece, piece),
        at,
        keep,
        *got,
        scalars=1,
    )
    got = [lax.ppermute(send, "y", ring(4, step)) for step, send in enumerate(pieces[1:], 1)]
    return whole(rows_kernel, "place_rows", ((16, HD), F32), at, pieces[0], *got, scalars=1)


def live_bias(rand, glob):
    kb = jnp.arange(NB, dtype=jnp.int32)[:, None]
    qb = jnp.arange(NB, dtype=jnp.int32)[None, :]
    live = (jnp.abs(kb - qb) <= 1) | jnp.any(kb[:, :, None] == glob[None, None, :], axis=-1)
    by_rand = jnp.any(rand.transpose(0, 2, 1)[:, :, None, :] == kb[None, None], axis=1)
    bias = jnp.where(live[None] | by_rand, 0.0, MASKED).astype(F32)
    return jnp.repeat(bias, BLK, axis=2)


TILE = 256


def scores_at(k, q, bias):
    s = dot(k, q, NT).reshape(NB, BLK, TILE)
    return s * (SCALE * LOG2E) + bias[:, None, :]


def forward_kernel(qkv_ref, bias_ref, o_ref, stat_ref):
    k = qkv_ref[:, 1].reshape(LEN, HS)
    v_t = qkv_ref[:, 2].reshape(LEN, HS).T
    for t in range(LEN // TILE):
        tok = slice(TILE * t, TILE * t + TILE)
        q = qkv_ref[2 * t : 2 * t + 2, 0].reshape(TILE, HS)
        s = scores_at(k, q, bias_ref[0, :, tok])
        top = jnp.max(s, axis=(0, 1), keepdims=True)
        p = jnp.exp2(s - top)
        total = jnp.sum(p, axis=(0, 1), keepdims=True)
        p_low = (p * (1.0 / total)).astype(BF).reshape(LEN, TILE)
        o_t = dot(v_t, p_low)
        o_ref[tok, :] = o_t.T.astype(BF)
        stat_ref[0, :, tok] = (top + jnp.log2(total))[0]


def forward(qkv, bias):
    return pl.pallas_call(
        forward_kernel,
        grid=(2,),
        in_specs=[
            pl.BlockSpec((8, 3, 128, HS), lambda h: (0, 0, 0, h)),
            pl.BlockSpec((1, NB, LEN), lambda h: (h, 0, 0)),
        ],
        out_specs=[
            pl.BlockSpec((LEN, HS), lambda h: (0, h)),
            pl.BlockSpec((1, 1, LEN), lambda h: (h, 0, 0)),
        ],
        out_shape=[
            jax.ShapeDtypeStruct((LEN, 2 * HS), BF),
            jax.ShapeDtypeStruct((2, 1, LEN), F32),
        ],
        compiler_params=params(),
        cost_estimate=pl.CostEstimate(flops=4 * 2**30, bytes_accessed=2**21, transcendentals=2**21),
        name="attention_forward",
    )(qkv, bias)


def backward_kernel(qkv_ref, bias_ref, stat_ref, o_ref, keep_ref, recv_ref, out_ref, dk_ref, dv_ref):
    k = qkv_ref[:, 1].reshape(LEN, HS)
    v = qkv_ref[:, 2].reshape(LEN, HS)
    k_t = k.T
    for t in range(LEN // TILE):
        tok = slice(TILE * t, TILE * t + TILE)
        q = qkv_ref[2 * t : 2 * t + 2, 0].reshape(TILE, HS)
        do = (keep_ref[tok, :] + recv_ref[tok, :].astype(F32)).astype(BF)
        delta = jnp.sum((do.astype(F32) * o_ref[tok, :].astype(F32)).T, axis=0, keepdims=True)
        p = jnp.exp2(scores_at(k, q, bias_ref[0, :, tok] - stat_ref[0, :, tok]))
        p = p.reshape(LEN, TILE)
        dp = dot(v, do, NT)
        ds = (p * (dp - delta)).astype(BF)
        dq = dot(k_t, ds).T * SCALE
        out_ref[2 * t : 2 * t + 2, 0] = dq.astype(BF).reshape(2, 128, HS)
        dk = dot(ds, q)
        dv = dot(p.astype(BF), do)
        if t == 0:
            dk_ref[...] = dk
            dv_ref[...] = dv
        else:
            dk_ref[...] += dk
            dv_ref[...] += dv
    out_ref[:, 1] = (dk_ref[...] * SCALE).astype(BF).reshape(8, 128, HS)
    out_ref[:, 2] = dv_ref[...].astype(BF).reshape(8, 128, HS)


def backward(qkv, bias, stat, attended, keep, recv):
    wide = pl.BlockSpec((LEN, HS), lambda h: (0, h))
    heads = pl.BlockSpec((8, 3, 128, HS), lambda h: (0, 0, 0, h))
    return pl.pallas_call(
        backward_kernel,
        grid=(2,),
        in_specs=[
            heads,
            pl.BlockSpec((1, NB, LEN), lambda h: (h, 0, 0)),
            pl.BlockSpec((1, 1, LEN), lambda h: (h, 0, 0)),
            wide,
            wide,
            wide,
        ],
        out_specs=heads,
        out_shape=jax.ShapeDtypeStruct((8, 3, 128, 2 * HS), BF),
        scratch_shapes=[pltpu.VMEM((LEN, HS), F32), pltpu.VMEM((LEN, HS), F32)],
        compiler_params=params(),
        cost_estimate=pl.CostEstimate(flops=8 * 2**30, bytes_accessed=2**22, transcendentals=2**21),
        name="attention_backward",
    )(qkv, bias, stat, attended, keep, recv)


def unpack_kernel(in_ref, q_ref, k_ref, v_ref):
    for c in range(8):
        cols = slice(256 * c, 256 * c + 256)
        q_ref[:, cols] = in_ref[c, 0]
        k_ref[:, cols] = in_ref[c, 1]
        v_ref[:, cols] = in_ref[c, 2]


def unpack_heads(grads):
    out = ((128, HD), BF)
    return whole(unpack_kernel, "unpack_heads", (out, out, out), grads)


def on_device(queries, keys, values, out_weight, cotangent, rand_blocks, glob_blocks):
    at = jnp.stack([lax.axis_index(name) for name in DP + CTX]).astype(jnp.int32)
    xl = at[3]
    sides = out_weight.reshape(16, 2, 1024)
    sides = jnp.where(xl == 0, sides, sides[:, ::-1])
    own_rows = sides.reshape(16, 2, 4, 256).transpose(2, 0, 1, 3).reshape(4, 16, 512)

    qkv = lax.all_to_all(pack_heads(queries[0], keys[0], values[0]), CTX, 0, 0, tiled=True)
    own, other = cot_halves(at, cotangent[0])
    cot = lax.all_to_all(cot_copies(at, own, swap(other)), "y", 0, 0, tiled=True)
    weight = gather_weight(at, own_rows)

    bias = live_bias(rand_blocks[0], glob_blocks[0])
    attended, stat = forward(qkv, bias)
    attended_other = swap(attended)
    keep, send = head_cot_parts(cot, weight)
    grads = backward(qkv, bias, stat, attended, keep, swap(send))
    grads = lax.all_to_all(grads, CTX, 0, 0, tiled=True)

    part = lax.all_to_all(mixed_parts(attended, attended_other, weight), "y", 0, 0, tiled=True)
    own, other = mixed_sum(at, part)
    mixed = mixed_join(at, own, swap(other))

    total_tokens = lax.axis_size(DP) * lax.axis_size(CTX) * cotangent.shape[1]
    rows = weight_grad(at, cot, attended, attended_other, 1.0 / math.sqrt(total_tokens))

    grad_q, grad_k, grad_v = unpack_heads(grads)
    return (mixed[None], grad_q[None], grad_k[None], grad_v[None], rows)


def solution(mesh):
    fine = Mesh(mesh.devices.reshape(4, 2, 2, 2, 4), ("z", "xh", "core", "xl", "y"))
    tokens = P(DP, CTX, None)
    return jax.shard_map(
        on_device,
        mesh=fine,
        in_specs=(tokens, tokens, tokens, P(DP + CTX, None), tokens, P(DP, CTX, None, None), P(DP, None)),
        out_specs=(tokens, tokens, tokens, tokens, P(DP + CTX, None)),
        check_vma=False,
    )
```

time: 199 us -> 180 us (0.905)
  matrix products: 13.7 us -> 0 us
  waiting for transfers between devices: 86.8 us -> 78.4 us
  between operations: 8.66 us -> 0.97 us
  starting transfers between devices: 45.3 us -> 52.1 us
  Pallas kernels: 28.6 us -> 33.6 us
  local copies, waits for them, and re-layouts: 11.8 us -> 14.1 us
  other arithmetic: 2.45 us -> 0.26 us
    ppermute x7 -> x20, waiting for transfers between devices: 23 us -> 76.6 us  [the longest x8 59.4 us: swap(): return lax.ppermute(array, axis, ring(2, 1))]
    all_to_all x5 -> x2, waiting for transfers between devices: 29.8 us -> 1.76 us  [the longest x1 1.76 us: on_device(): lax.all_to_all(mixed_parts(attended, attended_other, weight), 'y', 0, 0,...]
    ppermute x7 -> x20, starting transfers between devices: 12 us -> 33.1 us  [the longest x8 9.36 us: swap(): return lax.ppermute(array, axis, ring(2, 1))]
    all_to_all x1, waiting for transfers between devices: 17.7 us -> 0.01 us  [on_device(): lax.all_to_all(pack_heads(queries[0], keys[0], values[0]), CTX, 0, 0, til...]
    all_to_all x1, waiting for transfers between devices: 16.3 us -> 0.01 us  [on_device(): grads = lax.all_to_all(grads, CTX, 0, 0, tiled=True)]
    dot_general x4 -> x0, matrix products: 13.7 us -> none  [dot(): return lax.dot_general(a, b, dims, preferred_element_type=F32)]
    all_to_all x5 -> x2, starting transfers between devices: 22.4 us -> 9.09 us  [the longest x1 4.79 us: on_device(): lax.all_to_all(mixed_parts(attended, attended_other, weight), 'y', 0, 0,...]
    unnamed x17 -> x40, local copies, waits for them, and re-layouts: 3.31 us -> 13.6 us
  transfers between devices with their start and end apart: 14 -> 24, of which waited for: 9 -> 13; matrix products, arithmetic and copies ran while one was open for 12% -> 0% of each run, Pallas kernels for 14% -> 17%
where the time goes in v2:
time: 180 us; the launch traced here: 179 us
  waiting for transfers between devices  78.4 us (44%)
  starting transfers between devices  52.1 us (29%)
  Pallas kernels  33.6 us (19%)
  local copies, waits for them, and re-layouts  14.1 us (8%)
    ppermute x8, waiting for transfers between devices, swap(): return lax.ppermute(array, axis, ring(2, 1))  59.4 us
    pallas_call x14, Pallas kernels, whole(): pl.pallas_call(body, in_specs=[SMEM] * scalars + [VMEM] * (len(args) - sc...  19.6 us
    unnamed x40, local copies, waits for them, and re-layouts  13.6 us
    ppermute x3, waiting for transfers between devices, gather_weight(): far = [lax.ppermute(quad, 'z', ring(4, step)) for step in (1, 2, 3)]  10.5 us
    ppermute x8, starting transfers between devices, swap(): return lax.ppermute(array, axis, ring(2, 1))  9.36 us
    pallas_call x1, Pallas kernels, forward(): pl.pallas_call(forward_kernel, grid=(2,), in_specs=[pl.BlockSpec((8, 3, 1...  7.15 us
    pallas_call x1, Pallas kernels, backward(): pl.pallas_call(backward_kernel, grid=(2,), in_specs=[heads, pl.BlockSpec(...  6.87 us
    ppermute x3, starting transfers between devices, gather_weight(): far = [lax.ppermute(quad, 'z', ring(4, step)) for step in (1, 2, 3)]  6.58 us
  transfers between devices with their start and end apart: 24, of which 13 were waited for; matrix products, arithmetic and copies ran while one was open for 0% of the time, Pallas kernels for 17%

profile of v2, /device:TPU:0, one launch (start us, length us, event | category | flops | bytes accessed | tf_op | source)
XLA Modules:
  0.0 179.5 jit_solution(13104433043543128661)
XLA Ops:
  0.6 1.0 copy-done.9
  1.7 1.0 copy-done.10
  2.7 1.0 copy-done.11
  3.8 1.3 pack_heads.1
  5.1 5.6 %all-to-all-start = ((bf16[8,3,128,256]{3,2,1,0:T(8,128)(2,1)}), bf16[8,3,128,256]{3,2,1,0:T(8,128)(2,1)S(1)}, u32[]{:S(2)}, u32[]{:S(2)}) async-start(bf16[8,3,128,256]{3,2,1,0:T(8,128)(2,1)} %pack_heads.1), calls=%async_computation | async-start | bytes 3145728 | tf_op jit(solution)/shard_map/all_to_all | solution.py:408
  10.8 0.8 cot_halves.1
  11.6 2.1 %collective-permute-start.10 = (bf16[128,1024]{1,0:T(8,128)(2,1)S(1)}, bf16[128,1024]{1,0:T(8,128)(2,1)S(1)}, u32[]{:S(2)}, u32[]{:S(2)}) collective-permute-start(bf16[128,1024]{1,0:T(8,128)(2,1)S(1)} %get-tuple-element.33), channel_id=1, source_target_pairs={{0,4},{4,0},{1,5},{5,1},{2,6},{6,2},{3,7},{7,3},{8,12},{12,8},{9,1... | collective-permute-start | bytes 786440 | tf_op jit(solution)/shard_map/ppermute | solution.py:64
  13.9 1.5 collective-permute-start.1
  15.5 2.7 %collective-permute-start.2 = (bf16[16,512]{1,0:T(8,128)(2,1)S(1)}, bf16[16,512]{1,0:T(8,128)(2,1)S(1)}, u32[]{:S(2)}, u32[]{:S(2)}) collective-permute-start(bf16[16,512]{1,0:T(8,128)(2,1)S(1)} %get-tuple-element.57), channel_id=1, source_target_pairs={{0,2},{1,3},{2,0},{3,1},{4,6},{5,7},{6,4},{7,5},{8,10},{9,11},{10,... | collective-permute-start | bytes 49160 | tf_op jit(solution)/shard_map/ppermute | solution.py:126
  18.1 1.5 collective-permute-start.3
  19.6 0.1 compare_reduce_fusion
  19.8 15.8 %collective-permute-done.10.recv_ref = bf16[128,1024]{1,0:T(8,128)(2,1)S(1)} collective-permute-done((bf16[128,1024]{1,0:T(8,128)(2,1)S(1)}, bf16[128,1024]{1,0:T(8,128)(2,1)S(1)}, u32[]{:S(2)}, u32[]{:S(2)}) %collective-permute-start.10) | collective-permute-done | bytes 262176 | tf_op jit(solution)/shard_map/ppermute | solution.py:64
  35.6 2.1 %cot_copies.1 = bf16[4,2,128,1024]{3,2,1,0:T(8,128)(2,1)} custom-call(s32[5]{0:T(128)S(1)} %stack.54.at_ref, bf16[128,1024]{1,0:T(8,128)(2,1)S(1)} %get-tuple-element.32.own_ref, bf16[128,1024]{1,0:T(8,128)(2,1)S(1)} %collective-permute-done.10.recv_ref), custom_call_target="tpu_custom_call" | custom-call | bytes 2621460 | tf_op jit(solution)/shard_map/cot_copies/pallas_call | solution.py:46
  37.7 1.2 copy-done.4
  38.9 4.3 %all-to-all-start.2 = ((bf16[4,2,128,1024]{3,2,1,0:T(8,128)(2,1)}), bf16[4,2,128,1024]{3,2,1,0:T(8,128)(2,1)S(1)}, u32[]{:S(2)}, u32[]{:S(2)}) async-start(bf16[4,2,128,1024]{3,2,1,0:T(8,128)(2,1)} %cot_copies.1), calls=%async_computation.2 | async-start | bytes 4194304 | tf_op jit(solution)/shard_map/all_to_all | solution.py:410
  43.2 0.1 broadcast_in_dim.29
  43.3 0.1 reshape.88.bias_ref
  43.6 1.4 copy-done.5
  45.0 7.1 %attention_forward.1 = (bf16[1024,256]{1,0:T(8,128)(2,1)S(1)}, f32[2,1,1024]{2,1,0:T(1,128)S(1)}) custom-call(bf16[8,3,128,256]{3,2,1,0:T(8,128)(2,1)S(1)} %copy-done.5, f32[2,16,1024]{2,1,0:T(8,128)S(1)} %reshape.88.bias_ref), custom_call_target="tpu_custom_call" | custom-call | flops 4294967296 | bytes 2097152 | tf_op jit(solution)/shard_map/attention_forward/pallas_call | solution.py:317
  52.2 0.6 collective-permute-start
  52.8 2.8 %collective-permute-start.5 = (bf16[2,4,16,512]{3,2,1,0:T(8,128)(2,1)S(1)}, bf16[2,4,16,512]{3,2,1,0:T(8,128)(2,1)S(1)}, u32[]{:S(2)}, u32[]{:S(2)}) collective-permute-start(bf16[2,4,16,512]{3,2,1,0:T(8,128)(2,1)S(1)} %get-tuple-element.52), channel_id=1, source_target_pairs={{0,16},{16,0},{1,17},{17,1},{2,18},{18,2},{3,19},{19,3},{4,20},{20... | collective-permute-start | bytes 393224 | tf_op jit(solution)/shard_map/ppermute | solution.py:64
  55.6 15.0 %collective-permute-done.5 = bf16[2,4,16,512]{3,2,1,0:T(8,128)(2,1)S(1)} collective-permute-done((bf16[2,4,16,512]{3,2,1,0:T(8,128)(2,1)S(1)}, bf16[2,4,16,512]{3,2,1,0:T(8,128)(2,1)S(1)}, u32[]{:S(2)}, u32[]{:S(2)}) %collective-permute-start.5) | collective-permute-done | bytes 131104 | tf_op jit(solution)/shard_map/ppermute | solution.py:64
  70.6 2.0 %collective-permute-start.6 = (bf16[2,2,4,16,512]{4,3,2,1,0:T(8,128)(2,1)S(1)}, bf16[2,2,4,16,512]{4,3,2,1,0:T(8,128)(2,1)S(1)}, u32[]{:S(2)}, u32[]{:S(2)}) collective-permute-start(bf16[2,2,4,16,512]{4,3,2,1,0:T(8,128)(2,1)S(1)} %pad_maximum_fusion.refs_0_), channel_id=1, source_target_pairs={{0,32},{32,64},{64,96},{96,0},{1,33},{33,65},{65,97},{97,1},{2,34}... | collective-permute-start | bytes 786440 | tf_op jit(solution)/shard_map/ppermute | solution.py:130
  72.6 3.6 %collective-permute-start.7 = (bf16[2,2,4,16,512]{4,3,2,1,0:T(8,128)(2,1)S(1)}, bf16[2,2,4,16,512]{4,3,2,1,0:T(8,128)(2,1)S(1)}, u32[]{:S(2)}, u32[]{:S(2)}) collective-permute-start(bf16[2,2,4,16,512]{4,3,2,1,0:T(8,128)(2,1)S(1)} %pad_maximum_fusion.refs_0_), channel_id=1, source_target_pairs={{0,64},{32,96},{64,0},{96,32},{1,65},{33,97},{65,1},{97,33},{2,66}... | collective-permute-start | bytes 786440 | tf_op jit(solution)/shard_map/ppermute | solution.py:130
  76.2 1.0 collective-permute-start.8
  77.2 3.8 %collective-permute-done.6.refs_1_ = bf16[2,2,4,16,512]{4,3,2,1,0:T(8,128)(2,1)S(1)} collective-permute-done((bf16[2,2,4,16,512]{4,3,2,1,0:T(8,128)(2,1)S(1)}, bf16[2,2,4,16,512]{4,3,2,1,0:T(8,128)(2,1)S(1)}, u32[]{:S(2)}, u32[]{:S(2)}) %collective-permute-start.6) | collective-permute-done | bytes 262176 | tf_op jit(solution)/shard_map/ppermute | solution.py:130
  81.0 6.7 %collective-permute-done.7.refs_2_ = bf16[2,2,4,16,512]{4,3,2,1,0:T(8,128)(2,1)S(1)} collective-permute-done((bf16[2,2,4,16,512]{4,3,2,1,0:T(8,128)(2,1)S(1)}, bf16[2,2,4,16,512]{4,3,2,1,0:T(8,128)(2,1)S(1)}, u32[]{:S(2)}, u32[]{:S(2)}) %collective-permute-start.7) | collective-permute-done | bytes 262176 | tf_op jit(solution)/shard_map/ppermute | solution.py:130
  87.7 0.7 place_weight.1.w_ref
  88.5 2.8 %mixed_part.1 = bf16[4,2,128,1024]{3,2,1,0:T(8,128)(2,1)S(1)} custom-call(bf16[1024,256]{1,0:T(8,128)(2,1)S(1)} %get-tuple-element.28.own_ref.o_ref, bf16[1024,256]{1,0:T(8,128)(2,1)S(1)} %collective-permute-done.other_ref, bf16[1024,512]{1,0:T(8,128)(2,1)S(1)} %place_weight.1.w_ref), custom_call_target="tpu_custom_call" | custom-call | flops 1073741824 | bytes 4194304 | tf_op jit(solution)/shard_map/mixed_part/pallas_call | solution.py:46
  91.3 1.3 copy-done
  92.6 0.8 copy-done.15
  93.4 1.4 copy-done.1
  94.8 4.8 %all-to-all-start.1 = ((bf16[4,2,128,1024]{3,2,1,0:T(8,128)(2,1)}), bf16[4,2,128,1024]{3,2,1,0:T(8,128)(2,1)S(1)}, u32[]{:S(2)}, u32[]{:S(2)}) async-start(bf16[4,2,128,1024]{3,2,1,0:T(8,128)(2,1)} %copy-done), calls=%async_computation.1 | async-start | bytes 4194304 | tf_op jit(solution)/shard_map/all_to_all | solution.py:420
  99.6 1.6 copy-done.2
  101.2 1.2 head_cot.1
  102.4 1.2 collective-permute-start.11
  103.6 11.5 %collective-permute-done.11.recv_ref = bf16[1024,256]{1,0:T(8,128)(2,1)S(1)} collective-permute-done((bf16[1024,256]{1,0:T(8,128)(2,1)S(1)}, bf16[1024,256]{1,0:T(8,128)(2,1)S(1)}, u32[]{:S(2)}, u32[]{:S(2)}) %collective-permute-start.11) | collective-permute-done | bytes 524320 | tf_op jit(solution)/shard_map/ppermute | solution.py:64
  115.1 6.9 %attention_backward.1 = bf16[8,3,128,256]{3,2,1,0:T(8,128)(2,1)S(1)} custom-call(bf16[8,3,128,256]{3,2,1,0:T(8,128)(2,1)S(1)} %copy-done.6, f32[2,16,1024]{2,1,0:T(8,128)S(1)} %reshape.88.bias_ref, f32[2,1,1024]{2,1,0:T(1,128)S(1)} %get-tuple-element.31.stat_ref, bf16[1024,256]{1,0:T(8,128)(2,1)S(1)} %copy-done.13, ...), custom_call_target="tpu_custom_call" | custom-call | flops 8589934592 | bytes 4194304 | tf_op jit(solution)/shard_map/attention_backward/pallas_call | solution.py:368
  122.0 1.2 copy-done.7
  123.1 1.8 all-to-all-done.1.in_ref
  124.9 4.3 %all-to-all-start.3 = ((bf16[8,3,128,256]{3,2,1,0:T(8,128)(2,1)}), bf16[8,3,128,256]{3,2,1,0:T(8,128)(2,1)}, u32[]{:S(2)}, u32[]{:S(2)}) async-start(bf16[8,3,128,256]{3,2,1,0:T(8,128)(2,1)} %copy-done.7), calls=%async_computation.3 | async-start | bytes 3145728 | tf_op jit(solution)/shard_map/all_to_all | solution.py:418
  129.2 1.6 copy-done.3
  130.8 1.9 %weight_grad.1 = (f32[8,64,512]{2,1,0:T(8,128)S(1)}, bf16[8,64,512]{2,1,0:T(8,128)(2,1)S(1)}) custom-call(s32[5]{0:T(128)S(1)} %stack.54.at_ref, bf16[4,2,128,1024]{3,2,1,0:T(8,128)(2,1)S(1)} %copy-done.3, bf16[1024,256]{1,0:T(8,128)(2,1)S(1)} %copy-done.14, bf16[1024,256]{1,0:T(8,128)(2,1)S(1)} %copy-done.16), custom_call_target="tpu_custom_call" | custom-call | flops 1073741824 | bytes 4718612 | tf_op jit(solution)/shard_map/weight_grad/pallas_call | solution.py:46
  132.9 1.9 %collective-permute-done.12.recv_ref = bf16[8,64,512]{2,1,0:T(8,128)(2,1)S(1)} collective-permute-done((bf16[8,64,512]{2,1,0:T(8,128)(2,1)S(1)}, bf16[8,64,512]{2,1,0:T(8,128)(2,1)S(1)}, u32[]{:S(2)}, u32[]{:S(2)}) %collective-permute-start.12) | collective-permute-done | bytes 524320 | tf_op jit(solution)/shard_map/ppermute | solution.py:64
  134.8 0.7 add_core.1
  135.4 1.0 collective-permute-start.13
  136.4 0.8 mixed_sum.1
  137.2 1.5 collective-permute-start.9
  138.7 15.2 %collective-permute-done.13.recv_ref = bf16[4,64,512]{2,1,0:T(8,128)(2,1)S(1)} collective-permute-done((bf16[4,64,512]{2,1,0:T(8,128)(2,1)S(1)}, bf16[4,64,512]{2,1,0:T(8,128)(2,1)S(1)}, u32[]{:S(2)}, u32[]{:S(2)}) %collective-permute-start.13) | collective-permute-done | bytes 262176 | tf_op jit(solution)/shard_map/ppermute | solution.py:64
  153.9 0.6 add_xh.1
  154.5 2.6 %collective-permute-start.14 = (bf16[64,512]{1,0:T(8,128)(2,1)S(1)}, bf16[64,512]{1,0:T(8,128)(2,1)S(1)}, u32[]{:S(2)}, u32[]{:S(2)}) collective-permute-start(bf16[64,512]{1,0:T(8,128)(2,1)S(1)} %get-tuple-element.44), channel_id=1, source_target_pairs={{0,32},{32,64},{64,96},{96,0},{1,33},{33,65},{65,97},{97,1},{2,34}... | collective-permute-start | bytes 196616 | tf_op jit(solution)/shard_map/ppermute | solution.py:268
  157.1 2.8 %collective-permute-start.15 = (bf16[64,512]{1,0:T(8,128)(2,1)S(1)}, bf16[64,512]{1,0:T(8,128)(2,1)S(1)}, u32[]{:S(2)}, u32[]{:S(2)}) collective-permute-start(bf16[64,512]{1,0:T(8,128)(2,1)S(1)} %get-tuple-element.45), channel_id=1, source_target_pairs={{0,64},{32,96},{64,0},{96,32},{1,65},{33,97},{65,1},{97,33},{2,66}... | collective-permute-start | bytes 196616 | tf_op jit(solution)/shard_map/ppermute | solution.py:268
  159.9 0.8 collective-permute-done.14.a_ref
  160.7 2.2 %collective-permute-done.15.b_ref = bf16[64,512]{1,0:T(8,128)(2,1)S(1)} collective-permute-done((bf16[64,512]{1,0:T(8,128)(2,1)S(1)}, bf16[64,512]{1,0:T(8,128)(2,1)S(1)}, u32[]{:S(2)}, u32[]{:S(2)}) %collective-permute-start.15) | collective-permute-done | bytes 65568 | tf_op jit(solution)/shard_map/ppermute | solution.py:268
  162.9 1.3 collective-permute-done.16.c_ref
  164.2 1.2 add_z.1
  165.4 2.0 %collective-permute-start.17 = (f32[16,512]{1,0:T(8,128)S(1)}, f32[16,512]{1,0:T(8,128)S(1)}, u32[]{:S(2)}, u32[]{:S(2)}) collective-permute-start(f32[16,512]{1,0:T(8,128)S(1)} %get-tuple-element.48), channel_id=1, source_target_pairs={{0,1},{1,2},{2,3},{3,0},{4,5},{5,6},{6,7},{7,4},{8,9},{9,10},{10,1... | collective-permute-start | bytes 98312 | tf_op jit(solution)/shard_map/ppermute | solution.py:279
  167.4 2.7 %collective-permute-start.18 = (f32[16,512]{1,0:T(8,128)S(1)}, f32[16,512]{1,0:T(8,128)S(1)}, u32[]{:S(2)}, u32[]{:S(2)}) collective-permute-start(f32[16,512]{1,0:T(8,128)S(1)} %get-tuple-element.49), channel_id=1, source_target_pairs={{0,2},{1,3},{2,0},{3,1},{4,6},{5,7},{6,4},{7,5},{8,10},{9,11},{10,... | collective-permute-start | bytes 98312 | tf_op jit(solution)/shard_map/ppermute | solution.py:279
  170.1 1.5 collective-permute-start.19
  171.6 1.3 collective-permute-done.18.refs_2_
  172.8 1.2 collective-permute-done.19.refs_3_
  174.0 1.2 place_rows.1
  175.2 2.6 %unpack_heads.1 = (bf16[128,2048]{1,0:T(8,128)(2,1)}, bf16[128,2048]{1,0:T(8,128)(2,1)}, bf16[128,2048]{1,0:T(8,128)(2,1)}) custom-call(bf16[8,3,128,256]{3,2,1,0:T(8,128)(2,1)} %all-to-all-done.3.in_ref), custom_call_target="tpu_custom_call" | custom-call | bytes 3145728 | tf_op jit(solution)/shard_map/unpack_heads/pallas_call | solution.py:46
  177.8 1.6 mixed_join.1
  (57 shorter events, 0.7 us)
Async XLA Ops:
  0.6 1.0 copy-start.9
  1.7 1.0 copy-start.10
  2.7 1.0 copy-start.11
  5.0 5.7 %copy-start.8 = (bf16[1,128,2048]{2,1,0:T(8,128)(2,1)S(1)}, bf16[1,128,2048]{2,1,0:T(8,128)(2,1)}, u32[]{:S(2)}) copy-start(bf16[1,128,2048]{2,1,0:T(8,128)(2,1)} %param.11) | copy-start | bytes 1572868
  5.0 8.6 %copy-start.17 = (bf16[16,2048]{1,0:T(8,128)(2,1)S(1)}, bf16[16,2048]{1,0:T(8,128)(2,1)}, u32[]{:S(2)}) copy-start(bf16[16,2048]{1,0:T(8,128)(2,1)} %param.10) | copy-start | bytes 196612
  5.0 14.6 %copy-start.19 = (s32[1,2]{1,0:T(1,128)S(1)}, s32[1,2]{1,0:T(1,128)}, u32[]{:S(2)}) copy-start(s32[1,2]{1,0:T(1,128)} %param.13) | copy-start | bytes 28
  5.0 14.7 %copy-start.18 = (s32[1,2,16,3]{2,1,3,0:T(2,128)S(1)}, s32[1,2,16,3]{2,1,3,0:T(2,128)}, u32[]{:S(2)}) copy-start(s32[1,2,16,3]{2,1,3,0:T(2,128)} %param.12) | copy-start | bytes 1156
  5.1 32.6 %all-to-all-start = ((bf16[8,3,128,256]{3,2,1,0:T(8,128)(2,1)}), bf16[8,3,128,256]{3,2,1,0:T(8,128)(2,1)S(1)}, u32[]{:S(2)}, u32[]{:S(2)}) async-start(bf16[8,3,128,256]{3,2,1,0:T(8,128)(2,1)} %pack_heads.1), calls=%async_computation | async-start | bytes 3145728 | tf_op jit(solution)/shard_map/all_to_all | solution.py:408
  11.6 24.0 %collective-permute-start.10 = (bf16[128,1024]{1,0:T(8,128)(2,1)S(1)}, bf16[128,1024]{1,0:T(8,128)(2,1)S(1)}, u32[]{:S(2)}, u32[]{:S(2)}) collective-permute-start(bf16[128,1024]{1,0:T(8,128)(2,1)S(1)} %get-tuple-element.33), channel_id=1, source_target_pairs={{0,4},{4,0},{1,5},{5,1},{2,6},{6,2},{3,7},{7,3},{8,12},{12,8},{9,1... | collective-permute-start | bytes 786440 | tf_op jit(solution)/shard_map/ppermute | solution.py:64
  13.9 29.5 %collective-permute-start.1 = (bf16[16,512]{1,0:T(8,128)(2,1)S(1)}, bf16[16,512]{1,0:T(8,128)(2,1)S(1)}, u32[]{:S(2)}, u32[]{:S(2)}) collective-permute-start(bf16[16,512]{1,0:T(8,128)(2,1)S(1)} %get-tuple-element.58), channel_id=1, source_target_pairs={{0,1},{1,2},{2,3},{3,0},{4,5},{5,6},{6,7},{7,4},{8,9},{9,10},{10,1... | collective-permute-start | bytes 49160 | tf_op jit(solution)/shard_map/ppermute | solution.py:126
  15.5 28.0 %collective-permute-start.2 = (bf16[16,512]{1,0:T(8,128)(2,1)S(1)}, bf16[16,512]{1,0:T(8,128)(2,1)S(1)}, u32[]{:S(2)}, u32[]{:S(2)}) collective-permute-start(bf16[16,512]{1,0:T(8,128)(2,1)S(1)} %get-tuple-element.57), channel_id=1, source_target_pairs={{0,2},{1,3},{2,0},{3,1},{4,6},{5,7},{6,4},{7,5},{8,10},{9,11},{10,... | collective-permute-start | bytes 49160 | tf_op jit(solution)/shard_map/ppermute | solution.py:126
  18.1 25.3 %collective-permute-start.3 = (bf16[16,512]{1,0:T(8,128)(2,1)S(1)}, bf16[16,512]{1,0:T(8,128)(2,1)S(1)}, u32[]{:S(2)}, u32[]{:S(2)}) collective-permute-start(bf16[16,512]{1,0:T(8,128)(2,1)S(1)} %get-tuple-element.56), channel_id=1, source_target_pairs={{0,3},{1,0},{2,1},{3,2},{4,7},{5,4},{6,5},{7,6},{8,11},{9,8},{10,9... | collective-permute-start | bytes 49160 | tf_op jit(solution)/shard_map/ppermute | solution.py:126
  37.7 1.2 copy-start.4
  38.9 54.6 %all-to-all-start.2 = ((bf16[4,2,128,1024]{3,2,1,0:T(8,128)(2,1)}), bf16[4,2,128,1024]{3,2,1,0:T(8,128)(2,1)S(1)}, u32[]{:S(2)}, u32[]{:S(2)}) async-start(bf16[4,2,128,1024]{3,2,1,0:T(8,128)(2,1)} %cot_copies.1), calls=%async_computation.2 | async-start | bytes 4194304 | tf_op jit(solution)/shard_map/all_to_all | solution.py:410
  43.5 9.3 %collective-permute-start.4 = (bf16[4,16,512]{2,1,0:T(8,128)(2,1)S(1)}, bf16[4,16,512]{2,1,0:T(8,128)(2,1)S(1)}, u32[]{:S(2)}, u32[]{:S(2)}) collective-permute-start(bf16[4,16,512]{2,1,0:T(8,128)(2,1)S(1)} %get-tuple-element.54), channel_id=1, source_target_pairs={{0,8},{8,0},{1,9},{9,1},{2,10},{10,2},{3,11},{11,3},{4,12},{12,4},... | collective-permute-start | bytes 196616 | tf_op jit(solution)/shard_map/ppermute | solution.py:64
  43.6 1.4 copy-start.5
  52.2 36.3 %copy-start.12 = (bf16[1024,256]{1,0:T(8,128)(2,1)}, bf16[1024,256]{1,0:T(8,128)(2,1)S(1)}, u32[]{:S(2)}) copy-start(bf16[1024,256]{1,0:T(8,128)(2,1)S(1)} %get-tuple-element.28.own_ref.o_ref) | copy-start | bytes 1572868
  52.2 36.3 %collective-permute-start = (bf16[1024,256]{1,0:T(8,128)(2,1)S(1)}, bf16[1024,256]{1,0:T(8,128)(2,1)S(1)}, u32[]{:S(2)}, u32[]{:S(2)}) collective-permute-start(bf16[1024,256]{1,0:T(8,128)(2,1)S(1)} %get-tuple-element.28.own_ref.o_ref), channel_id=1, source_target_pairs={{0,4},{4,0},{1,5},{5,1},{2,6},{6,2},{3,7},{7,3},{8,12},{12,8},{9,1... | collective-permute-start | bytes 1572872 | tf_op jit(solution)/shard_map/ppermute | solution.py:64
  52.8 17.8 %collective-permute-start.5 = (bf16[2,4,16,512]{3,2,1,0:T(8,128)(2,1)S(1)}, bf16[2,4,16,512]{3,2,1,0:T(8,128)(2,1)S(1)}, u32[]{:S(2)}, u32[]{:S(2)}) collective-permute-start(bf16[2,4,16,512]{3,2,1,0:T(8,128)(2,1)S(1)} %get-tuple-element.52), channel_id=1, source_target_pairs={{0,16},{16,0},{1,17},{17,1},{2,18},{18,2},{3,19},{19,3},{4,20},{20... | collective-permute-start | bytes 393224 | tf_op jit(solution)/shard_map/ppermute | solution.py:64
  70.6 10.4 %collective-permute-start.6 = (bf16[2,2,4,16,512]{4,3,2,1,0:T(8,128)(2,1)S(1)}, bf16[2,2,4,16,512]{4,3,2,1,0:T(8,128)(2,1)S(1)}, u32[]{:S(2)}, u32[]{:S(2)}) collective-permute-start(bf16[2,2,4,16,512]{4,3,2,1,0:T(8,128)(2,1)S(1)} %pad_maximum_fusion.refs_0_), channel_id=1, source_target_pairs={{0,32},{32,64},{64,96},{96,0},{1,33},{33,65},{65,97},{97,1},{2,34}... | collective-permute-start | bytes 786440 | tf_op jit(solution)/shard_map/ppermute | solution.py:130
  72.6 15.1 %collective-permute-start.7 = (bf16[2,2,4,16,512]{4,3,2,1,0:T(8,128)(2,1)S(1)}, bf16[2,2,4,16,512]{4,3,2,1,0:T(8,128)(2,1)S(1)}, u32[]{:S(2)}, u32[]{:S(2)}) collective-permute-start(bf16[2,2,4,16,512]{4,3,2,1,0:T(8,128)(2,1)S(1)} %pad_maximum_fusion.refs_0_), channel_id=1, source_target_pairs={{0,64},{32,96},{64,0},{96,32},{1,65},{33,97},{65,1},{97,33},{2,66}... | collective-permute-start | bytes 786440 | tf_op jit(solution)/shard_map/ppermute | solution.py:130
  76.2 11.5 %collective-permute-start.8 = (bf16[2,2,4,16,512]{4,3,2,1,0:T(8,128)(2,1)S(1)}, bf16[2,2,4,16,512]{4,3,2,1,0:T(8,128)(2,1)S(1)}, u32[]{:S(2)}, u32[]{:S(2)}) collective-permute-start(bf16[2,2,4,16,512]{4,3,2,1,0:T(8,128)(2,1)S(1)} %pad_maximum_fusion.refs_0_), channel_id=1, source_target_pairs={{0,96},{32,0},{64,32},{96,64},{1,97},{33,1},{65,33},{97,65},{2,98}... | collective-permute-start | bytes 786440 | tf_op jit(solution)/shard_map/ppermute | solution.py:130
  91.3 1.3 copy-start
  92.6 0.8 copy-start.15
  93.4 1.4 copy-start.1
  94.8 30.1 %all-to-all-start.1 = ((bf16[4,2,128,1024]{3,2,1,0:T(8,128)(2,1)}), bf16[4,2,128,1024]{3,2,1,0:T(8,128)(2,1)S(1)}, u32[]{:S(2)}, u32[]{:S(2)}) async-start(bf16[4,2,128,1024]{3,2,1,0:T(8,128)(2,1)} %copy-done), calls=%async_computation.1 | async-start | bytes 4194304 | tf_op jit(solution)/shard_map/all_to_all | solution.py:420
  99.6 1.6 copy-start.2
  101.2 13.9 %copy-start.6 = (bf16[8,3,128,256]{3,2,1,0:T(8,128)(2,1)S(1)}, bf16[8,3,128,256]{3,2,1,0:T(8,128)(2,1)}, u32[]{:S(2)}) copy-start(bf16[8,3,128,256]{3,2,1,0:T(8,128)(2,1)} %copy-done.4) | copy-start | bytes 4718596
  101.2 13.9 %copy-start.13 = (bf16[1024,256]{1,0:T(8,128)(2,1)S(1)}, bf16[1024,256]{1,0:T(8,128)(2,1)}, u32[]{:S(2)}) copy-start(bf16[1024,256]{1,0:T(8,128)(2,1)} %copy-done.12) | copy-start | bytes 1572868
  102.4 12.6 %collective-permute-start.11 = (bf16[1024,256]{1,0:T(8,128)(2,1)S(1)}, bf16[1024,256]{1,0:T(8,128)(2,1)S(1)}, u32[]{:S(2)}, u32[]{:S(2)}) collective-permute-start(bf16[1024,256]{1,0:T(8,128)(2,1)S(1)} %get-tuple-element.35), channel_id=1, source_target_pairs={{0,4},{4,0},{1,5},{5,1},{2,6},{6,2},{3,7},{7,3},{8,12},{12,8},{9,1... | collective-permute-start | bytes 1572872 | tf_op jit(solution)/shard_map/ppermute | solution.py:64
  121.9 1.2 copy-start.7
  123.1 6.1 %copy-start.14 = (bf16[1024,256]{1,0:T(8,128)(2,1)S(1)}, bf16[1024,256]{1,0:T(8,128)(2,1)}, u32[]{:S(2)}) copy-start(bf16[1024,256]{1,0:T(8,128)(2,1)} %copy-done.12) | copy-start | bytes 1572868
  123.1 6.1 %copy-start.16 = (bf16[1024,256]{1,0:T(8,128)(2,1)S(1)}, bf16[1024,256]{1,0:T(8,128)(2,1)}, u32[]{:S(2)}) copy-start(bf16[1024,256]{1,0:T(8,128)(2,1)} %copy-done.15) | copy-start | bytes 1572868
  124.9 50.3 %all-to-all-start.3 = ((bf16[8,3,128,256]{3,2,1,0:T(8,128)(2,1)}), bf16[8,3,128,256]{3,2,1,0:T(8,128)(2,1)}, u32[]{:S(2)}, u32[]{:S(2)}) async-start(bf16[8,3,128,256]{3,2,1,0:T(8,128)(2,1)} %copy-done.7), calls=%async_computation.3 | async-start | bytes 3145728 | tf_op jit(solution)/shard_map/all_to_all | solution.py:418
  129.2 1.6 copy-start.3
  132.8 2.0 %collective-permute-start.12 = (bf16[8,64,512]{2,1,0:T(8,128)(2,1)S(1)}, bf16[8,64,512]{2,1,0:T(8,128)(2,1)S(1)}, u32[]{:S(2)}, u32[]{:S(2)}) collective-permute-start(bf16[8,64,512]{2,1,0:T(8,128)(2,1)S(1)} %get-tuple-element.40), channel_id=1, source_target_pairs={{0,8},{8,0},{1,9},{9,1},{2,10},{10,2},{3,11},{11,3},{4,12},{12,4},... | collective-permute-start | bytes 1572872 | tf_op jit(solution)/shard_map/ppermute | solution.py:64
  135.4 18.5 %collective-permute-start.13 = (bf16[4,64,512]{2,1,0:T(8,128)(2,1)S(1)}, bf16[4,64,512]{2,1,0:T(8,128)(2,1)S(1)}, u32[]{:S(2)}, u32[]{:S(2)}) collective-permute-start(bf16[4,64,512]{2,1,0:T(8,128)(2,1)S(1)} %get-tuple-element.42), channel_id=1, source_target_pairs={{0,16},{16,0},{1,17},{17,1},{2,18},{18,2},{3,19},{19,3},{4,20},{20... | collective-permute-start | bytes 786440 | tf_op jit(solution)/shard_map/ppermute | solution.py:64
  137.2 40.6 %collective-permute-start.9 = (bf16[128,1024]{1,0:T(8,128)(2,1)S(1)}, bf16[128,1024]{1,0:T(8,128)(2,1)S(1)}, u32[]{:S(2)}, u32[]{:S(2)}) collective-permute-start(bf16[128,1024]{1,0:T(8,128)(2,1)S(1)} %get-tuple-element.30), channel_id=1, source_target_pairs={{0,4},{4,0},{1,5},{5,1},{2,6},{6,2},{3,7},{7,3},{8,12},{12,8},{9,1... | collective-permute-start | bytes 786440 | tf_op jit(solution)/shard_map/ppermute | solution.py:64
  154.5 6.1 %collective-permute-start.14 = (bf16[64,512]{1,0:T(8,128)(2,1)S(1)}, bf16[64,512]{1,0:T(8,128)(2,1)S(1)}, u32[]{:S(2)}, u32[]{:S(2)}) collective-permute-start(bf16[64,512]{1,0:T(8,128)(2,1)S(1)} %get-tuple-element.44), channel_id=1, source_target_pairs={{0,32},{32,64},{64,96},{96,0},{1,33},{33,65},{65,97},{97,1},{2,34}... | collective-permute-start | bytes 196616 | tf_op jit(solution)/shard_map/ppermute | solution.py:268
  157.1 5.8 %collective-permute-start.15 = (bf16[64,512]{1,0:T(8,128)(2,1)S(1)}, bf16[64,512]{1,0:T(8,128)(2,1)S(1)}, u32[]{:S(2)}, u32[]{:S(2)}) collective-permute-start(bf16[64,512]{1,0:T(8,128)(2,1)S(1)} %get-tuple-element.45), channel_id=1, source_target_pairs={{0,64},{32,96},{64,0},{96,32},{1,65},{33,97},{65,1},{97,33},{2,66}... | collective-permute-start | bytes 196616 | tf_op jit(solution)/shard_map/ppermute | solution.py:268
  159.9 4.3 %collective-permute-start.16 = (bf16[64,512]{1,0:T(8,128)(2,1)S(1)}, bf16[64,512]{1,0:T(8,128)(2,1)S(1)}, u32[]{:S(2)}, u32[]{:S(2)}) collective-permute-start(bf16[64,512]{1,0:T(8,128)(2,1)S(1)} %get-tuple-element.46), channel_id=1, source_target_pairs={{0,96},{32,0},{64,32},{96,64},{1,97},{33,1},{65,33},{97,65},{2,98}... | collective-permute-start | bytes 196616 | tf_op jit(solution)/shard_map/ppermute | solution.py:268
  165.4 6.2 %collective-permute-start.17 = (f32[16,512]{1,0:T(8,128)S(1)}, f32[16,512]{1,0:T(8,128)S(1)}, u32[]{:S(2)}, u32[]{:S(2)}) collective-permute-start(f32[16,512]{1,0:T(8,128)S(1)} %get-tuple-element.48), channel_id=1, source_target_pairs={{0,1},{1,2},{2,3},{3,0},{4,5},{5,6},{6,7},{7,4},{8,9},{9,10},{10,1... | collective-permute-start | bytes 98312 | tf_op jit(solution)/shard_map/ppermute | solution.py:279
  167.4 5.4 %collective-permute-start.18 = (f32[16,512]{1,0:T(8,128)S(1)}, f32[16,512]{1,0:T(8,128)S(1)}, u32[]{:S(2)}, u32[]{:S(2)}) collective-permute-start(f32[16,512]{1,0:T(8,128)S(1)} %get-tuple-element.49), channel_id=1, source_target_pairs={{0,2},{1,3},{2,0},{3,1},{4,6},{5,7},{6,4},{7,5},{8,10},{9,11},{10,... | collective-permute-start | bytes 98312 | tf_op jit(solution)/shard_map/ppermute | solution.py:279
  170.1 3.9 %collective-permute-start.19 = (f32[16,512]{1,0:T(8,128)S(1)}, f32[16,512]{1,0:T(8,128)S(1)}, u32[]{:S(2)}, u32[]{:S(2)}) collective-permute-start(f32[16,512]{1,0:T(8,128)S(1)} %get-tuple-element.50), channel_id=1, source_target_pairs={{0,3},{1,0},{2,1},{3,2},{4,7},{5,4},{6,5},{7,6},{8,11},{9,8},{10,9... | collective-permute-start | bytes 98312 | tf_op jit(solution)/shard_map/ppermute | solution.py:279

commit v3 on v1

v3 whole, which is shorter than its diff:
```python
import functools
import math

import jax
import jax.numpy as jnp
from jax import lax
from jax.experimental import pallas as pl
from jax.experimental.pallas import tpu as pltpu
from jax.sharding import Mesh
from jax.sharding import PartitionSpec as P

HS = 128
BLK = 64
NB = 16
LEN = 1024
HD = 2048
SCALE = 1.0 / math.sqrt(HS)
LOG2E = math.log2(math.e)
QKV = 384
ROWS = 416
MASKED = -1e30
CTX = ("xl", "y")
DP = ("z", "xh", "core")
BF = jnp.bfloat16
F32 = jnp.float32
NT = (((1,), (1,)), ((), ()))
NN = (((1,), (0,)), ((), ()))
TN = (((0,), (0,)), ((), ()))


def dot(a, b, dims=NN):
    return lax.dot_general(a, b, dims, preferred_element_type=F32)


def params(mib=48):
    return pltpu.CompilerParams(vmem_limit_bytes=mib * 2**20)


VMEM = pl.BlockSpec(memory_space=pltpu.VMEM)
SMEM = pl.BlockSpec(memory_space=pltpu.SMEM)


HBM = pl.BlockSpec(memory_space=pl.ANY)


def whole(body, name, outs, *args, scalars=0, scratch=(), flops=0, after=()):
    read = len(args)

    def ordered(*refs):
        body(*refs[:read], *refs[read + len(after) :])

    one = isinstance(outs[0][0], int)
    made = [jax.ShapeDtypeStruct(*o) for o in ([outs] if one else outs)]
    moved = sum(math.prod(x.shape) * x.dtype.itemsize for x in args)
    moved += sum(math.prod(x.shape) * x.dtype.itemsize for x in made)
    given = pl.pallas_call(
        ordered,
        in_specs=[SMEM] * scalars + [VMEM] * (len(args) - scalars) + [HBM] * len(after),
        out_specs=[VMEM] * len(made),
        out_shape=made,
        scratch_shapes=list(scratch),
        compiler_params=params(),
        cost_estimate=pl.CostEstimate(flops=1, bytes_accessed=1, transcendentals=0),
        name=name,
    )(*args, *after)
    return given[0] if one else given


def hold(array, after):
    return pl.pallas_call(
        lambda *refs: None,
        in_specs=[HBM] * (1 + len(after)),
        out_specs=HBM,
        out_shape=jax.ShapeDtypeStruct(array.shape, array.dtype),
        input_output_aliases={0: 0},
        cost_estimate=pl.CostEstimate(flops=1, bytes_accessed=1, transcendentals=0),
        name="hold",
    )(array, *after)


def ring(size, step):
    return [(i, (i + step) % size) for i in range(size)]


def swap(array, axis="xl"):
    return lax.ppermute(array, axis, ring(2, 1))


def pack_kernel(q_ref, k_ref, v_ref, out_ref, held_ref, sems):
    copies = []
    for j, ref in enumerate((q_ref, k_ref, v_ref)):
        for half in range(2):
            rows = pl.ds(64 * half, 64)
            copy = pltpu.make_async_copy(ref.at[rows, :], held_ref.at[j, rows, :], sems.at[j, half])
            copy.start()
            copies.append(copy)
    for j in range(3):
        for half in range(2):
            copies[2 * j + half].wait()
            rows = slice(128 * j + 64 * half, 128 * j + 64 * half + 64)
            for c in range(8):
                out_ref[c, rows] = held_ref[j, 64 * half : 64 * half + 64, 256 * c : 256 * c + 256]


def pack_heads(q, k, v):
    return pl.pallas_call(
        pack_kernel,
        in_specs=[pl.BlockSpec(memory_space=pltpu.HBM)] * 3,
        out_specs=VMEM,
        out_shape=jax.ShapeDtypeStruct((8, QKV, 256), BF),
        scratch_shapes=[pltpu.VMEM((3, 128, HD), BF), pltpu.SemaphoreType.DMA((3, 2))],
        compiler_params=params(63),
        cost_estimate=pl.CostEstimate(flops=1, bytes_accessed=1, transcendentals=0),
        name="pack_heads",
    )(q, k, v)


def blocks_kernel(own_ref, out_ref):
    for xh in range(2):
        for xl in range(2):
            for y in range(4):
                for k, side in enumerate((xl, 1 - xl)):
                    cols = slice(1024 * side + 256 * y, 1024 * side + 256 * y + 256)
                    out_ref[8 * xh + 4 * xl + y, :, 256 * k : 256 * k + 256] = own_ref[:, cols]


def near_kernel(at_ref, *refs):
    out_ref = refs[-1]
    for step in range(4):
        out_ref[lax.rem(at_ref[0] - step + 4, 4)] = refs[step][...]


def weight_kernel(at_ref, own_ref, other_ref, out_ref):
    core = at_ref[2]
    for z in range(4):
        for h in range(2):
            out_ref[4 * z + 2 * h + core] = own_ref[z, h]
            out_ref[4 * z + 2 * h + 1 - core] = other_ref[z, h]


def gather_weight(at, own):
    blocks = whole(blocks_kernel, "weight_blocks", ((16, 16, 512), BF), own)
    rows = lax.all_to_all(blocks, ("xh",) + CTX, 0, 0, tiled=True).reshape(2, 128, 512)
    far = [lax.ppermute(rows, "z", ring(4, step)) for step in (1, 2, 3)]
    near = whole(near_kernel, "place_z", ((4, 2, 128, 512), BF), at, rows, *far, scalars=1)
    full = whole(weight_kernel, "place_core", ((16, 128, 512), BF), at, near, swap(near, "core"), scalars=1)
    return full.reshape(HD, 512), rows


def gather_cot(own):
    back = lax.ppermute(own, "y", ring(4, 1))
    on = lax.ppermute(own, "y", ring(4, 3))
    return own, back, on, lax.ppermute(back[:64], "y", ring(4, 1)), lax.ppermute(on[64:], "y", ring(4, 3))


def place_cot(y, full_ref, own_ref, back_ref, on_ref, far_0_ref, far_1_ref):
    full_ref[y] = own_ref[...]
    full_ref[lax.rem(y + 3, 4)] = back_ref[...]
    full_ref[lax.rem(y + 1, 4)] = on_ref[...]
    full_ref[lax.rem(y + 2, 4), :64] = far_0_ref[...]
    full_ref[lax.rem(y + 2, 4), 64:] = far_1_ref[...]


def head_cot_kernel(at_ref, *refs):
    cot_refs, (w_ref, keep_ref, send_ref, full_ref) = refs[:5], refs[5:]
    place_cot(at_ref[4], full_ref, *cot_refs)
    for t in range(2):
        rows = slice(256 * t, 256 * t + 256)
        both = dot(full_ref[2 * t : 2 * t + 2].reshape(256, HD), w_ref[...]).astype(BF)
        keep_ref[rows, :] = both[:, :256]
        send_ref[rows, :] = both[:, 256:]


def head_cot_parts(at, cot, weight):
    half = ((512, 256), BF)
    full = pltpu.VMEM((4, 128, HD), BF)
    return whole(head_cot_kernel, "head_cot", (half, half), at, *cot, weight, scalars=1, scratch=(full,))


def mixed_part_kernel(at_ref, own_ref, other_ref, w_ref, out_ref):
    for y in range(4):
        own = own_ref[pl.ds(pl.multiple_of(512 * at_ref[3] + 128 * y, 128), 128), :]
        other = other_ref[128 * y : 128 * y + 128, :]
        for n in range(4):
            outs = slice(512 * n, 512 * n + 512)
            part = dot(own, w_ref[outs, :256], NT) + dot(other, w_ref[outs, 256:], NT)
            out_ref[y, :, outs] = part.astype(BF)


def mixed_parts(at, own, other, weight):
    return whole(mixed_part_kernel, "mixed_part", ((4, 128, HD), BF), at, own, other, weight, scalars=1)


def mixed_kernel(in_ref, out_ref):
    out_ref[...] = sum(in_ref[y].astype(F32) for y in range(4)).astype(BF)


def finish_mixed(parts):
    return whole(mixed_kernel, "finish_mixed", ((128, HD), BF), parts)


def weight_grad_kernel(at_ref, *refs):
    cot_refs, (own_ref, other_ref, keep_ref, send_ref, full_ref, pair_ref, sum_ref) = refs[:5], refs[5:]
    core, xl = at_ref[2], at_ref[3]
    place_cot(at_ref[4], full_ref, *cot_refs)
    pair_ref[:, :256] = own_ref[pl.ds(pl.multiple_of(512 * xl, 512), 512), :]
    pair_ref[:, 256:] = other_ref[...]
    for z in range(4):
        cot = full_ref[:, :, 512 * z : 512 * z + 512].reshape(512, 512)
        sum_ref[...] = dot(cot, pair_ref[...], TN).reshape(4, 128, 512)
        for h in range(2):
            keep_ref[z, h] = sum_ref[2 * h + core]
            send_ref[z, h] = sum_ref[2 * h + 1 - core].astype(BF)


def add_core_kernel(at_ref, keep_ref, recv_ref, out_ref, *send_refs):
    z = at_ref[0]
    out_ref[...] = keep_ref[z] + recv_ref[z].astype(F32)
    for step, ref in enumerate(send_refs, 1):
        to = lax.rem(z + step, 4)
        ref[...] = (keep_ref[to] + recv_ref[to].astype(F32)).astype(BF)


def add_z_kernel(at_ref, own_ref, a_ref, b_ref, c_ref, out_ref, send_ref):
    xh = at_ref[1]

    def total(h):
        return own_ref[h] + a_ref[h].astype(F32) + b_ref[h].astype(F32) + c_ref[h].astype(F32)

    out_ref[...] = total(xh)
    send_ref[...] = total(1 - xh).astype(BF)


def attach_kernel(scale, keep_ref, recv_ref, grads_ref, out_ref):
    total = ((keep_ref[...] + recv_ref[...].astype(F32)) * scale).astype(BF)
    for c in range(8):
        rows = slice(16 * c, 16 * c + 16)
        out_ref[c, :QKV] = grads_ref[c]
        out_ref[c, QKV : QKV + 16] = total[rows, :256]
        out_ref[c, QKV + 16 :] = total[rows, 256:]


def attach(keep, recv, grads, scale):
    body = functools.partial(attach_kernel, scale)
    return whole(body, "attach", ((8, ROWS, 256), BF), keep, recv, grads)


def weight_grad(at, cot, own, other, after):
    shape = (4, 2, 128, 512)
    keep, send = whole(
        weight_grad_kernel,
        "weight_grad",
        ((shape, F32), (shape, BF)),
        at,
        *cot,
        own,
        other,
        scalars=1,
        after=after,
        scratch=(pltpu.VMEM((4, 128, HD), BF), pltpu.VMEM((512, 512), BF), pltpu.VMEM((4, 128, 512), F32)),
    )
    two, one = ((2, 128, 512), BF), ((128, 512), BF)
    keep, *sends = whole(
        add_core_kernel, "add_core", ((two[0], F32), two, two, two), at, keep, swap(send, "core"), scalars=1
    )
    started = sends[-1]
    got = [lax.ppermute(send, "z", ring(4, step)) for step, send in enumerate(sends, 1)]
    keep, send = whole(add_z_kernel, "add_z", ((one[0], F32), one), at, keep, *got, scalars=1)
    return started, keep, swap(send, "xh")


def live_bias(rand, glob):
    kb = jnp.arange(NB, dtype=jnp.int32)[:, None]
    qb = jnp.arange(NB, dtype=jnp.int32)[None, :]
    live = (jnp.abs(kb - qb) <= 1) | jnp.any(kb[:, :, None] == glob[None, None, :], axis=-1)
    by_rand = jnp.any(rand.transpose(0, 2, 1)[:, :, None, :] == kb[None, None], axis=1)
    bias = jnp.where(live[None] | by_rand, 0.0, MASKED).astype(F32)
    return jnp.repeat(bias, BLK, axis=2)


TILE = 256


def scores_at(k, q, bias):
    s = dot(k, q, NT).reshape(NB, BLK, TILE)
    return s * (SCALE * LOG2E) + bias[:, None, :]


def forward_kernel(qkv_ref, bias_ref, o_ref, stat_ref):
    k = qkv_ref[:, 128:256].reshape(LEN, HS)
    v_t = qkv_ref[:, 256:384].reshape(LEN, HS).T
    for t in range(LEN // TILE):
        tok = slice(TILE * t, TILE * t + TILE)
        q = qkv_ref[2 * t : 2 * t + 2, :128].reshape(TILE, HS)
        s = scores_at(k, q, bias_ref[0, :, tok])
        top = jnp.max(s, axis=(0, 1), keepdims=True)
        p = jnp.exp2(s - top)
        total = jnp.sum(p, axis=(0, 1), keepdims=True)
        p_low = (p * (1.0 / total)).astype(BF).reshape(LEN, TILE)
        o_t = dot(v_t, p_low)
        o_ref[tok, :] = o_t.T.astype(BF)
        stat_ref[0, :, tok] = (top + jnp.log2(total))[0]


def forward(qkv, bias):
    return pl.pallas_call(
        forward_kernel,
        grid=(2,),
        in_specs=[
            pl.BlockSpec((8, QKV, HS), lambda h: (0, 0, h)),
            pl.BlockSpec((1, NB, LEN), lambda h: (h, 0, 0)),
        ],
        out_specs=[
            pl.BlockSpec((LEN, HS), lambda h: (0, h)),
            pl.BlockSpec((1, 1, LEN), lambda h: (h, 0, 0)),
        ],
        out_shape=[
            jax.ShapeDtypeStruct((LEN, 2 * HS), BF),
            jax.ShapeDtypeStruct((2, 1, LEN), F32),
        ],
        compiler_params=params(),
        cost_estimate=pl.CostEstimate(flops=1, bytes_accessed=1, transcendentals=0),
        name="attention_forward",
    )(qkv, bias)


def backward_kernel(at_ref, qkv_ref, bias_ref, stat_ref, o_ref, keep_ref, recv_ref, *refs):
    out_ref, dk_ref, dv_ref = refs[-3:]
    k = qkv_ref[:, 128:256].reshape(LEN, HS)
    v = qkv_ref[:, 256:384].reshape(LEN, HS)
    k_t = k.T
    for t in range(LEN // TILE):
        tok = slice(TILE * t, TILE * t + TILE)
        q = qkv_ref[2 * t : 2 * t + 2, :128].reshape(TILE, HS)
        half, part = divmod(TILE * t, 512)
        part = slice(part, part + TILE)
        do = jnp.where(at_ref[3] == half, keep_ref[part, :], recv_ref[part, :])
        delta = jnp.sum((do.astype(F32) * o_ref[tok, :].astype(F32)).T, axis=0, keepdims=True)
        p = jnp.exp2(scores_at(k, q, bias_ref[0, :, tok] - stat_ref[0, :, tok]))
        p = p.reshape(LEN, TILE)
        dp = dot(v, do, NT)
        ds = (p * (dp - delta)).astype(BF)
        dq = dot(k_t, ds).T * SCALE
        out_ref[2 * t : 2 * t + 2, :128] = dq.astype(BF).reshape(2, 128, HS)
        dk = dot(ds, q)
        dv = dot(p.astype(BF), do)
        if t == 0:
            dk_ref[...] = dk
            dv_ref[...] = dv
        else:
            dk_ref[...] += dk
            dv_ref[...] += dv
    out_ref[:, 128:256] = (dk_ref[...] * SCALE).astype(BF).reshape(8, 128, HS)
    out_ref[:, 256:384] = dv_ref[...].astype(BF).reshape(8, 128, HS)


def backward(at, qkv, bias, stat, attended, keep, recv, after):
    wide = pl.BlockSpec((LEN, HS), lambda h: (0, h))
    half = pl.BlockSpec((512, HS), lambda h: (0, h))
    heads = pl.BlockSpec((8, QKV, HS), lambda h: (0, 0, h))
    return pl.pallas_call(
        backward_kernel,
        grid=(2,),
        in_specs=[
            SMEM,
            heads,
            pl.BlockSpec((1, NB, LEN), lambda h: (h, 0, 0)),
            pl.BlockSpec((1, 1, LEN), lambda h: (h, 0, 0)),
            wide,
            half,
            half,
            *[HBM] * len(after),
        ],
        out_specs=heads,
        out_shape=jax.ShapeDtypeStruct((8, QKV, 2 * HS), BF),
        scratch_shapes=[pltpu.VMEM((LEN, HS), F32), pltpu.VMEM((LEN, HS), F32)],
        compiler_params=params(),
        cost_estimate=pl.CostEstimate(flops=1, bytes_accessed=1, transcendentals=0),
        name="attention_backward",
    )(at, qkv, bias, stat, attended, keep, recv, *after)


def unpack_kernel(in_ref, q_ref, k_ref, v_ref, rows_ref):
    for c in range(8):
        cols = slice(256 * c, 256 * c + 256)
        for j, ref in enumerate((q_ref, k_ref, v_ref)):
            ref[:, cols] = in_ref[c, 128 * j : 128 * j + 128]
    for side in range(2):
        for y in range(4):
            first = in_ref[4 * side + y, QKV : QKV + 16].astype(F32)
            second = in_ref[4 * (1 - side) + y, QKV + 16 :].astype(F32)
            rows_ref[:, 1024 * side + 256 * y : 1024 * side + 256 * y + 256] = first + second


def unpack_heads(grads):
    out = ((128, HD), BF)
    return whole(unpack_kernel, "unpack_heads", (out, out, out, ((16, HD), F32)), grads)


def on_device(queries, keys, values, out_weight, cotangent, rand_blocks, glob_blocks):
    at = jnp.stack([lax.axis_index(name) for name in DP + CTX]).astype(jnp.int32)
    xl = at[3]
    cot = gather_cot(cotangent[0])
    weight, early = gather_weight(at, out_weight)
    qkv = hold(pack_heads(queries[0], keys[0], values[0]), (early,))
    qkv = lax.all_to_all(qkv, CTX, 0, 0, tiled=True)

    bias = live_bias(rand_blocks[0], glob_blocks[0])
    attended, stat = forward(qkv, bias)
    other = swap(lax.dynamic_slice(attended, (512 * (1 - xl), 0), (512, 256)))
    keep, send = head_cot_parts(at, cot, weight)
    part = mixed_parts(at, attended, other, weight)
    started, rows, rows_recv = weight_grad(at, cot, attended, other, (part,))
    part = lax.all_to_all(part, "y", 0, 0, tiled=True)
    grads = backward(at, qkv, bias, stat, attended, keep, swap(send), (started,))
    total_tokens = lax.axis_size(DP) * lax.axis_size(CTX) * cotangent.shape[1]
    grads = attach(rows, rows_recv, grads, 1.0 / math.sqrt(total_tokens))
    grads = lax.all_to_all(grads, CTX, 0, 0, tiled=True)

    mixed = finish_mixed(part)
    grad_q, grad_k, grad_v, grad_w = unpack_heads(grads)
    return (mixed[None], grad_q[None], grad_k[None], grad_v[None], grad_w)


def solution(mesh):
    fine = Mesh(mesh.devices.reshape(4, 2, 2, 2, 4), ("z", "xh", "core", "xl", "y"))
    tokens = P(DP, CTX, None)
    return jax.shard_map(
        on_device,
        mesh=fine,
        in_specs=(tokens, tokens, tokens, P(DP + CTX, None), tokens, P(DP, CTX, None, None), P(DP, None)),
        out_specs=(tokens, tokens, tokens, tokens, P(DP + CTX, None)),
        check_vma=False,
    )
```

time: 199 us -> 132 us (0.66)
  waiting for transfers between devices: 86.8 us -> 44 us
  matrix products: 13.7 us -> 0 us
  Pallas kernels: 28.6 us -> 38 us
  between operations: 8.66 us -> 0.87 us
  local copies, waits for them, and re-layouts: 11.8 us -> 6.21 us
  starting transfers between devices: 45.3 us -> 41.2 us
  other arithmetic: 2.45 us -> 0.19 us
    all_to_all x6 -> x3, waiting for transfers between devices: 47.5 us -> 5.92 us  [the longest x1 5.91 us: gather_weight(): lax.all_to_all(blocks, ('xh',) + CTX, 0, 0, tiled=True).reshape(2, 128, 512)]
    dot_general x4 -> x0, matrix products: 13.7 us -> none  [dot(): return lax.dot_general(a, b, dims, preferred_element_type=F32)]
    all_to_all x6 -> x3, starting transfers between devices: 27.9 us -> 15.3 us  [the longest x1 7.12 us: gather_weight(): lax.all_to_all(blocks, ('xh',) + CTX, 0, 0, tiled=True).reshape(2, 128, 512)]
    pallas_call x6 -> x15, Pallas kernels: 28.6 us -> 38 us  [the longest x11 21.2 us: whole(): pl.pallas_call(ordered, in_specs=[SMEM] * scalars + [VMEM] * (len(args) -...]
    ppermute x7 -> x15, starting transfers between devices: 12 us -> 20.8 us  [the longest x3 5.37 us: gather_weight(): far = [lax.ppermute(rows, 'z', ring(4, step)) for step in (1, 2, 3)]]
    ppermute x7 -> x15, waiting for transfers between devices: 23 us -> 19.7 us  [the longest x3 8.89 us: gather_weight(): far = [lax.ppermute(rows, 'z', ring(4, step)) for step in (1, 2, 3)]]
    reshape x5 -> x0, local copies, waits for them, and re-layouts: 2.37 us -> none  [the longest x1 0.85 us: on_device(): sides = out_weight.reshape(16, 2, 1024)]
    convert_element_type x1 -> x0, local copies, waits for them, and re-layouts: 2.27 us -> none  [on_device(): block = dot(cot, pair, TN).astype(BF).reshape(16, 64, 512)]
  transfers between devices with their start and end apart: 14 -> 19, of which waited for: 9 -> 10; matrix products, arithmetic and copies ran while one was open for 12% -> 2% of each run, Pallas kernels for 14% -> 28%
where the time goes in v3:
time: 132 us; the launch traced here: 130 us
  waiting for transfers between devices  44 us (33%)
  starting transfers between devices  41.2 us (31%)
  Pallas kernels  38 us (29%)
  local copies, waits for them, and re-layouts  6.21 us (5%)
    pallas_call x11, Pallas kernels, whole(): pl.pallas_call(ordered, in_specs=[SMEM] * scalars + [VMEM] * (len(args) -...  21.2 us
    all_to_all x1, waiting for transfers between devices, on_device(): grads = lax.all_to_all(grads, CTX, 0, 0, tiled=True)  18.4 us
    ppermute x3, waiting for transfers between devices, gather_weight(): far = [lax.ppermute(rows, 'z', ring(4, step)) for step in (1, 2, 3)]  8.89 us
    pallas_call x1, Pallas kernels, forward(): pl.pallas_call(forward_kernel, grid=(2,), in_specs=[pl.BlockSpec((8, QKV,...  7.16 us
    all_to_all x1, starting transfers between devices, gather_weight(): lax.all_to_all(blocks, ('xh',) + CTX, 0, 0, tiled=True).reshape(2, 128, 512)  7.12 us
    pallas_call x1, Pallas kernels, backward(): pl.pallas_call(backward_kernel, grid=(2,), in_specs=[SMEM, heads, pl.Bloc...  7.09 us
    ppermute x3, waiting for transfers between devices, weight_grad(): lax.ppermute(send, 'z', ring(4, step))  6.74 us
    all_to_all x1, waiting for transfers between devices, gather_weight(): lax.all_to_all(blocks, ('xh',) + CTX, 0, 0, tiled=True).reshape(2, 128, 512)  5.91 us
  transfers between devices with their start and end apart: 19, of which 10 were waited for; matrix products, arithmetic and copies ran while one was open for 2% of the time, Pallas kernels for 28%

profile of v3, /device:TPU:0, one launch (start us, length us, event | category | flops | bytes accessed | tf_op | source)
XLA Modules:
  0.0 130.5 jit_solution(10080807616835217651)
XLA Ops:
  0.6 0.8 copy-done.9
  1.5 0.7 weight_blocks.1
  2.2 7.1 %all-to-all-start = ((bf16[16,16,512]{2,1,0:T(8,128)(2,1)}), bf16[16,16,512]{2,1,0:T(8,128)(2,1)S(1)}, u32[]{:S(2)}, u32[]{:S(2)}) async-start(bf16[16,16,512]{2,1,0:T(8,128)(2,1)} %weight_blocks.1), calls=%async_computation | async-start | bytes 524288 | tf_op jit(solution)/shard_map/all_to_all | solution.py:143
  9.3 2.6 %pack_heads.1.refs_0_ = bf16[8,384,256]{2,1,0:T(8,128)(2,1)} custom-call(bf16[128,2048]{1,0:T(8,128)(2,1)} %bitcast.29, bf16[128,2048]{1,0:T(8,128)(2,1)} %bitcast.30, bf16[128,2048]{1,0:T(8,128)(2,1)} %bitcast.31), custom_call_target="tpu_custom_call" | custom-call | flops 1 | bytes 1 | tf_op jit(solution)/shard_map/pack_heads/pallas_call | solution.py:106
  11.9 5.9 %all-to-all-done = bf16[16,16,512]{2,1,0:T(8,128)(2,1)S(1)} async-done(((bf16[16,16,512]{2,1,0:T(8,128)(2,1)}), bf16[16,16,512]{2,1,0:T(8,128)(2,1)S(1)}, u32[]{:S(2)}, u32[]{:S(2)}) %all-to-all-start) | async-done | bytes 262176 | tf_op jit(solution)/shard_map/all_to_all | solution.py:143
  17.8 0.7 copy-done.5
  18.5 3.7 %all-to-all-start.1 = ((bf16[8,384,256]{2,1,0:T(8,128)(2,1)}), bf16[8,384,256]{2,1,0:T(8,128)(2,1)S(1)}, u32[]{:S(2)}, u32[]{:S(2)}) async-start(bf16[8,384,256]{2,1,0:T(8,128)(2,1)} %hold.1), calls=%async_computation.1 | async-start | bytes 3145728 | tf_op jit(solution)/shard_map/all_to_all | solution.py:406
  22.3 0.0 copy-start.11
  22.3 4.1 %collective-permute-start.3 = (bf16[2,128,512]{2,1,0:T(8,128)(2,1)S(1)}, bf16[2,128,512]{2,1,0:T(8,128)(2,1)S(1)}, u32[]{:S(2)}, u32[]{:S(2)}) collective-permute-start(bf16[2,128,512]{2,1,0:T(8,128)(2,1)S(1)} %bitcast.24), channel_id=1, source_target_pairs={{0,96},{32,0},{64,32},{96,64},{1,97},{33,1},{65,33},{97,65},{2,98}... | collective-permute-start | bytes 786440 | tf_op jit(solution)/shard_map/ppermute | solution.py:144
  26.4 0.0 collective-permute-start.2
  26.4 1.3 collective-permute-start.1
  27.6 3.1 %collective-permute-start.6 = (bf16[128,2048]{1,0:T(8,128)(2,1)}, bf16[128,2048]{1,0:T(8,128)(2,1)S(1)}, u32[]{:S(2)}, u32[]{:S(2)}) collective-permute-start(bf16[128,2048]{1,0:T(8,128)(2,1)} %bitcast.14.refs_1_), channel_id=1, source_target_pairs={{0,3},{1,0},{2,1},{3,2},{4,7},{5,4},{6,5},{7,6},{8,11},{9,8},{10,9... | collective-permute-start | bytes 1572872 | tf_op jit(solution)/shard_map/ppermute | solution.py:152
  30.8 0.0 collective-permute-start.5
  30.8 0.1 stack.23.refs_0_.at_ref
  30.9 5.4 %collective-permute-done.3.refs_4_ = bf16[2,128,512]{2,1,0:T(8,128)(2,1)S(1)} collective-permute-done((bf16[2,128,512]{2,1,0:T(8,128)(2,1)S(1)}, bf16[2,128,512]{2,1,0:T(8,128)(2,1)S(1)}, u32[]{:S(2)}, u32[]{:S(2)}) %collective-permute-start.3) | collective-permute-done | bytes 262176 | tf_op jit(solution)/shard_map/ppermute | solution.py:144
  36.2 0.9 collective-permute-done.2.refs_3_
  37.1 2.6 %collective-permute-done.1.refs_2_ = bf16[2,128,512]{2,1,0:T(8,128)(2,1)} collective-permute-done((bf16[2,128,512]{2,1,0:T(8,128)(2,1)S(1)}, bf16[2,128,512]{2,1,0:T(8,128)(2,1)}, u32[]{:S(2)}, u32[]{:S(2)}) %collective-permute-start.1) | collective-permute-done | bytes 262176 | tf_op jit(solution)/shard_map/ppermute | solution.py:144
  39.8 2.0 %place_z.1.refs_1_ = bf16[4,2,128,512]{3,2,1,0:T(8,128)(2,1)} custom-call(s32[5]{0:T(128)S(1)} %stack.23.refs_0_.at_ref, bf16[2,128,512]{2,1,0:T(8,128)(2,1)S(1)} %bitcast.27, bf16[2,128,512]{2,1,0:T(8,128)(2,1)} %collective-permute-done.1.refs_2_, bf16[2,128,512]{2,1,0:T(8,128)(2,1)S(1)} %collective-permute-done.2.refs_3_, ...), custom_call_target="tpu_custom_call" | custom-call | flops 1 | bytes 1 | tf_op jit(solution)/shard_map/place_z/pallas_call | solution.py:56
  41.8 0.0 collective-permute-start.4
  41.8 0.1 compare_reduce_fusion
  41.9 0.1 fusion.1
  42.0 0.1 broadcast_in_dim.29
  42.1 0.1 reshape.86.bias_ref
  42.2 0.0 all-to-all-done.1.qkv_ref
  42.3 7.2 %attention_forward.1 = (bf16[1024,256]{1,0:T(8,128)(2,1)S(1)}, f32[2,1,1024]{2,1,0:T(1,128)S(1)}) custom-call(bf16[8,384,256]{2,1,0:T(8,128)(2,1)S(1)} %all-to-all-done.1.qkv_ref, f32[2,16,1024]{2,1,0:T(8,128)S(1)} %reshape.86.bias_ref), custom_call_target="tpu_custom_call" | custom-call | flops 1 | bytes 1 | tf_op jit(solution)/shard_map/attention_forward/pallas_call | solution.py:306
  49.5 1.7 %collective-permute-start = (bf16[512,256]{1,0:T(8,128)(2,1)S(1)}, bf16[512,256]{1,0:T(8,128)(2,1)S(1)}, u32[]{:S(2)}, u32[]{:S(2)}) collective-permute-start(bf16[512,256]{1,0:T(8,128)(2,1)S(1)} %constant_dynamic-slice_fusion), channel_id=1, source_target_pairs={{0,4},{4,0},{1,5},{5,1},{2,6},{6,2},{3,7},{7,3},{8,12},{12,8},{9,1... | collective-permute-start | bytes 786440 | tf_op jit(solution)/shard_map/ppermute | solution.py:86
  51.2 0.3 collective-permute-done.6.refs_3_
  51.5 0.7 slice.9
  52.3 2.4 %collective-permute-start.8 = (bf16[64,2048]{1,0:T(8,128)(2,1)}, bf16[64,2048]{1,0:T(8,128)(2,1)S(1)}, u32[]{:S(2)}, u32[]{:S(2)}) collective-permute-start(bf16[64,2048]{1,0:T(8,128)(2,1)} %slice.9), channel_id=1, source_target_pairs={{0,3},{1,0},{2,1},{3,2},{4,7},{5,4},{6,5},{7,6},{8,11},{9,8},{10,9... | collective-permute-start | bytes 786440 | tf_op jit(solution)/shard_map/ppermute | solution.py:153
  54.6 0.0 collective-permute-done.5.refs_2_
  54.6 0.8 slice.8
  55.4 0.1 copy-done.2
  55.5 1.7 %place_core.1 = bf16[16,128,512]{2,1,0:T(8,128)(2,1)S(1)} custom-call(s32[5]{0:T(128)S(1)} %stack.23.refs_0_.at_ref, bf16[4,2,128,512]{3,2,1,0:T(8,128)(2,1)} %place_z.1.refs_1_, bf16[4,2,128,512]{3,2,1,0:T(8,128)(2,1)} %collective-permute-done.4.refs_2_), custom_call_target="tpu_custom_call" | custom-call | flops 1 | bytes 1 | tf_op jit(solution)/shard_map/place_core/pallas_call | solution.py:56
  57.2 1.1 collective-permute-done.refs_2_.refs_7_
  58.3 4.7 %mixed_part.1.refs_8_ = bf16[4,128,2048]{2,1,0:T(8,128)(2,1)} custom-call(s32[5]{0:T(128)S(1)} %stack.23.refs_0_.at_ref, bf16[1024,256]{1,0:T(8,128)(2,1)S(1)} %get-tuple-element.21.refs_1_.refs_6_.o_ref, bf16[512,256]{1,0:T(8,128)(2,1)S(1)} %collective-permute-done.refs_2_.refs_7_, bf16[2048,512]{1,0:T(8,128)(2,1)S(1)} %bitcast.21), custom_call_target="tpu_custom_call" | custom-call | flops 1 | bytes 1 | tf_op jit(solution)/shard_map/mixed_part/pallas_call | solution.py:56
  63.0 0.7 copy-done.7
  63.7 4.4 %all-to-all-start.2 = ((bf16[4,128,2048]{2,1,0:T(8,128)(2,1)}), bf16[4,128,2048]{2,1,0:T(8,128)(2,1)}, u32[]{:S(2)}, u32[]{:S(2)}) async-start(bf16[4,128,2048]{2,1,0:T(8,128)(2,1)} %mixed_part.1.refs_8_), calls=%async_computation.2 | async-start | bytes 4194304 | tf_op jit(solution)/shard_map/all_to_all | solution.py:414
  68.1 0.0 collective-permute-done.8.refs_5_
  68.1 0.0 copy-start.3
  68.2 1.0 copy-done.3
  69.2 0.9 copy-done.8
  70.1 2.7 %weight_grad.1 = (f32[4,2,128,512]{3,2,1,0:T(8,128)S(1)}, bf16[4,2,128,512]{3,2,1,0:T(8,128)(2,1)S(1)}) custom-call(s32[5]{0:T(128)S(1)} %stack.23.refs_0_.at_ref, bf16[128,2048]{1,0:T(8,128)(2,1)} %bitcast.14.refs_1_, bf16[128,2048]{1,0:T(8,128)(2,1)S(1)} %copy-done.3, bf16[128,2048]{1,0:T(8,128)(2,1)S(1)} %collective-permute-done.6.refs_3_, ...), custom_call_target="tpu_custom_call" | custom-call | flops 1 | bytes 1 | tf_op jit(solution)/shard_map/weight_grad/pallas_call | solution.py:56
  72.9 0.0 copy-start.4
  72.9 0.1 collective-permute-start.9
  73.0 2.6 %collective-permute-done.9.refs_2_ = bf16[4,2,128,512]{3,2,1,0:T(8,128)(2,1)S(1)} collective-permute-done((bf16[4,2,128,512]{3,2,1,0:T(8,128)(2,1)S(1)}, bf16[4,2,128,512]{3,2,1,0:T(8,128)(2,1)S(1)}, u32[]{:S(2)}, u32[]{:S(2)}) %collective-permute-start.9) | collective-permute-done | bytes 1048608 | tf_op jit(solution)/shard_map/ppermute | solution.py:86
  75.6 0.7 add_core.1
  76.4 0.5 collective-permute-start.10
  76.9 3.6 %collective-permute-start.11 = (bf16[2,128,512]{2,1,0:T(8,128)(2,1)S(1)}, bf16[2,128,512]{2,1,0:T(8,128)(2,1)S(1)}, u32[]{:S(2)}, u32[]{:S(2)}) collective-permute-start(bf16[2,128,512]{2,1,0:T(8,128)(2,1)S(1)} %get-tuple-element.26), channel_id=1, source_target_pairs={{0,64},{32,96},{64,0},{96,32},{1,65},{33,97},{65,1},{97,33},{2,66}... | collective-permute-start | bytes 786440 | tf_op jit(solution)/shard_map/ppermute | solution.py:267
  80.4 1.0 collective-permute-start.12
  81.5 2.6 %head_cot.1 = (bf16[512,256]{1,0:T(8,128)(2,1)S(1)}, bf16[512,256]{1,0:T(8,128)(2,1)S(1)}) custom-call(s32[5]{0:T(128)S(1)} %stack.23.refs_0_.at_ref, bf16[128,2048]{1,0:T(8,128)(2,1)} %bitcast.14.refs_1_, bf16[128,2048]{1,0:T(8,128)(2,1)S(1)} %copy-done.4, bf16[128,2048]{1,0:T(8,128)(2,1)S(1)} %collective-permute-done.6.refs_3_, ...), custom_call_target="tpu_custom_call" | custom-call | flops 1 | bytes 1 | tf_op jit(solution)/shard_map/head_cot/pallas_call | solution.py:56
  84.1 1.6 %collective-permute-start.14 = (bf16[512,256]{1,0:T(8,128)(2,1)S(1)}, bf16[512,256]{1,0:T(8,128)(2,1)S(1)}, u32[]{:S(2)}, u32[]{:S(2)}) collective-permute-start(bf16[512,256]{1,0:T(8,128)(2,1)S(1)} %get-tuple-element.32), channel_id=1, source_target_pairs={{0,4},{4,0},{1,5},{5,1},{2,6},{6,2},{3,7},{7,3},{8,12},{12,8},{9,1... | collective-permute-start | bytes 786440 | tf_op jit(solution)/shard_map/ppermute | solution.py:86
  85.6 0.4 collective-permute-done.10.refs_2_
  86.0 6.4 %collective-permute-done.11.refs_3_ = bf16[2,128,512]{2,1,0:T(8,128)(2,1)S(1)} collective-permute-done((bf16[2,128,512]{2,1,0:T(8,128)(2,1)S(1)}, bf16[2,128,512]{2,1,0:T(8,128)(2,1)S(1)}, u32[]{:S(2)}, u32[]{:S(2)}) %collective-permute-start.11) | collective-permute-done | bytes 262176 | tf_op jit(solution)/shard_map/ppermute | solution.py:267
  92.4 0.7 add_z.1
  93.0 1.5 %collective-permute-start.13 = (bf16[128,512]{1,0:T(8,128)(2,1)S(1)}, bf16[128,512]{1,0:T(8,128)(2,1)S(1)}, u32[]{:S(2)}, u32[]{:S(2)}) collective-permute-start(bf16[128,512]{1,0:T(8,128)(2,1)S(1)} %get-tuple-element.29), channel_id=1, source_target_pairs={{0,16},{16,0},{1,17},{17,1},{2,18},{18,2},{3,19},{19,3},{4,20},{20... | collective-permute-start | bytes 393224 | tf_op jit(solution)/shard_map/ppermute | solution.py:86
  94.5 0.0 collective-permute-done.14.recv_ref
  94.5 7.1 %attention_backward.1.refs_2_ = bf16[8,384,256]{2,1,0:T(8,128)(2,1)S(1)} custom-call(s32[5]{0:T(128)S(1)} %stack.23.refs_0_.at_ref, bf16[8,384,256]{2,1,0:T(8,128)(2,1)S(1)} %copy-done.1, f32[2,16,1024]{2,1,0:T(8,128)S(1)} %reshape.86.bias_ref, f32[2,1,1024]{2,1,0:T(1,128)S(1)} %get-tuple-element.30.stat_ref, ...), custom_call_target="tpu_custom_call" | custom-call | flops 1 | bytes 1 | tf_op jit(solution)/shard_map/attention_backward/pallas_call | solution.py:361
  101.6 0.0 collective-permute-done.13.refs_1_
  101.6 1.3 %attach.1 = bf16[8,416,256]{2,1,0:T(8,128)(2,1)} custom-call(f32[128,512]{1,0:T(8,128)S(1)} %get-tuple-element.28.refs_0_, bf16[128,512]{1,0:T(8,128)(2,1)S(1)} %collective-permute-done.13.refs_1_, bf16[8,384,256]{2,1,0:T(8,128)(2,1)S(1)} %attention_backward.1.refs_2_), custom_call_target="tpu_custom_call" | custom-call | flops 1 | bytes 1 | tf_op jit(solution)/shard_map/attach/pallas_call | solution.py:56
  103.0 0.0 all-to-all-done.2.refs_0_
  103.0 5.1 %all-to-all-start.3 = ((bf16[8,416,256]{2,1,0:T(8,128)(2,1)}), bf16[8,416,256]{2,1,0:T(8,128)(2,1)S(1)}, u32[]{:S(2)}, u32[]{:S(2)}) async-start(bf16[8,416,256]{2,1,0:T(8,128)(2,1)} %attach.1), calls=%async_computation.3 | async-start | bytes 3407872 | tf_op jit(solution)/shard_map/all_to_all | solution.py:418
  108.1 2.6 %finish_mixed.1 = bf16[128,2048]{1,0:T(8,128)(2,1)} custom-call(bf16[4,128,2048]{2,1,0:T(8,128)(2,1)} %all-to-all-done.2.refs_0_), custom_call_target="tpu_custom_call" | custom-call | flops 1 | bytes 1 | tf_op jit(solution)/shard_map/finish_mixed/pallas_call | solution.py:56
  110.7 18.4 %all-to-all-done.3.refs_0_ = bf16[8,416,256]{2,1,0:T(8,128)(2,1)S(1)} async-done(((bf16[8,416,256]{2,1,0:T(8,128)(2,1)}), bf16[8,416,256]{2,1,0:T(8,128)(2,1)S(1)}, u32[]{:S(2)}, u32[]{:S(2)}) %all-to-all-start.3) | async-done | bytes 1703968 | tf_op jit(solution)/shard_map/all_to_all | solution.py:418
  129.1 1.4 %unpack_heads.1 = (bf16[128,2048]{1,0:T(8,128)(2,1)}, bf16[128,2048]{1,0:T(8,128)(2,1)}, bf16[128,2048]{1,0:T(8,128)(2,1)}, f32[16,2048]{1,0:T(8,128)}) custom-call(bf16[8,416,256]{2,1,0:T(8,128)(2,1)S(1)} %all-to-all-done.3.refs_0_), custom_call_target="tpu_custom_call" | custom-call | flops 1 | bytes 1 | tf_op jit(solution)/shard_map/unpack_heads/pallas_call | solution.py:56
  (24 shorter events, 0.1 us)
Async XLA Ops:
  0.6 0.8 copy-start.9
  2.2 15.6 %all-to-all-start = ((bf16[16,16,512]{2,1,0:T(8,128)(2,1)}), bf16[16,16,512]{2,1,0:T(8,128)(2,1)S(1)}, u32[]{:S(2)}, u32[]{:S(2)}) async-start(bf16[16,16,512]{2,1,0:T(8,128)(2,1)} %weight_blocks.1), calls=%async_computation | async-start | bytes 524288 | tf_op jit(solution)/shard_map/all_to_all | solution.py:143
  17.8 0.7 copy-start.5
  18.5 3.7 %copy-start.6 = (bf16[16,16,512]{2,1,0:T(8,128)(2,1)S(1)}, bf16[16,16,512]{2,1,0:T(8,128)(2,1)}, u32[]{:S(2)}) copy-start(bf16[16,16,512]{2,1,0:T(8,128)(2,1)} %copy-done.5) | copy-start | bytes 786436
  18.5 12.2 %copy-start.10 = (s32[1,2,16,3]{2,1,3,0:T(2,128)S(1)}, s32[1,2,16,3]{2,1,3,0:T(2,128)}, u32[]{:S(2)}) copy-start(s32[1,2,16,3]{2,1,3,0:T(2,128)} %param.12) | copy-start | bytes 1156
  18.5 23.7 %all-to-all-start.1 = ((bf16[8,384,256]{2,1,0:T(8,128)(2,1)}), bf16[8,384,256]{2,1,0:T(8,128)(2,1)S(1)}, u32[]{:S(2)}, u32[]{:S(2)}) async-start(bf16[8,384,256]{2,1,0:T(8,128)(2,1)} %hold.1), calls=%async_computation.1 | async-start | bytes 3145728 | tf_op jit(solution)/shard_map/all_to_all | solution.py:406
  22.3 19.5 %copy-start.11 = (s32[1,2]{1,0:T(1,128)S(1)}, s32[1,2]{1,0:T(1,128)}, u32[]{:S(2)}) copy-start(s32[1,2]{1,0:T(1,128)} %param.13) | copy-start | bytes 28
  22.3 13.9 %collective-permute-start.3 = (bf16[2,128,512]{2,1,0:T(8,128)(2,1)S(1)}, bf16[2,128,512]{2,1,0:T(8,128)(2,1)S(1)}, u32[]{:S(2)}, u32[]{:S(2)}) collective-permute-start(bf16[2,128,512]{2,1,0:T(8,128)(2,1)S(1)} %bitcast.24), channel_id=1, source_target_pairs={{0,96},{32,0},{64,32},{96,64},{1,97},{33,1},{65,33},{97,65},{2,98}... | collective-permute-start | bytes 786440 | tf_op jit(solution)/shard_map/ppermute | solution.py:144
  26.4 10.8 %collective-permute-start.2 = (bf16[2,128,512]{2,1,0:T(8,128)(2,1)S(1)}, bf16[2,128,512]{2,1,0:T(8,128)(2,1)S(1)}, u32[]{:S(2)}, u32[]{:S(2)}) collective-permute-start(bf16[2,128,512]{2,1,0:T(8,128)(2,1)S(1)} %bitcast.25), channel_id=1, source_target_pairs={{0,64},{32,96},{64,0},{96,32},{1,65},{33,97},{65,1},{97,33},{2,66}... | collective-permute-start | bytes 786440 | tf_op jit(solution)/shard_map/ppermute | solution.py:144
  26.4 13.4 %collective-permute-start.1 = (bf16[2,128,512]{2,1,0:T(8,128)(2,1)S(1)}, bf16[2,128,512]{2,1,0:T(8,128)(2,1)}, u32[]{:S(2)}, u32[]{:S(2)}) collective-permute-start(bf16[2,128,512]{2,1,0:T(8,128)(2,1)S(1)} %bitcast.26), channel_id=1, source_target_pairs={{0,32},{32,64},{64,96},{96,0},{1,33},{33,65},{65,97},{97,1},{2,34}... | collective-permute-start | bytes 786440 | tf_op jit(solution)/shard_map/ppermute | solution.py:144
  27.6 23.9 %collective-permute-start.6 = (bf16[128,2048]{1,0:T(8,128)(2,1)}, bf16[128,2048]{1,0:T(8,128)(2,1)S(1)}, u32[]{:S(2)}, u32[]{:S(2)}) collective-permute-start(bf16[128,2048]{1,0:T(8,128)(2,1)} %bitcast.14.refs_1_), channel_id=1, source_target_pairs={{0,3},{1,0},{2,1},{3,2},{4,7},{5,4},{6,5},{7,6},{8,11},{9,8},{10,9... | collective-permute-start | bytes 1572872 | tf_op jit(solution)/shard_map/ppermute | solution.py:152
  30.8 23.8 %collective-permute-start.5 = (bf16[128,2048]{1,0:T(8,128)(2,1)}, bf16[128,2048]{1,0:T(8,128)(2,1)S(1)}, u32[]{:S(2)}, u32[]{:S(2)}) collective-permute-start(bf16[128,2048]{1,0:T(8,128)(2,1)} %bitcast.14.refs_1_), channel_id=1, source_target_pairs={{0,1},{1,2},{2,3},{3,0},{4,5},{5,6},{6,7},{7,4},{8,9},{9,10},{10,1... | collective-permute-start | bytes 1572872 | tf_op jit(solution)/shard_map/ppermute | solution.py:151
  41.8 13.7 %collective-permute-start.4 = (bf16[4,2,128,512]{3,2,1,0:T(8,128)(2,1)}, bf16[4,2,128,512]{3,2,1,0:T(8,128)(2,1)}, u32[]{:S(2)}, u32[]{:S(2)}) collective-permute-start(bf16[4,2,128,512]{3,2,1,0:T(8,128)(2,1)} %place_z.1.refs_1_), channel_id=1, source_target_pairs={{0,8},{8,0},{1,9},{9,1},{2,10},{10,2},{3,11},{11,3},{4,12},{12,4},... | collective-permute-start | bytes 3145736 | tf_op jit(solution)/shard_map/ppermute | solution.py:86
  42.3 13.2 %copy-start = (bf16[8,384,256]{2,1,0:T(8,128)(2,1)}, bf16[8,384,256]{2,1,0:T(8,128)(2,1)S(1)}, u32[]{:S(2)}) copy-start(bf16[8,384,256]{2,1,0:T(8,128)(2,1)S(1)} %all-to-all-done.1.qkv_ref) | copy-start | bytes 4718596
  49.5 8.8 %collective-permute-start = (bf16[512,256]{1,0:T(8,128)(2,1)S(1)}, bf16[512,256]{1,0:T(8,128)(2,1)S(1)}, u32[]{:S(2)}, u32[]{:S(2)}) collective-permute-start(bf16[512,256]{1,0:T(8,128)(2,1)S(1)} %constant_dynamic-slice_fusion), channel_id=1, source_target_pairs={{0,4},{4,0},{1,5},{5,1},{2,6},{6,2},{3,7},{7,3},{8,12},{12,8},{9,1... | collective-permute-start | bytes 786440 | tf_op jit(solution)/shard_map/ppermute | solution.py:86
  52.3 15.9 %collective-permute-start.8 = (bf16[64,2048]{1,0:T(8,128)(2,1)}, bf16[64,2048]{1,0:T(8,128)(2,1)S(1)}, u32[]{:S(2)}, u32[]{:S(2)}) collective-permute-start(bf16[64,2048]{1,0:T(8,128)(2,1)} %slice.9), channel_id=1, source_target_pairs={{0,3},{1,0},{2,1},{3,2},{4,7},{5,4},{6,5},{7,6},{8,11},{9,8},{10,9... | collective-permute-start | bytes 786440 | tf_op jit(solution)/shard_map/ppermute | solution.py:153
  54.6 0.9 copy-start.2
  55.4 12.7 %collective-permute-start.7 = (bf16[64,2048]{1,0:T(8,128)(2,1)}, bf16[64,2048]{1,0:T(8,128)(2,1)}, u32[]{:S(2)}, u32[]{:S(2)}) collective-permute-start(bf16[64,2048]{1,0:T(8,128)(2,1)} %slice.8), channel_id=1, source_target_pairs={{0,1},{1,2},{2,3},{3,0},{4,5},{5,6},{6,7},{7,4},{8,9},{9,10},{10,1... | collective-permute-start | bytes 786440 | tf_op jit(solution)/shard_map/ppermute | solution.py:153
  63.0 0.7 copy-start.7
  63.7 39.3 %all-to-all-start.2 = ((bf16[4,128,2048]{2,1,0:T(8,128)(2,1)}), bf16[4,128,2048]{2,1,0:T(8,128)(2,1)}, u32[]{:S(2)}, u32[]{:S(2)}) async-start(bf16[4,128,2048]{2,1,0:T(8,128)(2,1)} %mixed_part.1.refs_8_), calls=%async_computation.2 | async-start | bytes 4194304 | tf_op jit(solution)/shard_map/all_to_all | solution.py:414
  68.1 1.0 copy-start.3
  69.2 0.9 copy-start.8
  72.9 8.6 %copy-start.4 = (bf16[128,2048]{1,0:T(8,128)(2,1)S(1)}, bf16[128,2048]{1,0:T(8,128)(2,1)}, u32[]{:S(2)}) copy-start(bf16[128,2048]{1,0:T(8,128)(2,1)} %copy-done.2) | copy-start | bytes 1572868
  72.9 2.7 %collective-permute-start.9 = (bf16[4,2,128,512]{3,2,1,0:T(8,128)(2,1)S(1)}, bf16[4,2,128,512]{3,2,1,0:T(8,128)(2,1)S(1)}, u32[]{:S(2)}, u32[]{:S(2)}) collective-permute-start(bf16[4,2,128,512]{3,2,1,0:T(8,128)(2,1)S(1)} %get-tuple-element.23), channel_id=1, source_target_pairs={{0,8},{8,0},{1,9},{9,1},{2,10},{10,2},{3,11},{11,3},{4,12},{12,4},... | collective-permute-start | bytes 3145736 | tf_op jit(solution)/shard_map/ppermute | solution.py:86
  76.4 9.7 %collective-permute-start.10 = (bf16[2,128,512]{2,1,0:T(8,128)(2,1)S(1)}, bf16[2,128,512]{2,1,0:T(8,128)(2,1)S(1)}, u32[]{:S(2)}, u32[]{:S(2)}) collective-permute-start(bf16[2,128,512]{2,1,0:T(8,128)(2,1)S(1)} %get-tuple-element.25), channel_id=1, source_target_pairs={{0,32},{32,64},{64,96},{96,0},{1,33},{33,65},{65,97},{97,1},{2,34}... | collective-permute-start | bytes 786440 | tf_op jit(solution)/shard_map/ppermute | solution.py:267
  76.9 15.5 %collective-permute-start.11 = (bf16[2,128,512]{2,1,0:T(8,128)(2,1)S(1)}, bf16[2,128,512]{2,1,0:T(8,128)(2,1)S(1)}, u32[]{:S(2)}, u32[]{:S(2)}) collective-permute-start(bf16[2,128,512]{2,1,0:T(8,128)(2,1)S(1)} %get-tuple-element.26), channel_id=1, source_target_pairs={{0,64},{32,96},{64,0},{96,32},{1,65},{33,97},{65,1},{97,33},{2,66}... | collective-permute-start | bytes 786440 | tf_op jit(solution)/shard_map/ppermute | solution.py:267
  80.4 11.9 %collective-permute-start.12 = (bf16[2,128,512]{2,1,0:T(8,128)(2,1)S(1)}, bf16[2,128,512]{2,1,0:T(8,128)(2,1)S(1)}, u32[]{:S(2)}, u32[]{:S(2)}) collective-permute-start(bf16[2,128,512]{2,1,0:T(8,128)(2,1)S(1)} %get-tuple-element.27.refs_0_), channel_id=1, source_target_pairs={{0,96},{32,0},{64,32},{96,64},{1,97},{33,1},{65,33},{97,65},{2,98}... | collective-permute-start | bytes 786440 | tf_op jit(solution)/shard_map/ppermute | solution.py:267
  81.5 13.1 %copy-start.1 = (bf16[8,384,256]{2,1,0:T(8,128)(2,1)S(1)}, bf16[8,384,256]{2,1,0:T(8,128)(2,1)}, u32[]{:S(2)}) copy-start(bf16[8,384,256]{2,1,0:T(8,128)(2,1)} %copy-done) | copy-start | bytes 4718596
  84.1 10.5 %collective-permute-start.14 = (bf16[512,256]{1,0:T(8,128)(2,1)S(1)}, bf16[512,256]{1,0:T(8,128)(2,1)S(1)}, u32[]{:S(2)}, u32[]{:S(2)}) collective-permute-start(bf16[512,256]{1,0:T(8,128)(2,1)S(1)} %get-tuple-element.32), channel_id=1, source_target_pairs={{0,4},{4,0},{1,5},{5,1},{2,6},{6,2},{3,7},{7,3},{8,12},{12,8},{9,1... | collective-permute-start | bytes 786440 | tf_op jit(solution)/shard_map/ppermute | solution.py:86
  93.0 8.6 %collective-permute-start.13 = (bf16[128,512]{1,0:T(8,128)(2,1)S(1)}, bf16[128,512]{1,0:T(8,128)(2,1)S(1)}, u32[]{:S(2)}, u32[]{:S(2)}) collective-permute-start(bf16[128,512]{1,0:T(8,128)(2,1)S(1)} %get-tuple-element.29), channel_id=1, source_target_pairs={{0,16},{16,0},{1,17},{17,1},{2,18},{18,2},{3,19},{19,3},{4,20},{20... | collective-permute-start | bytes 393224 | tf_op jit(solution)/shard_map/ppermute | solution.py:86
  103.0 26.1 %all-to-all-start.3 = ((bf16[8,416,256]{2,1,0:T(8,128)(2,1)}), bf16[8,416,256]{2,1,0:T(8,128)(2,1)S(1)}, u32[]{:S(2)}, u32[]{:S(2)}) async-start(bf16[8,416,256]{2,1,0:T(8,128)(2,1)} %attach.1), calls=%async_computation.3 | async-start | bytes 3407872 | tf_op jit(solution)/shard_map/all_to_all | solution.py:418

commit v4 on v3

--- a/solution.py
+++ b/solution.py
@@ -147,10 +147,19 @@
     return full.reshape(HD, 512), rows
 
 
-def gather_cot(own):
-    back = lax.ppermute(own, "y", ring(4, 1))
-    on = lax.ppermute(own, "y", ring(4, 3))
-    return own, back, on, lax.ppermute(back[:64], "y", ring(4, 1)), lax.ppermute(on[64:], "y", ring(4, 3))
+def near_cot(own):
+    return own, lax.ppermute(own, "y", ring(4, 1)), lax.ppermute(own, "y", ring(4, 3))
+
+
+def relay_kernel(back_ref, on_ref, first_ref, last_ref):
+    first_ref[...] = back_ref[:64]
+    last_ref[...] = on_ref[64:]
+
+
+def far_cot(back, on, after):
+    half = ((64, HD), BF)
+    first, last = whole(relay_kernel, "cot_relay", (half, half), back, on, after=after)
+    return lax.ppermute(first, "y", ring(4, 1)), lax.ppermute(last, "y", ring(4, 3))
 
 
 def place_cot(y, full_ref, own_ref, back_ref, on_ref, far_0_ref, far_1_ref):
@@ -164,31 +173,38 @@
 def head_cot_kernel(at_ref, *refs):
     cot_refs, (w_ref, keep_ref, send_ref, full_ref) = refs[:5], refs[5:]
     place_cot(at_ref[4], full_ref, *cot_refs)
-    for t in range(2):
-        rows = slice(256 * t, 256 * t + 256)
-        both = dot(full_ref[2 * t : 2 * t + 2].reshape(256, HD), w_ref[...]).astype(BF)
-        keep_ref[rows, :] = both[:, :256]
-        send_ref[rows, :] = both[:, 256:]
-
-
-def head_cot_parts(at, cot, weight):
+    both = dot(full_ref[...].reshape(512, HD), w_ref[...]).astype(BF)
+    keep_ref[...] = both[:, :256]
+    send_ref[...] = both[:, 256:]
+
+
+def head_cot_parts(at, cot, weight, after):
     half = ((512, 256), BF)
     full = pltpu.VMEM((4, 128, HD), BF)
-    return whole(head_cot_kernel, "head_cot", (half, half), at, *cot, weight, scalars=1, scratch=(full,))
-
-
-def mixed_part_kernel(at_ref, own_ref, other_ref, w_ref, out_ref):
-    for y in range(4):
-        own = own_ref[pl.ds(pl.multiple_of(512 * at_ref[3] + 128 * y, 128), 128), :]
-        other = other_ref[128 * y : 128 * y + 128, :]
-        for n in range(4):
-            outs = slice(512 * n, 512 * n + 512)
-            part = dot(own, w_ref[outs, :256], NT) + dot(other, w_ref[outs, 256:], NT)
-            out_ref[y, :, outs] = part.astype(BF)
-
-
-def mixed_parts(at, own, other, weight):
-    return whole(mixed_part_kernel, "mixed_part", ((4, 128, HD), BF), at, own, other, weight, scalars=1)
+    return whole(head_cot_kernel, "head_cot", (half, half), at, *cot, weight, scalars=1, after=after, scratch=(full,))
+
+
+def mixed_part_kernel(at_ref, own_ref, other_ref, w_ref, out_ref, pair_ref):
+    pair_ref[:, :256] = own_ref[pl.ds(pl.multiple_of(512 * at_ref[3], 512), 512), :]
+    pair_ref[:, 256:] = other_ref[...]
+    for n in range(4):
+        outs = slice(512 * n, 512 * n + 512)
+        out_ref[:, :, outs] = dot(pair_ref[...], w_ref[outs, :], NT).astype(BF).reshape(4, 128, 512)
+
+
+def mixed_parts(at, own, other, weight, after):
+    return whole(
+        mixed_part_kernel,
+        "mixed_part",
+        ((4, 128, HD), BF),
+        at,
+        own,
+        other,
+        weight,
+        scalars=1,
+        after=after,
+        scratch=(pltpu.VMEM((512, 512), BF),),
+    )
 
 
 def mixed_kernel(in_ref, out_ref):
@@ -209,16 +225,16 @@
         cot = full_ref[:, :, 512 * z : 512 * z + 512].reshape(512, 512)
         sum_ref[...] = dot(cot, pair_ref[...], TN).reshape(4, 128, 512)
         for h in range(2):
-            keep_ref[z, h] = sum_ref[2 * h + core]
+            keep_ref[z, h] = sum_ref[2 * h + core].astype(BF)
             send_ref[z, h] = sum_ref[2 * h + 1 - core].astype(BF)
 
 
 def add_core_kernel(at_ref, keep_ref, recv_ref, out_ref, *send_refs):
     z = at_ref[0]
-    out_ref[...] = keep_ref[z] + recv_ref[z].astype(F32)
+    out_ref[...] = keep_ref[z].astype(F32) + recv_ref[z].astype(F32)
     for step, ref in enumerate(send_refs, 1):
         to = lax.rem(z + step, 4)
-        ref[...] = (keep_ref[to] + recv_ref[to].astype(F32)).astype(BF)
+        ref[...] = (keep_ref[to].astype(F32) + recv_ref[to].astype(F32)).astype(BF)
 
 
 def add_z_kernel(at_ref, own_ref, a_ref, b_ref, c_ref, out_ref, send_ref):
@@ -250,7 +266,7 @@
     keep, send = whole(
         weight_grad_kernel,
         "weight_grad",
-        ((shape, F32), (shape, BF)),
+        ((shape, BF), (shape, BF)),
         at,
         *cot,
         own,
@@ -259,14 +275,19 @@
         after=after,
         scratch=(pltpu.VMEM((4, 128, HD), BF), pltpu.VMEM((512, 512), BF), pltpu.VMEM((4, 128, 512), F32)),
     )
-    two, one = ((2, 128, 512), BF), ((128, 512), BF)
+    first, two = send, ((2, 128, 512), BF)
     keep, *sends = whole(
         add_core_kernel, "add_core", ((two[0], F32), two, two, two), at, keep, swap(send, "core"), scalars=1
     )
-    started = sends[-1]
-    got = [lax.ppermute(send, "z", ring(4, step)) for step, send in enumerate(sends, 1)]
-    keep, send = whole(add_z_kernel, "add_z", ((one[0], F32), one), at, keep, *got, scalars=1)
-    return started, keep, swap(send, "xh")
+    return keep, [lax.ppermute(send, "z", ring(4, step)) for step, send in enumerate(sends, 1)], sends[-1], first
+
+
+def sum_z(at, keep, got, after):
+    one = ((128, 512), BF)
+    keep, send = whole(
+        add_z_kernel, "add_z", ((one[0], F32), one), at, keep, *got, scalars=1, after=after
+    )
+    return keep, swap(send, "xh")
 
 
 def live_bias(rand, glob):
@@ -286,7 +307,8 @@
     return s * (SCALE * LOG2E) + bias[:, None, :]
 
 
-def forward_kernel(qkv_ref, bias_ref, o_ref, stat_ref):
+def forward_kernel(qkv_ref, bias_ref, *refs):
+    o_ref, stat_ref = refs[-2:]
     k = qkv_ref[:, 128:256].reshape(LEN, HS)
     v_t = qkv_ref[:, 256:384].reshape(LEN, HS).T
     for t in range(LEN // TILE):
@@ -296,19 +318,19 @@
         top = jnp.max(s, axis=(0, 1), keepdims=True)
         p = jnp.exp2(s - top)
         total = jnp.sum(p, axis=(0, 1), keepdims=True)
-        p_low = (p * (1.0 / total)).astype(BF).reshape(LEN, TILE)
-        o_t = dot(v_t, p_low)
+        o_t = dot(v_t, p.astype(BF).reshape(LEN, TILE)) * (1.0 / total[0])
         o_ref[tok, :] = o_t.T.astype(BF)
         stat_ref[0, :, tok] = (top + jnp.log2(total))[0]
 
 
-def forward(qkv, bias):
+def forward(qkv, bias, after):
     return pl.pallas_call(
         forward_kernel,
         grid=(2,),
         in_specs=[
             pl.BlockSpec((8, QKV, HS), lambda h: (0, 0, h)),
             pl.BlockSpec((1, NB, LEN), lambda h: (h, 0, 0)),
+            *[HBM] * len(after),
         ],
         out_specs=[
             pl.BlockSpec((LEN, HS), lambda h: (0, h)),
@@ -319,9 +341,9 @@
             jax.ShapeDtypeStruct((2, 1, LEN), F32),
         ],
         compiler_params=params(),
-        cost_estimate=pl.CostEstimate(flops=1, bytes_accessed=1, transcendentals=0),
+        cost_estimate=pl.CostEstimate(flops=9 * 10**9, bytes_accessed=1, transcendentals=0),
         name="attention_forward",
-    )(qkv, bias)
+    )(qkv, bias, *after)
 
 
 def backward_kernel(at_ref, qkv_ref, bias_ref, stat_ref, o_ref, keep_ref, recv_ref, *refs):
@@ -400,19 +422,21 @@
 def on_device(queries, keys, values, out_weight, cotangent, rand_blocks, glob_blocks):
     at = jnp.stack([lax.axis_index(name) for name in DP + CTX]).astype(jnp.int32)
     xl = at[3]
-    cot = gather_cot(cotangent[0])
+    cot = near_cot(cotangent[0])
     weight, early = gather_weight(at, out_weight)
     qkv = hold(pack_heads(queries[0], keys[0], values[0]), (early,))
     qkv = lax.all_to_all(qkv, CTX, 0, 0, tiled=True)
 
     bias = live_bias(rand_blocks[0], glob_blocks[0])
-    attended, stat = forward(qkv, bias)
+    attended, stat = forward(qkv, bias, ())
+    cot += far_cot(cot[1], cot[2], (stat,))
     other = swap(lax.dynamic_slice(attended, (512 * (1 - xl), 0), (512, 256)))
-    keep, send = head_cot_parts(at, cot, weight)
-    part = mixed_parts(at, attended, other, weight)
-    started, rows, rows_recv = weight_grad(at, cot, attended, other, (part,))
+    part = mixed_parts(at, attended, other, weight, ())
+    rows, got, started, first = weight_grad(at, cot, attended, other, (part,))
+    keep, send = head_cot_parts(at, cot, weight, (first,))
     part = lax.all_to_all(part, "y", 0, 0, tiled=True)
     grads = backward(at, qkv, bias, stat, attended, keep, swap(send), (started,))
+    rows, rows_recv = sum_z(at, rows, got, (grads,))
     total_tokens = lax.axis_size(DP) * lax.axis_size(CTX) * cotangent.shape[1]
     grads = attach(rows, rows_recv, grads, 1.0 / math.sqrt(total_tokens))
     grads = lax.all_to_all(grads, CTX, 0, 0, tiled=True)

time: 132 us -> 129 us (0.977)
  starting transfers between devices: 41.2 us -> 44.4 us
  waiting for transfers between devices: 44 us -> 41 us
  local copies, waits for them, and re-layouts: 6.21 us -> 4.6 us
  Pallas kernels: 38 us -> 36.6 us
    ppermute x3, waiting for transfers between devices: 6.74 us -> 3.89 us  [weight_grad(): lax.ppermute(send, 'z', ring(4, step))]
    ppermute x3, waiting for transfers between devices: 8.89 us -> 6.71 us  [gather_weight(): far = [lax.ppermute(rows, 'z', ring(4, step)) for step in (1, 2, 3)]]
    unnamed x24 -> x20, local copies, waits for them, and re-layouts: 4.33 us -> 2.6 us
    slice x2 -> x0, local copies, waits for them, and re-layouts: 1.51 us -> none  [the longest x1 0.79 us: gather_cot(): back[:64]]
    ppermute x3, starting transfers between devices: 5.08 us -> 6.58 us  [weight_grad(): lax.ppermute(send, 'z', ring(4, step))]
    ppermute x4, waiting for transfers between devices: 0.35 us -> 1.78 us  [the longest x1 1.77 us: near_cot(): lax.ppermute(own, 'y', ring(4, 1))]
    ppermute x5, waiting for transfers between devices: 3.73 us -> 5.11 us  [swap(): return lax.ppermute(array, axis, ring(2, 1))]
    pallas_call x11 -> x12, Pallas kernels: 21.2 us -> 20.7 us  [whole(): pl.pallas_call(ordered, in_specs=[SMEM] * scalars + [VMEM] * (len(args) -...]
  transfers between devices with their start and end apart: 19 -> 19, of which waited for: 10 -> 7; matrix products, arithmetic and copies ran while one was open for 2% -> 2% of each run, Pallas kernels for 28% -> 27%
where the time goes in v4:
time: 129 us; the launch traced here: 128 us
  starting transfers between devices  44.4 us (34%)
  waiting for transfers between devices  41 us (32%)
  Pallas kernels  36.6 us (28%)
  local copies, waits for them, and re-layouts  4.6 us (4%)
    pallas_call x12, Pallas kernels, whole(): pl.pallas_call(ordered, in_specs=[SMEM] * scalars + [VMEM] * (len(args) -...  20.7 us
    all_to_all x1, waiting for transfers between devices, on_device(): grads = lax.all_to_all(grads, CTX, 0, 0, tiled=True)  17.6 us
    all_to_all x1, starting transfers between devices, gather_weight(): lax.all_to_all(blocks, ('xh',) + CTX, 0, 0, tiled=True).reshape(2, 128, 512)  7.12 us
    pallas_call x1, Pallas kernels, backward(): pl.pallas_call(backward_kernel, grid=(2,), in_specs=[SMEM, heads, pl.Bloc...  7.09 us
    ppermute x3, waiting for transfers between devices, gather_weight(): far = [lax.ppermute(rows, 'z', ring(4, step)) for step in (1, 2, 3)]  6.71 us
    ppermute x3, starting transfers between devices, weight_grad(): lax.ppermute(send, 'z', ring(4, step))  6.58 us
    ppermute x3, starting transfers between devices, gather_weight(): far = [lax.ppermute(rows, 'z', ring(4, step)) for step in (1, 2, 3)]  6.52 us
    pallas_call x1, Pallas kernels, forward(): pl.pallas_call(forward_kernel, grid=(2,), in_specs=[pl.BlockSpec((8, QKV,...  6.23 us
  transfers between devices with their start and end apart: 19, of which 7 were waited for; matrix products, arithmetic and copies ran while one was open for 2% of the time, Pallas kernels for 27%

profile of v4, /device:TPU:0, one launch (start us, length us, event | category | flops | bytes accessed | tf_op | source)
XLA Modules:
  0.0 127.6 jit_solution(7699899302446897449)
XLA Ops:
  0.6 0.0 copy-start.7
  0.6 0.8 copy-done.7
  1.5 0.7 weight_blocks.1
  2.2 7.1 %all-to-all-start = ((bf16[16,16,512]{2,1,0:T(8,128)(2,1)}), bf16[16,16,512]{2,1,0:T(8,128)(2,1)S(1)}, u32[]{:S(2)}, u32[]{:S(2)}) async-start(bf16[16,16,512]{2,1,0:T(8,128)(2,1)} %weight_blocks.1), calls=%async_computation | async-start | bytes 524288 | tf_op jit(solution)/shard_map/all_to_all | solution.py:143
  9.3 2.6 %pack_heads.1.refs_0_ = bf16[8,384,256]{2,1,0:T(8,128)(2,1)} custom-call(bf16[128,2048]{1,0:T(8,128)(2,1)} %bitcast.29, bf16[128,2048]{1,0:T(8,128)(2,1)} %bitcast.30, bf16[128,2048]{1,0:T(8,128)(2,1)} %bitcast.31), custom_call_target="tpu_custom_call" | custom-call | flops 1 | bytes 1 | tf_op jit(solution)/shard_map/pack_heads/pallas_call | solution.py:106
  11.9 5.9 %all-to-all-done = bf16[16,16,512]{2,1,0:T(8,128)(2,1)S(1)} async-done(((bf16[16,16,512]{2,1,0:T(8,128)(2,1)}), bf16[16,16,512]{2,1,0:T(8,128)(2,1)S(1)}, u32[]{:S(2)}, u32[]{:S(2)}) %all-to-all-start) | async-done | bytes 262176 | tf_op jit(solution)/shard_map/all_to_all | solution.py:143
  17.8 0.7 copy-done.5
  18.5 3.7 %all-to-all-start.1 = ((bf16[8,384,256]{2,1,0:T(8,128)(2,1)}), bf16[8,384,256]{2,1,0:T(8,128)(2,1)S(1)}, u32[]{:S(2)}, u32[]{:S(2)}) async-start(bf16[8,384,256]{2,1,0:T(8,128)(2,1)} %hold.1), calls=%async_computation.1 | async-start | bytes 3145728 | tf_op jit(solution)/shard_map/all_to_all | solution.py:428
  22.3 1.9 %collective-permute-start.5 = (bf16[128,2048]{1,0:T(8,128)(2,1)}, bf16[128,2048]{1,0:T(8,128)(2,1)S(1)}, u32[]{:S(2)}, u32[]{:S(2)}) collective-permute-start(bf16[128,2048]{1,0:T(8,128)(2,1)} %bitcast.14.refs_1_), channel_id=1, source_target_pairs={{0,1},{1,2},{2,3},{3,0},{4,5},{5,6},{6,7},{7,4},{8,9},{9,10},{10,1... | collective-permute-start | bytes 1572872 | tf_op jit(solution)/shard_map/ppermute | solution.py:151
  24.2 1.4 %collective-permute-start.6 = (bf16[128,2048]{1,0:T(8,128)(2,1)}, bf16[128,2048]{1,0:T(8,128)(2,1)S(1)}, u32[]{:S(2)}, u32[]{:S(2)}) collective-permute-start(bf16[128,2048]{1,0:T(8,128)(2,1)} %bitcast.14.refs_1_), channel_id=1, source_target_pairs={{0,3},{1,0},{2,1},{3,2},{4,7},{5,4},{6,5},{7,6},{8,11},{9,8},{10,9... | collective-permute-start | bytes 1572872 | tf_op jit(solution)/shard_map/ppermute | solution.py:151
  25.6 0.0 copy-done.8
  25.6 0.1 compare_reduce_fusion
  25.7 0.1 fusion.1
  25.7 1.9 %collective-permute-start.1 = (bf16[2,128,512]{2,1,0:T(8,128)(2,1)S(1)}, bf16[2,128,512]{2,1,0:T(8,128)(2,1)S(1)}, u32[]{:S(2)}, u32[]{:S(2)}) collective-permute-start(bf16[2,128,512]{2,1,0:T(8,128)(2,1)S(1)} %bitcast.24), channel_id=1, source_target_pairs={{0,32},{32,64},{64,96},{96,0},{1,33},{33,65},{65,97},{97,1},{2,34}... | collective-permute-start | bytes 786440 | tf_op jit(solution)/shard_map/ppermute | solution.py:144
  27.7 3.6 %collective-permute-start.2 = (bf16[2,128,512]{2,1,0:T(8,128)(2,1)S(1)}, bf16[2,128,512]{2,1,0:T(8,128)(2,1)S(1)}, u32[]{:S(2)}, u32[]{:S(2)}) collective-permute-start(bf16[2,128,512]{2,1,0:T(8,128)(2,1)S(1)} %bitcast.25), channel_id=1, source_target_pairs={{0,64},{32,96},{64,0},{96,32},{1,65},{33,97},{65,1},{97,33},{2,66}... | collective-permute-start | bytes 786440 | tf_op jit(solution)/shard_map/ppermute | solution.py:144
  31.3 1.0 collective-permute-start.3
  32.3 0.8 broadcast_in_dim.29
  33.1 1.1 reshape.86.bias_ref
  34.2 0.1 stack.23.refs_0_.at_ref
  34.3 1.8 %collective-permute-done.1.refs_2_ = bf16[2,128,512]{2,1,0:T(8,128)(2,1)S(1)} collective-permute-done((bf16[2,128,512]{2,1,0:T(8,128)(2,1)S(1)}, bf16[2,128,512]{2,1,0:T(8,128)(2,1)S(1)}, u32[]{:S(2)}, u32[]{:S(2)}) %collective-permute-start.1) | collective-permute-done | bytes 262176 | tf_op jit(solution)/shard_map/ppermute | solution.py:144
  36.1 4.9 %collective-permute-done.2.refs_3_ = bf16[2,128,512]{2,1,0:T(8,128)(2,1)S(1)} collective-permute-done((bf16[2,128,512]{2,1,0:T(8,128)(2,1)S(1)}, bf16[2,128,512]{2,1,0:T(8,128)(2,1)S(1)}, u32[]{:S(2)}, u32[]{:S(2)}) %collective-permute-start.2) | collective-permute-done | bytes 262176 | tf_op jit(solution)/shard_map/ppermute | solution.py:144
  41.0 0.0 collective-permute-done.3.refs_4_
  41.0 2.0 %place_z.1.refs_1_ = bf16[4,2,128,512]{3,2,1,0:T(8,128)(2,1)} custom-call(s32[5]{0:T(128)S(1)} %stack.23.refs_0_.at_ref, bf16[2,128,512]{2,1,0:T(8,128)(2,1)S(1)} %bitcast.27, bf16[2,128,512]{2,1,0:T(8,128)(2,1)S(1)} %collective-permute-done.1.refs_2_, bf16[2,128,512]{2,1,0:T(8,128)(2,1)S(1)} %collective-permute-done.2.refs_3_, ...), custom_call_target="tpu_custom_call" | custom-call | flops 1 | bytes 1 | tf_op jit(solution)/shard_map/place_z/pallas_call | solution.py:56
  43.0 0.0 collective-permute-start.4
  43.0 0.0 all-to-all-done.1.qkv_ref
  43.0 6.2 %attention_forward.1 = (bf16[1024,256]{1,0:T(8,128)(2,1)S(1)}, f32[2,1,1024]{2,1,0:T(1,128)S(1)}) custom-call(bf16[8,384,256]{2,1,0:T(8,128)(2,1)S(1)} %all-to-all-done.1.qkv_ref, f32[2,16,1024]{2,1,0:T(8,128)S(1)} %reshape.86.bias_ref), custom_call_target="tpu_custom_call" | custom-call | flops 8999999488 | bytes 1 | tf_op jit(solution)/shard_map/attention_forward/pallas_call | solution.py:327
  49.3 1.7 %collective-permute-start = (bf16[512,256]{1,0:T(8,128)(2,1)S(1)}, bf16[512,256]{1,0:T(8,128)(2,1)S(1)}, u32[]{:S(2)}, u32[]{:S(2)}) collective-permute-start(bf16[512,256]{1,0:T(8,128)(2,1)S(1)} %constant_dynamic-slice_fusion), channel_id=1, source_target_pairs={{0,4},{4,0},{1,5},{5,1},{2,6},{6,2},{3,7},{7,3},{8,12},{12,8},{9,1... | collective-permute-start | bytes 786440 | tf_op jit(solution)/shard_map/ppermute | solution.py:86
  51.0 1.8 %collective-permute-done.5.refs_0_.refs_2_ = bf16[128,2048]{1,0:T(8,128)(2,1)S(1)} collective-permute-done((bf16[128,2048]{1,0:T(8,128)(2,1)}, bf16[128,2048]{1,0:T(8,128)(2,1)S(1)}, u32[]{:S(2)}, u32[]{:S(2)}) %collective-permute-start.5) | collective-permute-done | bytes 524320 | tf_op jit(solution)/shard_map/ppermute | solution.py:151
  52.8 0.0 collective-permute-done.6.refs_1_.refs_3_
  52.8 0.9 cot_relay.1
  53.7 0.2 collective-permute-start.7
  53.9 3.0 %collective-permute-start.8 = (bf16[64,2048]{1,0:T(8,128)(2,1)}, bf16[64,2048]{1,0:T(8,128)(2,1)}, u32[]{:S(2)}, u32[]{:S(2)}) collective-permute-start(bf16[64,2048]{1,0:T(8,128)(2,1)} %get-tuple-element.26), channel_id=1, source_target_pairs={{0,3},{1,0},{2,1},{3,2},{4,7},{5,4},{6,5},{7,6},{8,11},{9,8},{10,9... | collective-permute-start | bytes 786440 | tf_op jit(solution)/shard_map/ppermute | solution.py:162
  56.9 0.0 collective-permute-done.4.refs_2_
  56.9 1.7 %place_core.1 = bf16[16,128,512]{2,1,0:T(8,128)(2,1)S(1)} custom-call(s32[5]{0:T(128)S(1)} %stack.23.refs_0_.at_ref, bf16[4,2,128,512]{3,2,1,0:T(8,128)(2,1)} %place_z.1.refs_1_, bf16[4,2,128,512]{3,2,1,0:T(8,128)(2,1)} %collective-permute-done.4.refs_2_), custom_call_target="tpu_custom_call" | custom-call | flops 1 | bytes 1 | tf_op jit(solution)/shard_map/place_core/pallas_call | solution.py:56
  58.6 0.0 collective-permute-done.refs_2_.refs_7_
  58.6 3.2 %mixed_part.1.refs_8_ = bf16[4,128,2048]{2,1,0:T(8,128)(2,1)} custom-call(s32[5]{0:T(128)S(1)} %stack.23.refs_0_.at_ref, bf16[1024,256]{1,0:T(8,128)(2,1)S(1)} %get-tuple-element.23.refs_1_.refs_6_.o_ref, bf16[512,256]{1,0:T(8,128)(2,1)S(1)} %collective-permute-done.refs_2_.refs_7_, bf16[2048,512]{1,0:T(8,128)(2,1)S(1)} %bitcast.21), custom_call_target="tpu_custom_call" | custom-call | flops 1 | bytes 1 | tf_op jit(solution)/shard_map/mixed_part/pallas_call | solution.py:56
  61.8 4.4 %all-to-all-start.2 = ((bf16[4,128,2048]{2,1,0:T(8,128)(2,1)}), bf16[4,128,2048]{2,1,0:T(8,128)(2,1)}, u32[]{:S(2)}, u32[]{:S(2)}) async-start(bf16[4,128,2048]{2,1,0:T(8,128)(2,1)} %mixed_part.1.refs_8_), calls=%async_computation.2 | async-start | bytes 4194304 | tf_op jit(solution)/shard_map/all_to_all | solution.py:437
  66.3 0.0 collective-permute-done.7.refs_4_
  66.3 0.0 collective-permute-done.8.refs_5_
  66.3 0.0 copy-start.3
  66.3 1.0 copy-done.3
  67.3 2.9 %weight_grad.1 = (bf16[4,2,128,512]{3,2,1,0:T(8,128)(2,1)S(1)}, bf16[4,2,128,512]{3,2,1,0:T(8,128)(2,1)S(1)}) custom-call(s32[5]{0:T(128)S(1)} %stack.23.refs_0_.at_ref, bf16[128,2048]{1,0:T(8,128)(2,1)} %bitcast.14.refs_1_, bf16[128,2048]{1,0:T(8,128)(2,1)S(1)} %collective-permute-done.5.refs_0_.refs_2_, bf16[128,2048]{1,0:T(8,128)(2,1)S(1)} %copy-done.3, ...), custom_call_target="tpu_custom_call" | custom-call | flops 1 | bytes 1 | tf_op jit(solution)/shard_map/weight_grad/pallas_call | solution.py:56
  70.2 0.1 collective-permute-start.9
  70.3 2.5 %head_cot.1 = (bf16[512,256]{1,0:T(8,128)(2,1)S(1)}, bf16[512,256]{1,0:T(8,128)(2,1)S(1)}) custom-call(s32[5]{0:T(128)S(1)} %stack.23.refs_0_.at_ref, bf16[128,2048]{1,0:T(8,128)(2,1)} %bitcast.14.refs_1_, bf16[128,2048]{1,0:T(8,128)(2,1)S(1)} %collective-permute-done.5.refs_0_.refs_2_, bf16[128,2048]{1,0:T(8,128)(2,1)S(1)} %copy-done.4, ...), custom_call_target="tpu_custom_call" | custom-call | flops 1 | bytes 1 | tf_op jit(solution)/shard_map/head_cot/pallas_call | solution.py:56
  72.8 1.6 %collective-permute-start.13 = (bf16[512,256]{1,0:T(8,128)(2,1)S(1)}, bf16[512,256]{1,0:T(8,128)(2,1)S(1)}, u32[]{:S(2)}, u32[]{:S(2)}) collective-permute-start(bf16[512,256]{1,0:T(8,128)(2,1)S(1)} %get-tuple-element.34), channel_id=1, source_target_pairs={{0,4},{4,0},{1,5},{5,1},{2,6},{6,2},{3,7},{7,3},{8,12},{12,8},{9,1... | collective-permute-start | bytes 786440 | tf_op jit(solution)/shard_map/ppermute | solution.py:86
  74.4 0.0 collective-permute-done.9.refs_2_
  74.4 0.8 add_core.1
  75.2 2.0 %collective-permute-start.10 = (bf16[2,128,512]{2,1,0:T(8,128)(2,1)S(1)}, bf16[2,128,512]{2,1,0:T(8,128)(2,1)S(1)}, u32[]{:S(2)}, u32[]{:S(2)}) collective-permute-start(bf16[2,128,512]{2,1,0:T(8,128)(2,1)S(1)} %get-tuple-element.30), channel_id=1, source_target_pairs={{0,32},{32,64},{64,96},{96,0},{1,33},{33,65},{65,97},{97,1},{2,34}... | collective-permute-start | bytes 786440 | tf_op jit(solution)/shard_map/ppermute | solution.py:282
  77.1 3.6 %collective-permute-start.11 = (bf16[2,128,512]{2,1,0:T(8,128)(2,1)S(1)}, bf16[2,128,512]{2,1,0:T(8,128)(2,1)S(1)}, u32[]{:S(2)}, u32[]{:S(2)}) collective-permute-start(bf16[2,128,512]{2,1,0:T(8,128)(2,1)S(1)} %get-tuple-element.31), channel_id=1, source_target_pairs={{0,64},{32,96},{64,0},{96,32},{1,65},{33,97},{65,1},{97,33},{2,66}... | collective-permute-start | bytes 786440 | tf_op jit(solution)/shard_map/ppermute | solution.py:282
  80.7 1.0 collective-permute-start.12
  81.7 0.0 collective-permute-done.13.recv_ref
  81.7 7.1 %attention_backward.1.refs_5_.refs_2_ = bf16[8,384,256]{2,1,0:T(8,128)(2,1)S(1)} custom-call(s32[5]{0:T(128)S(1)} %stack.23.refs_0_.at_ref, bf16[8,384,256]{2,1,0:T(8,128)(2,1)S(1)} %copy-done.1, f32[2,16,1024]{2,1,0:T(8,128)S(1)} %reshape.86.bias_ref, f32[2,1,1024]{2,1,0:T(1,128)S(1)} %get-tuple-element.24.refs_2_.stat_ref, ...), custom_call_target="tpu_custom_call" | custom-call | flops 1 | bytes 1 | tf_op jit(solution)/shard_map/attention_backward/pallas_call | solution.py:383
  88.8 0.0 collective-permute-done.10.refs_2_
  88.8 3.9 %collective-permute-done.11.refs_3_ = bf16[2,128,512]{2,1,0:T(8,128)(2,1)S(1)} collective-permute-done((bf16[2,128,512]{2,1,0:T(8,128)(2,1)S(1)}, bf16[2,128,512]{2,1,0:T(8,128)(2,1)S(1)}, u32[]{:S(2)}, u32[]{:S(2)}) %collective-permute-start.11) | collective-permute-done | bytes 262176 | tf_op jit(solution)/shard_map/ppermute | solution.py:282
  92.7 0.0 collective-permute-done.12.refs_4_
  92.7 0.7 add_z.1
  93.4 1.4 %collective-permute-start.14 = (bf16[128,512]{1,0:T(8,128)(2,1)S(1)}, bf16[128,512]{1,0:T(8,128)(2,1)S(1)}, u32[]{:S(2)}, u32[]{:S(2)}) collective-permute-start(bf16[128,512]{1,0:T(8,128)(2,1)S(1)} %get-tuple-element.36), channel_id=1, source_target_pairs={{0,16},{16,0},{1,17},{17,1},{2,18},{18,2},{3,19},{19,3},{4,20},{20... | collective-permute-start | bytes 393224 | tf_op jit(solution)/shard_map/ppermute | solution.py:86
  94.9 5.1 %collective-permute-done.14.refs_1_ = bf16[128,512]{1,0:T(8,128)(2,1)S(1)} collective-permute-done((bf16[128,512]{1,0:T(8,128)(2,1)S(1)}, bf16[128,512]{1,0:T(8,128)(2,1)S(1)}, u32[]{:S(2)}, u32[]{:S(2)}) %collective-permute-start.14) | collective-permute-done | bytes 131104 | tf_op jit(solution)/shard_map/ppermute | solution.py:86
  100.0 1.3 %attach.1 = bf16[8,416,256]{2,1,0:T(8,128)(2,1)} custom-call(f32[128,512]{1,0:T(8,128)S(1)} %get-tuple-element.35.refs_0_, bf16[128,512]{1,0:T(8,128)(2,1)S(1)} %collective-permute-done.14.refs_1_, bf16[8,384,256]{2,1,0:T(8,128)(2,1)S(1)} %attention_backward.1.refs_5_.refs_2_), custom_call_target="tpu_custom_call" | custom-call | flops 1 | bytes 1 | tf_op jit(solution)/shard_map/attach/pallas_call | solution.py:56
  101.3 0.0 all-to-all-done.2.refs_0_
  101.3 4.7 %all-to-all-start.3 = ((bf16[8,416,256]{2,1,0:T(8,128)(2,1)}), bf16[8,416,256]{2,1,0:T(8,128)(2,1)S(1)}, u32[]{:S(2)}, u32[]{:S(2)}) async-start(bf16[8,416,256]{2,1,0:T(8,128)(2,1)} %attach.1), calls=%async_computation.3 | async-start | bytes 3407872 | tf_op jit(solution)/shard_map/all_to_all | solution.py:442
  106.0 2.6 %finish_mixed.1 = bf16[128,2048]{1,0:T(8,128)(2,1)} custom-call(bf16[4,128,2048]{2,1,0:T(8,128)(2,1)} %all-to-all-done.2.refs_0_), custom_call_target="tpu_custom_call" | custom-call | flops 1 | bytes 1 | tf_op jit(solution)/shard_map/finish_mixed/pallas_call | solution.py:56
  108.7 17.6 %all-to-all-done.3.refs_0_ = bf16[8,416,256]{2,1,0:T(8,128)(2,1)S(1)} async-done(((bf16[8,416,256]{2,1,0:T(8,128)(2,1)}), bf16[8,416,256]{2,1,0:T(8,128)(2,1)S(1)}, u32[]{:S(2)}, u32[]{:S(2)}) %all-to-all-start.3) | async-done | bytes 1703968 | tf_op jit(solution)/shard_map/all_to_all | solution.py:442
  126.3 1.4 %unpack_heads.1 = (bf16[128,2048]{1,0:T(8,128)(2,1)}, bf16[128,2048]{1,0:T(8,128)(2,1)}, bf16[128,2048]{1,0:T(8,128)(2,1)}, f32[16,2048]{1,0:T(8,128)}) custom-call(bf16[8,416,256]{2,1,0:T(8,128)(2,1)S(1)} %all-to-all-done.3.refs_0_), custom_call_target="tpu_custom_call" | custom-call | flops 1 | bytes 1 | tf_op jit(solution)/shard_map/unpack_heads/pallas_call | solution.py:56
  (19 shorter events, 0.1 us)
Async XLA Ops:
  0.6 0.8 copy-start.7
  2.2 15.6 %all-to-all-start = ((bf16[16,16,512]{2,1,0:T(8,128)(2,1)}), bf16[16,16,512]{2,1,0:T(8,128)(2,1)S(1)}, u32[]{:S(2)}, u32[]{:S(2)}) async-start(bf16[16,16,512]{2,1,0:T(8,128)(2,1)} %weight_blocks.1), calls=%async_computation | async-start | bytes 524288 | tf_op jit(solution)/shard_map/all_to_all | solution.py:143
  17.8 0.7 copy-start.5
  18.5 7.0 %copy-start.8 = (s32[1,2,16,3]{2,1,3,0:T(2,128)S(1)}, s32[1,2,16,3]{2,1,3,0:T(2,128)}, u32[]{:S(2)}) copy-start(s32[1,2,16,3]{2,1,3,0:T(2,128)} %param.12) | copy-start | bytes 1156
  18.5 7.0 %copy-start.9 = (s32[1,2]{1,0:T(1,128)S(1)}, s32[1,2]{1,0:T(1,128)}, u32[]{:S(2)}) copy-start(s32[1,2]{1,0:T(1,128)} %param.13) | copy-start | bytes 28
  18.5 7.2 %copy-start.6 = (bf16[16,16,512]{2,1,0:T(8,128)(2,1)S(1)}, bf16[16,16,512]{2,1,0:T(8,128)(2,1)}, u32[]{:S(2)}) copy-start(bf16[16,16,512]{2,1,0:T(8,128)(2,1)} %copy-done.5) | copy-start | bytes 786436
  18.5 24.5 %all-to-all-start.1 = ((bf16[8,384,256]{2,1,0:T(8,128)(2,1)}), bf16[8,384,256]{2,1,0:T(8,128)(2,1)S(1)}, u32[]{:S(2)}, u32[]{:S(2)}) async-start(bf16[8,384,256]{2,1,0:T(8,128)(2,1)} %hold.1), calls=%async_computation.1 | async-start | bytes 3145728 | tf_op jit(solution)/shard_map/all_to_all | solution.py:428
  22.3 30.5 %collective-permute-start.5 = (bf16[128,2048]{1,0:T(8,128)(2,1)}, bf16[128,2048]{1,0:T(8,128)(2,1)S(1)}, u32[]{:S(2)}, u32[]{:S(2)}) collective-permute-start(bf16[128,2048]{1,0:T(8,128)(2,1)} %bitcast.14.refs_1_), channel_id=1, source_target_pairs={{0,1},{1,2},{2,3},{3,0},{4,5},{5,6},{6,7},{7,4},{8,9},{9,10},{10,1... | collective-permute-start | bytes 1572872 | tf_op jit(solution)/shard_map/ppermute | solution.py:151
  24.2 28.6 %collective-permute-start.6 = (bf16[128,2048]{1,0:T(8,128)(2,1)}, bf16[128,2048]{1,0:T(8,128)(2,1)S(1)}, u32[]{:S(2)}, u32[]{:S(2)}) collective-permute-start(bf16[128,2048]{1,0:T(8,128)(2,1)} %bitcast.14.refs_1_), channel_id=1, source_target_pairs={{0,3},{1,0},{2,1},{3,2},{4,7},{5,4},{6,5},{7,6},{8,11},{9,8},{10,9... | collective-permute-start | bytes 1572872 | tf_op jit(solution)/shard_map/ppermute | solution.py:151
  25.7 10.4 %collective-permute-start.1 = (bf16[2,128,512]{2,1,0:T(8,128)(2,1)S(1)}, bf16[2,128,512]{2,1,0:T(8,128)(2,1)S(1)}, u32[]{:S(2)}, u32[]{:S(2)}) collective-permute-start(bf16[2,128,512]{2,1,0:T(8,128)(2,1)S(1)} %bitcast.24), channel_id=1, source_target_pairs={{0,32},{32,64},{64,96},{96,0},{1,33},{33,65},{65,97},{97,1},{2,34}... | collective-permute-start | bytes 786440 | tf_op jit(solution)/shard_map/ppermute | solution.py:144
  27.7 13.3 %collective-permute-start.2 = (bf16[2,128,512]{2,1,0:T(8,128)(2,1)S(1)}, bf16[2,128,512]{2,1,0:T(8,128)(2,1)S(1)}, u32[]{:S(2)}, u32[]{:S(2)}) collective-permute-start(bf16[2,128,512]{2,1,0:T(8,128)(2,1)S(1)} %bitcast.25), channel_id=1, source_target_pairs={{0,64},{32,96},{64,0},{96,32},{1,65},{33,97},{65,1},{97,33},{2,66}... | collective-permute-start | bytes 786440 | tf_op jit(solution)/shard_map/ppermute | solution.py:144
  31.3 9.7 %collective-permute-start.3 = (bf16[2,128,512]{2,1,0:T(8,128)(2,1)S(1)}, bf16[2,128,512]{2,1,0:T(8,128)(2,1)}, u32[]{:S(2)}, u32[]{:S(2)}) collective-permute-start(bf16[2,128,512]{2,1,0:T(8,128)(2,1)S(1)} %bitcast.26), channel_id=1, source_target_pairs={{0,96},{32,0},{64,32},{96,64},{1,97},{33,1},{65,33},{97,65},{2,98}... | collective-permute-start | bytes 786440 | tf_op jit(solution)/shard_map/ppermute | solution.py:144
  43.0 13.9 %collective-permute-start.4 = (bf16[4,2,128,512]{3,2,1,0:T(8,128)(2,1)}, bf16[4,2,128,512]{3,2,1,0:T(8,128)(2,1)}, u32[]{:S(2)}, u32[]{:S(2)}) collective-permute-start(bf16[4,2,128,512]{3,2,1,0:T(8,128)(2,1)} %place_z.1.refs_1_), channel_id=1, source_target_pairs={{0,8},{8,0},{1,9},{9,1},{2,10},{10,2},{3,11},{11,3},{4,12},{12,4},... | collective-permute-start | bytes 3145736 | tf_op jit(solution)/shard_map/ppermute | solution.py:86
  43.0 6.2 %copy-start = (bf16[8,384,256]{2,1,0:T(8,128)(2,1)}, bf16[8,384,256]{2,1,0:T(8,128)(2,1)S(1)}, u32[]{:S(2)}) copy-start(bf16[8,384,256]{2,1,0:T(8,128)(2,1)S(1)} %all-to-all-done.1.qkv_ref) | copy-start | bytes 4718596
  49.3 9.3 %collective-permute-start = (bf16[512,256]{1,0:T(8,128)(2,1)S(1)}, bf16[512,256]{1,0:T(8,128)(2,1)S(1)}, u32[]{:S(2)}, u32[]{:S(2)}) collective-permute-start(bf16[512,256]{1,0:T(8,128)(2,1)S(1)} %constant_dynamic-slice_fusion), channel_id=1, source_target_pairs={{0,4},{4,0},{1,5},{5,1},{2,6},{6,2},{3,7},{7,3},{8,12},{12,8},{9,1... | collective-permute-start | bytes 786440 | tf_op jit(solution)/shard_map/ppermute | solution.py:86
  52.8 4.2 %copy-start.2 = (bf16[128,2048]{1,0:T(8,128)(2,1)}, bf16[128,2048]{1,0:T(8,128)(2,1)S(1)}, u32[]{:S(2)}) copy-start(bf16[128,2048]{1,0:T(8,128)(2,1)S(1)} %collective-permute-done.6.refs_1_.refs_3_) | copy-start | bytes 1572868
  53.7 12.6 %collective-permute-start.7 = (bf16[64,2048]{1,0:T(8,128)(2,1)}, bf16[64,2048]{1,0:T(8,128)(2,1)}, u32[]{:S(2)}, u32[]{:S(2)}) collective-permute-start(bf16[64,2048]{1,0:T(8,128)(2,1)} %get-tuple-element.25), channel_id=1, source_target_pairs={{0,1},{1,2},{2,3},{3,0},{4,5},{5,6},{6,7},{7,4},{8,9},{9,10},{10,1... | collective-permute-start | bytes 786440 | tf_op jit(solution)/shard_map/ppermute | solution.py:162
  53.9 12.3 %collective-permute-start.8 = (bf16[64,2048]{1,0:T(8,128)(2,1)}, bf16[64,2048]{1,0:T(8,128)(2,1)}, u32[]{:S(2)}, u32[]{:S(2)}) collective-permute-start(bf16[64,2048]{1,0:T(8,128)(2,1)} %get-tuple-element.26), channel_id=1, source_target_pairs={{0,3},{1,0},{2,1},{3,2},{4,7},{5,4},{6,5},{7,6},{8,11},{9,8},{10,9... | collective-permute-start | bytes 786440 | tf_op jit(solution)/shard_map/ppermute | solution.py:162
  61.8 39.5 %all-to-all-start.2 = ((bf16[4,128,2048]{2,1,0:T(8,128)(2,1)}), bf16[4,128,2048]{2,1,0:T(8,128)(2,1)}, u32[]{:S(2)}, u32[]{:S(2)}) async-start(bf16[4,128,2048]{2,1,0:T(8,128)(2,1)} %mixed_part.1.refs_8_), calls=%async_computation.2 | async-start | bytes 4194304 | tf_op jit(solution)/shard_map/all_to_all | solution.py:437
  66.3 1.0 copy-start.3
  67.3 3.0 %copy-start.4 = (bf16[128,2048]{1,0:T(8,128)(2,1)S(1)}, bf16[128,2048]{1,0:T(8,128)(2,1)}, u32[]{:S(2)}) copy-start(bf16[128,2048]{1,0:T(8,128)(2,1)} %copy-done.2) | copy-start | bytes 1572868
  70.2 4.2 %collective-permute-start.9 = (bf16[4,2,128,512]{3,2,1,0:T(8,128)(2,1)S(1)}, bf16[4,2,128,512]{3,2,1,0:T(8,128)(2,1)S(1)}, u32[]{:S(2)}, u32[]{:S(2)}) collective-permute-start(bf16[4,2,128,512]{3,2,1,0:T(8,128)(2,1)S(1)} %get-tuple-element.28.refs_7_), channel_id=1, source_target_pairs={{0,8},{8,0},{1,9},{9,1},{2,10},{10,2},{3,11},{11,3},{4,12},{12,4},... | collective-permute-start | bytes 3145736 | tf_op jit(solution)/shard_map/ppermute | solution.py:86
  72.8 8.9 %copy-start.1 = (bf16[8,384,256]{2,1,0:T(8,128)(2,1)S(1)}, bf16[8,384,256]{2,1,0:T(8,128)(2,1)}, u32[]{:S(2)}) copy-start(bf16[8,384,256]{2,1,0:T(8,128)(2,1)} %copy-done) | copy-start | bytes 4718596
  72.8 8.9 %collective-permute-start.13 = (bf16[512,256]{1,0:T(8,128)(2,1)S(1)}, bf16[512,256]{1,0:T(8,128)(2,1)S(1)}, u32[]{:S(2)}, u32[]{:S(2)}) collective-permute-start(bf16[512,256]{1,0:T(8,128)(2,1)S(1)} %get-tuple-element.34), channel_id=1, source_target_pairs={{0,4},{4,0},{1,5},{5,1},{2,6},{6,2},{3,7},{7,3},{8,12},{12,8},{9,1... | collective-permute-start | bytes 786440 | tf_op jit(solution)/shard_map/ppermute | solution.py:86
  75.2 13.7 %collective-permute-start.10 = (bf16[2,128,512]{2,1,0:T(8,128)(2,1)S(1)}, bf16[2,128,512]{2,1,0:T(8,128)(2,1)S(1)}, u32[]{:S(2)}, u32[]{:S(2)}) collective-permute-start(bf16[2,128,512]{2,1,0:T(8,128)(2,1)S(1)} %get-tuple-element.30), channel_id=1, source_target_pairs={{0,32},{32,64},{64,96},{96,0},{1,33},{33,65},{65,97},{97,1},{2,34}... | collective-permute-start | bytes 786440 | tf_op jit(solution)/shard_map/ppermute | solution.py:282
  77.1 15.6 %collective-permute-start.11 = (bf16[2,128,512]{2,1,0:T(8,128)(2,1)S(1)}, bf16[2,128,512]{2,1,0:T(8,128)(2,1)S(1)}, u32[]{:S(2)}, u32[]{:S(2)}) collective-permute-start(bf16[2,128,512]{2,1,0:T(8,128)(2,1)S(1)} %get-tuple-element.31), channel_id=1, source_target_pairs={{0,64},{32,96},{64,0},{96,32},{1,65},{33,97},{65,1},{97,33},{2,66}... | collective-permute-start | bytes 786440 | tf_op jit(solution)/shard_map/ppermute | solution.py:282
  80.7 12.0 %collective-permute-start.12 = (bf16[2,128,512]{2,1,0:T(8,128)(2,1)S(1)}, bf16[2,128,512]{2,1,0:T(8,128)(2,1)S(1)}, u32[]{:S(2)}, u32[]{:S(2)}) collective-permute-start(bf16[2,128,512]{2,1,0:T(8,128)(2,1)S(1)} %get-tuple-element.32.refs_0_), channel_id=1, source_target_pairs={{0,96},{32,0},{64,32},{96,64},{1,97},{33,1},{65,33},{97,65},{2,98}... | collective-permute-start | bytes 786440 | tf_op jit(solution)/shard_map/ppermute | solution.py:282
  93.4 6.6 %collective-permute-start.14 = (bf16[128,512]{1,0:T(8,128)(2,1)S(1)}, bf16[128,512]{1,0:T(8,128)(2,1)S(1)}, u32[]{:S(2)}, u32[]{:S(2)}) collective-permute-start(bf16[128,512]{1,0:T(8,128)(2,1)S(1)} %get-tuple-element.36), channel_id=1, source_target_pairs={{0,16},{16,0},{1,17},{17,1},{2,18},{18,2},{3,19},{19,3},{4,20},{20... | collective-permute-start | bytes 393224 | tf_op jit(solution)/shard_map/ppermute | solution.py:86
  101.3 24.9 %all-to-all-start.3 = ((bf16[8,416,256]{2,1,0:T(8,128)(2,1)}), bf16[8,416,256]{2,1,0:T(8,128)(2,1)S(1)}, u32[]{:S(2)}, u32[]{:S(2)}) async-start(bf16[8,416,256]{2,1,0:T(8,128)(2,1)} %attach.1), calls=%async_computation.3 | async-start | bytes 3407872 | tf_op jit(solution)/shard_map/all_to_all | solution.py:442

commit v5 on v4

--- a/solution.py
+++ b/solution.py
@@ -299,7 +299,8 @@
     return jnp.repeat(bias, BLK, axis=2)
 
 
-TILE = 256
+TILE = 512
+STEP = TILE // 128
 
 
 def scores_at(k, q, bias):
@@ -313,7 +314,7 @@
     v_t = qkv_ref[:, 256:384].reshape(LEN, HS).T
     for t in range(LEN // TILE):
         tok = slice(TILE * t, TILE * t + TILE)
-        q = qkv_ref[2 * t : 2 * t + 2, :128].reshape(TILE, HS)
+        q = qkv_ref[STEP * t : STEP * t + STEP, :128].reshape(TILE, HS)
         s = scores_at(k, q, bias_ref[0, :, tok])
         top = jnp.max(s, axis=(0, 1), keepdims=True)
         p = jnp.exp2(s - top)
@@ -353,7 +354,7 @@
     k_t = k.T
     for t in range(LEN // TILE):
         tok = slice(TILE * t, TILE * t + TILE)
-        q = qkv_ref[2 * t : 2 * t + 2, :128].reshape(TILE, HS)
+        q = qkv_ref[STEP * t : STEP * t + STEP, :128].reshape(TILE, HS)
         half, part = divmod(TILE * t, 512)
         part = slice(part, part + TILE)
         do = jnp.where(at_ref[3] == half, keep_ref[part, :], recv_ref[part, :])
@@ -363,7 +364,7 @@
         dp = dot(v, do, NT)
         ds = (p * (dp - delta)).astype(BF)
         dq = dot(k_t, ds).T * SCALE
-        out_ref[2 * t : 2 * t + 2, :128] = dq.astype(BF).reshape(2, 128, HS)
+        out_ref[STEP * t : STEP * t + STEP, :128] = dq.astype(BF).reshape(STEP, 128, HS)
         dk = dot(ds, q)
         dv = dot(p.astype(BF), do)
         if t == 0:
@@ -424,7 +425,7 @@
     xl = at[3]
     cot = near_cot(cotangent[0])
     weight, early = gather_weight(at, out_weight)
-    qkv = hold(pack_heads(queries[0], keys[0], values[0]), (early,))
+    qkv = hold(pack_heads(queries[0], keys[0], values[0]), (early, *cot[1:3]))
     qkv = lax.all_to_all(qkv, CTX, 0, 0, tiled=True)
 
     bias = live_bias(rand_blocks[0], glob_blocks[0])

time: 129 us -> 127 us (0.984)
  Pallas kernels: 36.6 us -> 34.4 us
  local copies, waits for them, and re-layouts: 4.6 us -> 3.13 us
  waiting for transfers between devices: 41 us -> 42.3 us
    ppermute x3, waiting for transfers between devices: 6.71 us -> 8.85 us  [gather_weight(): far = [lax.ppermute(rows, 'z', ring(4, step)) for step in (1, 2, 3)]]
    pallas_call x1, Pallas kernels: 6.23 us -> 4.22 us  [forward(): pl.pallas_call(forward_kernel, grid=(2,), in_specs=[pl.BlockSpec((8, QKV,...]
    ppermute x1, waiting for transfers between devices: 1.77 us -> 0.01 us  [near_cot(): lax.ppermute(own, 'y', ring(4, 1))]
    all_to_all x1, waiting for transfers between devices: 0.01 us -> 1.73 us  [on_device(): qkv = lax.all_to_all(qkv, CTX, 0, 0, tiled=True)]
  transfers between devices with their start and end apart: 19 -> 19, of which waited for: 7 -> 8; matrix products, arithmetic and copies ran while one was open for 2% -> 0% of each run, Pallas kernels for 27% -> 26%
where the time goes in v5:
time: 127 us; the launch traced here: 126 us
  starting transfers between devices  44.9 us (35%)
  waiting for transfers between devices  42.3 us (33%)
  Pallas kernels  34.4 us (27%)
  local copies, waits for them, and re-layouts  3.13 us (2%)
    pallas_call x12, Pallas kernels, whole(): pl.pallas_call(ordered, in_specs=[SMEM] * scalars + [VMEM] * (len(args) -...  21.1 us
    all_to_all x1, waiting for transfers between devices, on_device(): grads = lax.all_to_all(grads, CTX, 0, 0, tiled=True)  17.6 us
    ppermute x3, waiting for transfers between devices, gather_weight(): far = [lax.ppermute(rows, 'z', ring(4, step)) for step in (1, 2, 3)]  8.85 us
    ppermute x3, starting transfers between devices, weight_grad(): lax.ppermute(send, 'z', ring(4, step))  6.59 us
    pallas_call x1, Pallas kernels, backward(): pl.pallas_call(backward_kernel, grid=(2,), in_specs=[SMEM, heads, pl.Bloc...  6.54 us
    ppermute x3, starting transfers between devices, gather_weight(): far = [lax.ppermute(rows, 'z', ring(4, step)) for step in (1, 2, 3)]  6.52 us
    all_to_all x1, waiting for transfers between devices, gather_weight(): lax.all_to_all(blocks, ('xh',) + CTX, 0, 0, tiled=True).reshape(2, 128, 512)  5.91 us
    all_to_all x1, starting transfers between devices, gather_weight(): lax.all_to_all(blocks, ('xh',) + CTX, 0, 0, tiled=True).reshape(2, 128, 512)  5.91 us
  transfers between devices with their start and end apart: 19, of which 8 were waited for; matrix products, arithmetic and copies ran while one was open for 0% of the time, Pallas kernels for 26%

profile of v5, /device:TPU:0, one launch (start us, length us, event | category | flops | bytes accessed | tf_op | source)
XLA Modules:
  0.0 125.8 jit_solution(10706743494229993430)
XLA Ops:
  0.6 1.7 %collective-permute-start = (bf16[128,2048]{1,0:T(8,128)(2,1)}, bf16[128,2048]{1,0:T(8,128)(2,1)S(1)}, u32[]{:S(2)}, u32[]{:S(2)}) collective-permute-start(bf16[128,2048]{1,0:T(8,128)(2,1)} %bitcast.28), channel_id=1, source_target_pairs={{0,1},{1,2},{2,3},{3,0},{4,5},{5,6},{6,7},{7,4},{8,9},{9,10},{10,1... | collective-permute-start | bytes 1572872 | tf_op jit(solution)/shard_map/ppermute | solution.py:151
  2.4 1.6 %collective-permute-start.1 = (bf16[128,2048]{1,0:T(8,128)(2,1)}, bf16[128,2048]{1,0:T(8,128)(2,1)}, u32[]{:S(2)}, u32[]{:S(2)}) collective-permute-start(bf16[128,2048]{1,0:T(8,128)(2,1)} %bitcast.29), channel_id=1, source_target_pairs={{0,3},{1,0},{2,1},{3,2},{4,7},{5,4},{6,5},{7,6},{8,11},{9,8},{10,9... | collective-permute-start | bytes 1572872 | tf_op jit(solution)/shard_map/ppermute | solution.py:151
  3.9 0.8 copy-done.7
  4.8 0.7 weight_blocks.1
  5.5 5.9 %all-to-all-start = ((bf16[16,16,512]{2,1,0:T(8,128)(2,1)}), bf16[16,16,512]{2,1,0:T(8,128)(2,1)S(1)}, u32[]{:S(2)}, u32[]{:S(2)}) async-start(bf16[16,16,512]{2,1,0:T(8,128)(2,1)} %weight_blocks.1), calls=%async_computation | async-start | bytes 524288 | tf_op jit(solution)/shard_map/all_to_all | solution.py:143
  11.4 2.6 %pack_heads.1.refs_0_ = bf16[8,384,256]{2,1,0:T(8,128)(2,1)} custom-call(bf16[128,2048]{1,0:T(8,128)(2,1)} %bitcast.33, bf16[128,2048]{1,0:T(8,128)(2,1)} %bitcast.34, bf16[128,2048]{1,0:T(8,128)(2,1)} %bitcast.35), custom_call_target="tpu_custom_call" | custom-call | flops 1 | bytes 1 | tf_op jit(solution)/shard_map/pack_heads/pallas_call | solution.py:106
  14.0 5.9 %all-to-all-done = bf16[16,16,512]{2,1,0:T(8,128)(2,1)S(1)} async-done(((bf16[16,16,512]{2,1,0:T(8,128)(2,1)}), bf16[16,16,512]{2,1,0:T(8,128)(2,1)S(1)}, u32[]{:S(2)}, u32[]{:S(2)}) %all-to-all-start) | async-done | bytes 262176 | tf_op jit(solution)/shard_map/all_to_all | solution.py:143
  19.9 0.0 collective-permute-done.refs_2_.refs_0_
  19.9 0.0 collective-permute-done.1.refs_3_.refs_1_
  19.9 0.7 copy-done.4
  20.6 0.2 copy-done
  20.8 4.2 %all-to-all-start.1 = ((bf16[8,384,256]{2,1,0:T(8,128)(2,1)}), bf16[8,384,256]{2,1,0:T(8,128)(2,1)S(1)}, u32[]{:S(2)}, u32[]{:S(2)}) async-start(bf16[8,384,256]{2,1,0:T(8,128)(2,1)} %hold.1), calls=%async_computation.1 | async-start | bytes 3145728 | tf_op jit(solution)/shard_map/all_to_all | solution.py:429
  25.0 0.0 copy-done.9
  25.0 0.1 compare_reduce_fusion
  25.1 0.1 fusion.1
  25.2 1.9 %collective-permute-start.3 = (bf16[2,128,512]{2,1,0:T(8,128)(2,1)S(1)}, bf16[2,128,512]{2,1,0:T(8,128)(2,1)S(1)}, u32[]{:S(2)}, u32[]{:S(2)}) collective-permute-start(bf16[2,128,512]{2,1,0:T(8,128)(2,1)S(1)} %bitcast.24), channel_id=1, source_target_pairs={{0,32},{32,64},{64,96},{96,0},{1,33},{33,65},{65,97},{97,1},{2,34}... | collective-permute-start | bytes 786440 | tf_op jit(solution)/shard_map/ppermute | solution.py:144
  27.1 3.6 %collective-permute-start.4 = (bf16[2,128,512]{2,1,0:T(8,128)(2,1)S(1)}, bf16[2,128,512]{2,1,0:T(8,128)(2,1)S(1)}, u32[]{:S(2)}, u32[]{:S(2)}) collective-permute-start(bf16[2,128,512]{2,1,0:T(8,128)(2,1)S(1)} %bitcast.25), channel_id=1, source_target_pairs={{0,64},{32,96},{64,0},{96,32},{1,65},{33,97},{65,1},{97,33},{2,66}... | collective-permute-start | bytes 786440 | tf_op jit(solution)/shard_map/ppermute | solution.py:144
  30.7 1.0 collective-permute-start.5
  31.8 0.1 broadcast_in_dim.29
  31.9 0.1 reshape.86.bias_ref
  32.0 0.1 stack.23.refs_0_.at_ref
  32.1 3.5 %collective-permute-done.3.refs_2_ = bf16[2,128,512]{2,1,0:T(8,128)(2,1)S(1)} collective-permute-done((bf16[2,128,512]{2,1,0:T(8,128)(2,1)S(1)}, bf16[2,128,512]{2,1,0:T(8,128)(2,1)S(1)}, u32[]{:S(2)}, u32[]{:S(2)}) %collective-permute-start.3) | collective-permute-done | bytes 262176 | tf_op jit(solution)/shard_map/ppermute | solution.py:144
  35.6 5.4 %collective-permute-done.4.refs_3_ = bf16[2,128,512]{2,1,0:T(8,128)(2,1)S(1)} collective-permute-done((bf16[2,128,512]{2,1,0:T(8,128)(2,1)S(1)}, bf16[2,128,512]{2,1,0:T(8,128)(2,1)S(1)}, u32[]{:S(2)}, u32[]{:S(2)}) %collective-permute-start.4) | collective-permute-done | bytes 262176 | tf_op jit(solution)/shard_map/ppermute | solution.py:144
  41.0 0.0 collective-permute-done.5.refs_4_
  41.0 1.6 %place_z.1.refs_1_ = bf16[4,2,128,512]{3,2,1,0:T(8,128)(2,1)} custom-call(s32[5]{0:T(128)S(1)} %stack.23.refs_0_.at_ref, bf16[2,128,512]{2,1,0:T(8,128)(2,1)S(1)} %bitcast.27, bf16[2,128,512]{2,1,0:T(8,128)(2,1)S(1)} %collective-permute-done.3.refs_2_, bf16[2,128,512]{2,1,0:T(8,128)(2,1)S(1)} %collective-permute-done.4.refs_3_, ...), custom_call_target="tpu_custom_call" | custom-call | flops 1 | bytes 1 | tf_op jit(solution)/shard_map/place_z/pallas_call | solution.py:56
  42.6 0.0 collective-permute-start.6
  42.6 1.7 %all-to-all-done.1.qkv_ref = bf16[8,384,256]{2,1,0:T(8,128)(2,1)S(1)} async-done(((bf16[8,384,256]{2,1,0:T(8,128)(2,1)}), bf16[8,384,256]{2,1,0:T(8,128)(2,1)S(1)}, u32[]{:S(2)}, u32[]{:S(2)}) %all-to-all-start.1) | async-done | bytes 1572896 | tf_op jit(solution)/shard_map/all_to_all | solution.py:429
  44.3 4.2 %attention_forward.1 = (bf16[1024,256]{1,0:T(8,128)(2,1)S(1)}, f32[2,1,1024]{2,1,0:T(1,128)S(1)}) custom-call(bf16[8,384,256]{2,1,0:T(8,128)(2,1)S(1)} %all-to-all-done.1.qkv_ref, f32[2,16,1024]{2,1,0:T(8,128)S(1)} %reshape.86.bias_ref), custom_call_target="tpu_custom_call" | custom-call | flops 8999999488 | bytes 1 | tf_op jit(solution)/shard_map/attention_forward/pallas_call | solution.py:328
  48.6 1.5 %collective-permute-start.2 = (bf16[512,256]{1,0:T(8,128)(2,1)S(1)}, bf16[512,256]{1,0:T(8,128)(2,1)S(1)}, u32[]{:S(2)}, u32[]{:S(2)}) collective-permute-start(bf16[512,256]{1,0:T(8,128)(2,1)S(1)} %constant_dynamic-slice_fusion), channel_id=1, source_target_pairs={{0,4},{4,0},{1,5},{5,1},{2,6},{6,2},{3,7},{7,3},{8,12},{12,8},{9,1... | collective-permute-start | bytes 786440 | tf_op jit(solution)/shard_map/ppermute | solution.py:86
  50.1 1.8 %cot_relay.1 = (bf16[64,2048]{1,0:T(8,128)(2,1)}, bf16[64,2048]{1,0:T(8,128)(2,1)}) custom-call(bf16[128,2048]{1,0:T(8,128)(2,1)S(1)} %copy-done.1, bf16[128,2048]{1,0:T(8,128)(2,1)} %collective-permute-done.1.refs_3_.refs_1_, f32[2,1,1024]{2,1,0:T(1,128)S(1)} %get-tuple-element.24.refs_2_.stat_ref), custom_call_target="tpu_custom_call" | custom-call | flops 1 | bytes 1 | tf_op jit(solution)/shard_map/cot_relay/pallas_call | solution.py:56
  52.0 0.8 collective-permute-start.7
  52.8 2.4 %collective-permute-start.8 = (bf16[64,2048]{1,0:T(8,128)(2,1)}, bf16[64,2048]{1,0:T(8,128)(2,1)}, u32[]{:S(2)}, u32[]{:S(2)}) collective-permute-start(bf16[64,2048]{1,0:T(8,128)(2,1)} %get-tuple-element.26), channel_id=1, source_target_pairs={{0,3},{1,0},{2,1},{3,2},{4,7},{5,4},{6,5},{7,6},{8,11},{9,8},{10,9... | collective-permute-start | bytes 786440 | tf_op jit(solution)/shard_map/ppermute | solution.py:162
  55.2 0.0 collective-permute-done.6.refs_2_
  55.2 1.7 %place_core.1 = bf16[16,128,512]{2,1,0:T(8,128)(2,1)S(1)} custom-call(s32[5]{0:T(128)S(1)} %stack.23.refs_0_.at_ref, bf16[4,2,128,512]{3,2,1,0:T(8,128)(2,1)} %place_z.1.refs_1_, bf16[4,2,128,512]{3,2,1,0:T(8,128)(2,1)} %collective-permute-done.6.refs_2_), custom_call_target="tpu_custom_call" | custom-call | flops 1 | bytes 1 | tf_op jit(solution)/shard_map/place_core/pallas_call | solution.py:56
  56.9 0.0 collective-permute-done.2.refs_2_.refs_7_
  56.9 3.2 %mixed_part.1.refs_8_ = bf16[4,128,2048]{2,1,0:T(8,128)(2,1)} custom-call(s32[5]{0:T(128)S(1)} %stack.23.refs_0_.at_ref, bf16[1024,256]{1,0:T(8,128)(2,1)S(1)} %get-tuple-element.23.refs_1_.refs_6_.o_ref, bf16[512,256]{1,0:T(8,128)(2,1)S(1)} %collective-permute-done.2.refs_2_.refs_7_, bf16[2048,512]{1,0:T(8,128)(2,1)S(1)} %bitcast.21), custom_call_target="tpu_custom_call" | custom-call | flops 1 | bytes 1 | tf_op jit(solution)/shard_map/mixed_part/pallas_call | solution.py:56
  60.1 4.4 %all-to-all-start.2 = ((bf16[4,128,2048]{2,1,0:T(8,128)(2,1)}), bf16[4,128,2048]{2,1,0:T(8,128)(2,1)}, u32[]{:S(2)}, u32[]{:S(2)}) async-start(bf16[4,128,2048]{2,1,0:T(8,128)(2,1)} %mixed_part.1.refs_8_), calls=%async_computation.2 | async-start | bytes 4194304 | tf_op jit(solution)/shard_map/all_to_all | solution.py:438
  64.5 0.0 collective-permute-done.7.refs_4_
  64.5 0.0 collective-permute-done.8.refs_5_
  64.6 0.0 copy-start.6
  64.6 1.0 copy-done.6
  65.6 2.8 %weight_grad.1 = (bf16[4,2,128,512]{3,2,1,0:T(8,128)(2,1)S(1)}, bf16[4,2,128,512]{3,2,1,0:T(8,128)(2,1)S(1)}) custom-call(s32[5]{0:T(128)S(1)} %stack.23.refs_0_.at_ref, bf16[128,2048]{1,0:T(8,128)(2,1)S(1)} %bitcast.30, bf16[128,2048]{1,0:T(8,128)(2,1)S(1)} %copy-done.1, bf16[128,2048]{1,0:T(8,128)(2,1)} %collective-permute-done.1.refs_3_.refs_1_, ...), custom_call_target="tpu_custom_call" | custom-call | flops 1 | bytes 1 | tf_op jit(solution)/shard_map/weight_grad/pallas_call | solution.py:56
  68.4 0.1 collective-permute-start.9
  68.5 2.5 %head_cot.1 = (bf16[512,256]{1,0:T(8,128)(2,1)S(1)}, bf16[512,256]{1,0:T(8,128)(2,1)S(1)}) custom-call(s32[5]{0:T(128)S(1)} %stack.23.refs_0_.at_ref, bf16[128,2048]{1,0:T(8,128)(2,1)S(1)} %bitcast.31, bf16[128,2048]{1,0:T(8,128)(2,1)S(1)} %copy-done.1, bf16[128,2048]{1,0:T(8,128)(2,1)} %collective-permute-done.1.refs_3_.refs_1_, ...), custom_call_target="tpu_custom_call" | custom-call | flops 1 | bytes 1 | tf_op jit(solution)/shard_map/head_cot/pallas_call | solution.py:56
  71.0 1.1 collective-permute-start.13
  72.1 0.0 collective-permute-done.9.refs_2_
  72.1 0.8 add_core.1
  72.9 2.0 %collective-permute-start.10 = (bf16[2,128,512]{2,1,0:T(8,128)(2,1)S(1)}, bf16[2,128,512]{2,1,0:T(8,128)(2,1)S(1)}, u32[]{:S(2)}, u32[]{:S(2)}) collective-permute-start(bf16[2,128,512]{2,1,0:T(8,128)(2,1)S(1)} %get-tuple-element.30), channel_id=1, source_target_pairs={{0,32},{32,64},{64,96},{96,0},{1,33},{33,65},{65,97},{97,1},{2,34}... | collective-permute-start | bytes 786440 | tf_op jit(solution)/shard_map/ppermute | solution.py:282
  74.9 3.6 %collective-permute-start.11 = (bf16[2,128,512]{2,1,0:T(8,128)(2,1)S(1)}, bf16[2,128,512]{2,1,0:T(8,128)(2,1)S(1)}, u32[]{:S(2)}, u32[]{:S(2)}) collective-permute-start(bf16[2,128,512]{2,1,0:T(8,128)(2,1)S(1)} %get-tuple-element.31), channel_id=1, source_target_pairs={{0,64},{32,96},{64,0},{96,32},{1,65},{33,97},{65,1},{97,33},{2,66}... | collective-permute-start | bytes 786440 | tf_op jit(solution)/shard_map/ppermute | solution.py:282
  78.5 1.0 collective-permute-start.12
  79.5 0.3 collective-permute-done.13.recv_ref
  79.8 6.5 %attention_backward.1.refs_5_.refs_2_ = bf16[8,384,256]{2,1,0:T(8,128)(2,1)S(1)} custom-call(s32[5]{0:T(128)S(1)} %stack.23.refs_0_.at_ref, bf16[8,384,256]{2,1,0:T(8,128)(2,1)S(1)} %copy-done.3, f32[2,16,1024]{2,1,0:T(8,128)S(1)} %reshape.86.bias_ref, f32[2,1,1024]{2,1,0:T(1,128)S(1)} %get-tuple-element.24.refs_2_.stat_ref, ...), custom_call_target="tpu_custom_call" | custom-call | flops 1 | bytes 1 | tf_op jit(solution)/shard_map/attention_backward/pallas_call | solution.py:384
  86.3 0.0 collective-permute-done.10.refs_2_
  86.3 4.2 %collective-permute-done.11.refs_3_ = bf16[2,128,512]{2,1,0:T(8,128)(2,1)S(1)} collective-permute-done((bf16[2,128,512]{2,1,0:T(8,128)(2,1)S(1)}, bf16[2,128,512]{2,1,0:T(8,128)(2,1)S(1)}, u32[]{:S(2)}, u32[]{:S(2)}) %collective-permute-start.11) | collective-permute-done | bytes 262176 | tf_op jit(solution)/shard_map/ppermute | solution.py:282
  90.5 0.0 collective-permute-done.12.refs_4_
  90.5 0.7 add_z.1
  91.2 2.8 %collective-permute-start.14 = (bf16[128,512]{1,0:T(8,128)(2,1)S(1)}, bf16[128,512]{1,0:T(8,128)(2,1)S(1)}, u32[]{:S(2)}, u32[]{:S(2)}) collective-permute-start(bf16[128,512]{1,0:T(8,128)(2,1)S(1)} %get-tuple-element.36), channel_id=1, source_target_pairs={{0,16},{16,0},{1,17},{17,1},{2,18},{18,2},{3,19},{19,3},{4,20},{20... | collective-permute-start | bytes 393224 | tf_op jit(solution)/shard_map/ppermute | solution.py:86
  94.0 3.7 %collective-permute-done.14.refs_1_ = bf16[128,512]{1,0:T(8,128)(2,1)S(1)} collective-permute-done((bf16[128,512]{1,0:T(8,128)(2,1)S(1)}, bf16[128,512]{1,0:T(8,128)(2,1)S(1)}, u32[]{:S(2)}, u32[]{:S(2)}) %collective-permute-start.14) | collective-permute-done | bytes 131104 | tf_op jit(solution)/shard_map/ppermute | solution.py:86
  97.7 1.3 %attach.1 = bf16[8,416,256]{2,1,0:T(8,128)(2,1)} custom-call(f32[128,512]{1,0:T(8,128)S(1)} %get-tuple-element.35.refs_0_, bf16[128,512]{1,0:T(8,128)(2,1)S(1)} %collective-permute-done.14.refs_1_, bf16[8,384,256]{2,1,0:T(8,128)(2,1)S(1)} %attention_backward.1.refs_5_.refs_2_), custom_call_target="tpu_custom_call" | custom-call | flops 1 | bytes 1 | tf_op jit(solution)/shard_map/attach/pallas_call | solution.py:56
  99.1 0.0 all-to-all-done.2.refs_0_
  99.1 5.2 %all-to-all-start.3 = ((bf16[8,416,256]{2,1,0:T(8,128)(2,1)}), bf16[8,416,256]{2,1,0:T(8,128)(2,1)S(1)}, u32[]{:S(2)}, u32[]{:S(2)}) async-start(bf16[8,416,256]{2,1,0:T(8,128)(2,1)} %attach.1), calls=%async_computation.3 | async-start | bytes 3407872 | tf_op jit(solution)/shard_map/all_to_all | solution.py:443
  104.2 2.6 %finish_mixed.1 = bf16[128,2048]{1,0:T(8,128)(2,1)} custom-call(bf16[4,128,2048]{2,1,0:T(8,128)(2,1)} %all-to-all-done.2.refs_0_), custom_call_target="tpu_custom_call" | custom-call | flops 1 | bytes 1 | tf_op jit(solution)/shard_map/finish_mixed/pallas_call | solution.py:56
  106.9 17.6 %all-to-all-done.3.refs_0_ = bf16[8,416,256]{2,1,0:T(8,128)(2,1)S(1)} async-done(((bf16[8,416,256]{2,1,0:T(8,128)(2,1)}), bf16[8,416,256]{2,1,0:T(8,128)(2,1)S(1)}, u32[]{:S(2)}, u32[]{:S(2)}) %all-to-all-start.3) | async-done | bytes 1703968 | tf_op jit(solution)/shard_map/all_to_all | solution.py:443
  124.5 1.4 %unpack_heads.1 = (bf16[128,2048]{1,0:T(8,128)(2,1)}, bf16[128,2048]{1,0:T(8,128)(2,1)}, bf16[128,2048]{1,0:T(8,128)(2,1)}, f32[16,2048]{1,0:T(8,128)}) custom-call(bf16[8,416,256]{2,1,0:T(8,128)(2,1)S(1)} %all-to-all-done.3.refs_0_), custom_call_target="tpu_custom_call" | custom-call | flops 1 | bytes 1 | tf_op jit(solution)/shard_map/unpack_heads/pallas_call | solution.py:56
  (19 shorter events, 0.1 us)
Async XLA Ops:
  0.6 19.3 %collective-permute-start = (bf16[128,2048]{1,0:T(8,128)(2,1)}, bf16[128,2048]{1,0:T(8,128)(2,1)S(1)}, u32[]{:S(2)}, u32[]{:S(2)}) collective-permute-start(bf16[128,2048]{1,0:T(8,128)(2,1)} %bitcast.28), channel_id=1, source_target_pairs={{0,1},{1,2},{2,3},{3,0},{4,5},{5,6},{6,7},{7,4},{8,9},{9,10},{10,1... | collective-permute-start | bytes 1572872 | tf_op jit(solution)/shard_map/ppermute | solution.py:151
  2.4 17.6 %collective-permute-start.1 = (bf16[128,2048]{1,0:T(8,128)(2,1)}, bf16[128,2048]{1,0:T(8,128)(2,1)}, u32[]{:S(2)}, u32[]{:S(2)}) collective-permute-start(bf16[128,2048]{1,0:T(8,128)(2,1)} %bitcast.29), channel_id=1, source_target_pairs={{0,3},{1,0},{2,1},{3,2},{4,7},{5,4},{6,5},{7,6},{8,11},{9,8},{10,9... | collective-permute-start | bytes 1572872 | tf_op jit(solution)/shard_map/ppermute | solution.py:151
  3.9 0.8 copy-start.7
  5.5 14.4 %all-to-all-start = ((bf16[16,16,512]{2,1,0:T(8,128)(2,1)}), bf16[16,16,512]{2,1,0:T(8,128)(2,1)S(1)}, u32[]{:S(2)}, u32[]{:S(2)}) async-start(bf16[16,16,512]{2,1,0:T(8,128)(2,1)} %weight_blocks.1), calls=%async_computation | async-start | bytes 524288 | tf_op jit(solution)/shard_map/all_to_all | solution.py:143
  19.9 0.7 copy-start.4
  19.9 0.9 copy-start
  20.8 4.2 %copy-start.8 = (s32[1,2,16,3]{2,1,3,0:T(2,128)S(1)}, s32[1,2,16,3]{2,1,3,0:T(2,128)}, u32[]{:S(2)}) copy-start(s32[1,2,16,3]{2,1,3,0:T(2,128)} %param.12) | copy-start | bytes 1156
  20.8 4.2 %copy-start.9 = (s32[1,2]{1,0:T(1,128)S(1)}, s32[1,2]{1,0:T(1,128)}, u32[]{:S(2)}) copy-start(s32[1,2]{1,0:T(1,128)} %param.13) | copy-start | bytes 28
  20.8 4.4 %copy-start.5 = (bf16[16,16,512]{2,1,0:T(8,128)(2,1)S(1)}, bf16[16,16,512]{2,1,0:T(8,128)(2,1)}, u32[]{:S(2)}) copy-start(bf16[16,16,512]{2,1,0:T(8,128)(2,1)} %copy-done.4) | copy-start | bytes 786436
  20.8 23.5 %all-to-all-start.1 = ((bf16[8,384,256]{2,1,0:T(8,128)(2,1)}), bf16[8,384,256]{2,1,0:T(8,128)(2,1)S(1)}, u32[]{:S(2)}, u32[]{:S(2)}) async-start(bf16[8,384,256]{2,1,0:T(8,128)(2,1)} %hold.1), calls=%async_computation.1 | async-start | bytes 3145728 | tf_op jit(solution)/shard_map/all_to_all | solution.py:429
  25.2 10.4 %collective-permute-start.3 = (bf16[2,128,512]{2,1,0:T(8,128)(2,1)S(1)}, bf16[2,128,512]{2,1,0:T(8,128)(2,1)S(1)}, u32[]{:S(2)}, u32[]{:S(2)}) collective-permute-start(bf16[2,128,512]{2,1,0:T(8,128)(2,1)S(1)} %bitcast.24), channel_id=1, source_target_pairs={{0,32},{32,64},{64,96},{96,0},{1,33},{33,65},{65,97},{97,1},{2,34}... | collective-permute-start | bytes 786440 | tf_op jit(solution)/shard_map/ppermute | solution.py:144
  27.1 13.8 %collective-permute-start.4 = (bf16[2,128,512]{2,1,0:T(8,128)(2,1)S(1)}, bf16[2,128,512]{2,1,0:T(8,128)(2,1)S(1)}, u32[]{:S(2)}, u32[]{:S(2)}) collective-permute-start(bf16[2,128,512]{2,1,0:T(8,128)(2,1)S(1)} %bitcast.25), channel_id=1, source_target_pairs={{0,64},{32,96},{64,0},{96,32},{1,65},{33,97},{65,1},{97,33},{2,66}... | collective-permute-start | bytes 786440 | tf_op jit(solution)/shard_map/ppermute | solution.py:144
  30.7 10.3 %collective-permute-start.5 = (bf16[2,128,512]{2,1,0:T(8,128)(2,1)S(1)}, bf16[2,128,512]{2,1,0:T(8,128)(2,1)S(1)}, u32[]{:S(2)}, u32[]{:S(2)}) collective-permute-start(bf16[2,128,512]{2,1,0:T(8,128)(2,1)S(1)} %bitcast.26), channel_id=1, source_target_pairs={{0,96},{32,0},{64,32},{96,64},{1,97},{33,1},{65,33},{97,65},{2,98}... | collective-permute-start | bytes 786440 | tf_op jit(solution)/shard_map/ppermute | solution.py:144
  42.6 7.6 %copy-start.1 = (bf16[128,2048]{1,0:T(8,128)(2,1)S(1)}, bf16[128,2048]{1,0:T(8,128)(2,1)}, u32[]{:S(2)}) copy-start(bf16[128,2048]{1,0:T(8,128)(2,1)} %copy-done) | copy-start | bytes 1572868
  42.6 12.6 %collective-permute-start.6 = (bf16[4,2,128,512]{3,2,1,0:T(8,128)(2,1)}, bf16[4,2,128,512]{3,2,1,0:T(8,128)(2,1)}, u32[]{:S(2)}, u32[]{:S(2)}) collective-permute-start(bf16[4,2,128,512]{3,2,1,0:T(8,128)(2,1)} %place_z.1.refs_1_), channel_id=1, source_target_pairs={{0,8},{8,0},{1,9},{9,1},{2,10},{10,2},{3,11},{11,3},{4,12},{12,4},... | collective-permute-start | bytes 3145736 | tf_op jit(solution)/shard_map/ppermute | solution.py:86
  44.3 4.2 %copy-start.2 = (bf16[8,384,256]{2,1,0:T(8,128)(2,1)}, bf16[8,384,256]{2,1,0:T(8,128)(2,1)S(1)}, u32[]{:S(2)}) copy-start(bf16[8,384,256]{2,1,0:T(8,128)(2,1)S(1)} %all-to-all-done.1.qkv_ref) | copy-start | bytes 4718596
  48.6 8.3 %collective-permute-start.2 = (bf16[512,256]{1,0:T(8,128)(2,1)S(1)}, bf16[512,256]{1,0:T(8,128)(2,1)S(1)}, u32[]{:S(2)}, u32[]{:S(2)}) collective-permute-start(bf16[512,256]{1,0:T(8,128)(2,1)S(1)} %constant_dynamic-slice_fusion), channel_id=1, source_target_pairs={{0,4},{4,0},{1,5},{5,1},{2,6},{6,2},{3,7},{7,3},{8,12},{12,8},{9,1... | collective-permute-start | bytes 786440 | tf_op jit(solution)/shard_map/ppermute | solution.py:86
  52.0 12.6 %collective-permute-start.7 = (bf16[64,2048]{1,0:T(8,128)(2,1)}, bf16[64,2048]{1,0:T(8,128)(2,1)}, u32[]{:S(2)}, u32[]{:S(2)}) collective-permute-start(bf16[64,2048]{1,0:T(8,128)(2,1)} %get-tuple-element.25), channel_id=1, source_target_pairs={{0,1},{1,2},{2,3},{3,0},{4,5},{5,6},{6,7},{7,4},{8,9},{9,10},{10,1... | collective-permute-start | bytes 786440 | tf_op jit(solution)/shard_map/ppermute | solution.py:162
  52.8 11.7 %collective-permute-start.8 = (bf16[64,2048]{1,0:T(8,128)(2,1)}, bf16[64,2048]{1,0:T(8,128)(2,1)}, u32[]{:S(2)}, u32[]{:S(2)}) collective-permute-start(bf16[64,2048]{1,0:T(8,128)(2,1)} %get-tuple-element.26), channel_id=1, source_target_pairs={{0,3},{1,0},{2,1},{3,2},{4,7},{5,4},{6,5},{7,6},{8,11},{9,8},{10,9... | collective-permute-start | bytes 786440 | tf_op jit(solution)/shard_map/ppermute | solution.py:162
  60.1 39.0 %all-to-all-start.2 = ((bf16[4,128,2048]{2,1,0:T(8,128)(2,1)}), bf16[4,128,2048]{2,1,0:T(8,128)(2,1)}, u32[]{:S(2)}, u32[]{:S(2)}) async-start(bf16[4,128,2048]{2,1,0:T(8,128)(2,1)} %mixed_part.1.refs_8_), calls=%async_computation.2 | async-start | bytes 4194304 | tf_op jit(solution)/shard_map/all_to_all | solution.py:438
  64.6 1.0 copy-start.6
  68.4 3.7 %collective-permute-start.9 = (bf16[4,2,128,512]{3,2,1,0:T(8,128)(2,1)S(1)}, bf16[4,2,128,512]{3,2,1,0:T(8,128)(2,1)S(1)}, u32[]{:S(2)}, u32[]{:S(2)}) collective-permute-start(bf16[4,2,128,512]{3,2,1,0:T(8,128)(2,1)S(1)} %get-tuple-element.28.refs_7_), channel_id=1, source_target_pairs={{0,8},{8,0},{1,9},{9,1},{2,10},{10,2},{3,11},{11,3},{4,12},{12,4},... | collective-permute-start | bytes 3145736 | tf_op jit(solution)/shard_map/ppermute | solution.py:86
  71.0 8.8 %copy-start.3 = (bf16[8,384,256]{2,1,0:T(8,128)(2,1)S(1)}, bf16[8,384,256]{2,1,0:T(8,128)(2,1)}, u32[]{:S(2)}) copy-start(bf16[8,384,256]{2,1,0:T(8,128)(2,1)} %copy-done.2) | copy-start | bytes 4718596
  71.0 8.8 %collective-permute-start.13 = (bf16[512,256]{1,0:T(8,128)(2,1)S(1)}, bf16[512,256]{1,0:T(8,128)(2,1)S(1)}, u32[]{:S(2)}, u32[]{:S(2)}) collective-permute-start(bf16[512,256]{1,0:T(8,128)(2,1)S(1)} %get-tuple-element.34), channel_id=1, source_target_pairs={{0,4},{4,0},{1,5},{5,1},{2,6},{6,2},{3,7},{7,3},{8,12},{12,8},{9,1... | collective-permute-start | bytes 786440 | tf_op jit(solution)/shard_map/ppermute | solution.py:86
  72.9 13.4 %collective-permute-start.10 = (bf16[2,128,512]{2,1,0:T(8,128)(2,1)S(1)}, bf16[2,128,512]{2,1,0:T(8,128)(2,1)S(1)}, u32[]{:S(2)}, u32[]{:S(2)}) collective-permute-start(bf16[2,128,512]{2,1,0:T(8,128)(2,1)S(1)} %get-tuple-element.30), channel_id=1, source_target_pairs={{0,32},{32,64},{64,96},{96,0},{1,33},{33,65},{65,97},{97,1},{2,34}... | collective-permute-start | bytes 786440 | tf_op jit(solution)/shard_map/ppermute | solution.py:282
  74.9 15.6 %collective-permute-start.11 = (bf16[2,128,512]{2,1,0:T(8,128)(2,1)S(1)}, bf16[2,128,512]{2,1,0:T(8,128)(2,1)S(1)}, u32[]{:S(2)}, u32[]{:S(2)}) collective-permute-start(bf16[2,128,512]{2,1,0:T(8,128)(2,1)S(1)} %get-tuple-element.31), channel_id=1, source_target_pairs={{0,64},{32,96},{64,0},{96,32},{1,65},{33,97},{65,1},{97,33},{2,66}... | collective-permute-start | bytes 786440 | tf_op jit(solution)/shard_map/ppermute | solution.py:282
  78.5 12.0 %collective-permute-start.12 = (bf16[2,128,512]{2,1,0:T(8,128)(2,1)S(1)}, bf16[2,128,512]{2,1,0:T(8,128)(2,1)S(1)}, u32[]{:S(2)}, u32[]{:S(2)}) collective-permute-start(bf16[2,128,512]{2,1,0:T(8,128)(2,1)S(1)} %get-tuple-element.32.refs_0_), channel_id=1, source_target_pairs={{0,96},{32,0},{64,32},{96,64},{1,97},{33,1},{65,33},{97,65},{2,98}... | collective-permute-start | bytes 786440 | tf_op jit(solution)/shard_map/ppermute | solution.py:282
  91.2 6.6 %collective-permute-start.14 = (bf16[128,512]{1,0:T(8,128)(2,1)S(1)}, bf16[128,512]{1,0:T(8,128)(2,1)S(1)}, u32[]{:S(2)}, u32[]{:S(2)}) collective-permute-start(bf16[128,512]{1,0:T(8,128)(2,1)S(1)} %get-tuple-element.36), channel_id=1, source_target_pairs={{0,16},{16,0},{1,17},{17,1},{2,18},{18,2},{3,19},{19,3},{4,20},{20... | collective-permute-start | bytes 393224 | tf_op jit(solution)/shard_map/ppermute | solution.py:86
  99.1 25.4 %all-to-all-start.3 = ((bf16[8,416,256]{2,1,0:T(8,128)(2,1)}), bf16[8,416,256]{2,1,0:T(8,128)(2,1)S(1)}, u32[]{:S(2)}, u32[]{:S(2)}) async-start(bf16[8,416,256]{2,1,0:T(8,128)(2,1)} %attach.1), calls=%async_computation.3 | async-start | bytes 3407872 | tf_op jit(solution)/shard_map/all_to_all | solution.py:443

commit v6 on v5

--- a/solution.py
+++ b/solution.py
@@ -21,6 +21,7 @@
 MASKED = -1e30
 CTX = ("xl", "y")
 DP = ("z", "xh", "core")
+Z_STEPS = (2, 1, 3)
 BF = jnp.bfloat16
 F32 = jnp.float32
 NT = (((1,), (1,)), ((), ()))
@@ -232,7 +233,7 @@
 def add_core_kernel(at_ref, keep_ref, recv_ref, out_ref, *send_refs):
     z = at_ref[0]
     out_ref[...] = keep_ref[z].astype(F32) + recv_ref[z].astype(F32)
-    for step, ref in enumerate(send_refs, 1):
+    for step, ref in zip(Z_STEPS, send_refs):
         to = lax.rem(z + step, 4)
         ref[...] = (keep_ref[to].astype(F32) + recv_ref[to].astype(F32)).astype(BF)
 
@@ -279,7 +280,7 @@
     keep, *sends = whole(
         add_core_kernel, "add_core", ((two[0], F32), two, two, two), at, keep, swap(send, "core"), scalars=1
     )
-    return keep, [lax.ppermute(send, "z", ring(4, step)) for step, send in enumerate(sends, 1)], sends[-1], first
+    return keep, [lax.ppermute(send, "z", ring(4, step)) for step, send in zip(Z_STEPS, sends)], sends[-1], first
 
 
 def sum_z(at, keep, got, after):

time: 127 us -> 126 us (level)
  no operation moved by 1% of the time
where the time goes in v6:
time: 126 us; the launch traced here: 125 us
  starting transfers between devices  45.5 us (36%)
  waiting for transfers between devices  41.1 us (33%)
  Pallas kernels  34.4 us (27%)
  local copies, waits for them, and re-layouts  3.13 us (2%)
    pallas_call x12, Pallas kernels, whole(): pl.pallas_call(ordered, in_specs=[SMEM] * scalars + [VMEM] * (len(args) -...  21.1 us
    all_to_all x1, waiting for transfers between devices, on_device(): grads = lax.all_to_all(grads, CTX, 0, 0, tiled=True)  17.6 us
    ppermute x3, waiting for transfers between devices, gather_weight(): far = [lax.ppermute(rows, 'z', ring(4, step)) for step in (1, 2, 3)]  8.85 us
    ppermute x3, starting transfers between devices, weight_grad(): lax.ppermute(send, 'z', ring(4, step))  7.2 us
    pallas_call x1, Pallas kernels, backward(): pl.pallas_call(backward_kernel, grid=(2,), in_specs=[SMEM, heads, pl.Bloc...  6.55 us
    ppermute x3, starting transfers between devices, gather_weight(): far = [lax.ppermute(rows, 'z', ring(4, step)) for step in (1, 2, 3)]  6.52 us
    all_to_all x1, waiting for transfers between devices, gather_weight(): lax.all_to_all(blocks, ('xh',) + CTX, 0, 0, tiled=True).reshape(2, 128, 512)  5.91 us
    all_to_all x1, starting transfers between devices, gather_weight(): lax.all_to_all(blocks, ('xh',) + CTX, 0, 0, tiled=True).reshape(2, 128, 512)  5.91 us
  transfers between devices with their start and end apart: 19, of which 8 were waited for; matrix products, arithmetic and copies ran while one was open for 0% of the time, Pallas kernels for 26%

profile of v6, /device:TPU:0, one launch (start us, length us, event | category | flops | bytes accessed | tf_op | source)
XLA Modules:
  0.0 125.3 jit_solution(5886484026828445920)
XLA Ops:
  0.6 1.7 %collective-permute-start = (bf16[128,2048]{1,0:T(8,128)(2,1)}, bf16[128,2048]{1,0:T(8,128)(2,1)S(1)}, u32[]{:S(2)}, u32[]{:S(2)}) collective-permute-start(bf16[128,2048]{1,0:T(8,128)(2,1)} %bitcast.28), channel_id=1, source_target_pairs={{0,1},{1,2},{2,3},{3,0},{4,5},{5,6},{6,7},{7,4},{8,9},{9,10},{10,1... | collective-permute-start | bytes 1572872 | tf_op jit(solution)/shard_map/ppermute | solution.py:152
  2.4 1.6 %collective-permute-start.1 = (bf16[128,2048]{1,0:T(8,128)(2,1)}, bf16[128,2048]{1,0:T(8,128)(2,1)}, u32[]{:S(2)}, u32[]{:S(2)}) collective-permute-start(bf16[128,2048]{1,0:T(8,128)(2,1)} %bitcast.29), channel_id=1, source_target_pairs={{0,3},{1,0},{2,1},{3,2},{4,7},{5,4},{6,5},{7,6},{8,11},{9,8},{10,9... | collective-permute-start | bytes 1572872 | tf_op jit(solution)/shard_map/ppermute | solution.py:152
  3.9 0.8 copy-done.7
  4.8 0.7 weight_blocks.1
  5.5 5.9 %all-to-all-start = ((bf16[16,16,512]{2,1,0:T(8,128)(2,1)}), bf16[16,16,512]{2,1,0:T(8,128)(2,1)S(1)}, u32[]{:S(2)}, u32[]{:S(2)}) async-start(bf16[16,16,512]{2,1,0:T(8,128)(2,1)} %weight_blocks.1), calls=%async_computation | async-start | bytes 524288 | tf_op jit(solution)/shard_map/all_to_all | solution.py:144
  11.4 2.6 %pack_heads.1.refs_0_ = bf16[8,384,256]{2,1,0:T(8,128)(2,1)} custom-call(bf16[128,2048]{1,0:T(8,128)(2,1)} %bitcast.33, bf16[128,2048]{1,0:T(8,128)(2,1)} %bitcast.34, bf16[128,2048]{1,0:T(8,128)(2,1)} %bitcast.35), custom_call_target="tpu_custom_call" | custom-call | flops 1 | bytes 1 | tf_op jit(solution)/shard_map/pack_heads/pallas_call | solution.py:107
  14.0 5.9 %all-to-all-done = bf16[16,16,512]{2,1,0:T(8,128)(2,1)S(1)} async-done(((bf16[16,16,512]{2,1,0:T(8,128)(2,1)}), bf16[16,16,512]{2,1,0:T(8,128)(2,1)S(1)}, u32[]{:S(2)}, u32[]{:S(2)}) %all-to-all-start) | async-done | bytes 262176 | tf_op jit(solution)/shard_map/all_to_all | solution.py:144
  19.9 0.0 collective-permute-done.refs_2_.refs_0_
  19.9 0.0 collective-permute-done.1.refs_3_.refs_1_
  19.9 0.7 copy-done.4
  20.6 0.2 copy-done
  20.8 4.2 %all-to-all-start.1 = ((bf16[8,384,256]{2,1,0:T(8,128)(2,1)}), bf16[8,384,256]{2,1,0:T(8,128)(2,1)S(1)}, u32[]{:S(2)}, u32[]{:S(2)}) async-start(bf16[8,384,256]{2,1,0:T(8,128)(2,1)} %hold.1), calls=%async_computation.1 | async-start | bytes 3145728 | tf_op jit(solution)/shard_map/all_to_all | solution.py:430
  25.0 0.0 copy-done.9
  25.0 0.1 compare_reduce_fusion
  25.1 0.1 fusion.1
  25.2 1.9 %collective-permute-start.3 = (bf16[2,128,512]{2,1,0:T(8,128)(2,1)S(1)}, bf16[2,128,512]{2,1,0:T(8,128)(2,1)S(1)}, u32[]{:S(2)}, u32[]{:S(2)}) collective-permute-start(bf16[2,128,512]{2,1,0:T(8,128)(2,1)S(1)} %bitcast.24), channel_id=1, source_target_pairs={{0,32},{32,64},{64,96},{96,0},{1,33},{33,65},{65,97},{97,1},{2,34}... | collective-permute-start | bytes 786440 | tf_op jit(solution)/shard_map/ppermute | solution.py:145
  27.1 3.6 %collective-permute-start.4 = (bf16[2,128,512]{2,1,0:T(8,128)(2,1)S(1)}, bf16[2,128,512]{2,1,0:T(8,128)(2,1)S(1)}, u32[]{:S(2)}, u32[]{:S(2)}) collective-permute-start(bf16[2,128,512]{2,1,0:T(8,128)(2,1)S(1)} %bitcast.25), channel_id=1, source_target_pairs={{0,64},{32,96},{64,0},{96,32},{1,65},{33,97},{65,1},{97,33},{2,66}... | collective-permute-start | bytes 786440 | tf_op jit(solution)/shard_map/ppermute | solution.py:145
  30.7 1.0 collective-permute-start.5
  31.8 0.1 broadcast_in_dim.29
  31.9 0.1 reshape.86.bias_ref
  32.0 0.1 stack.23.refs_0_.at_ref
  32.1 3.5 %collective-permute-done.3.refs_2_ = bf16[2,128,512]{2,1,0:T(8,128)(2,1)S(1)} collective-permute-done((bf16[2,128,512]{2,1,0:T(8,128)(2,1)S(1)}, bf16[2,128,512]{2,1,0:T(8,128)(2,1)S(1)}, u32[]{:S(2)}, u32[]{:S(2)}) %collective-permute-start.3) | collective-permute-done | bytes 262176 | tf_op jit(solution)/shard_map/ppermute | solution.py:145
  35.6 5.4 %collective-permute-done.4.refs_3_ = bf16[2,128,512]{2,1,0:T(8,128)(2,1)S(1)} collective-permute-done((bf16[2,128,512]{2,1,0:T(8,128)(2,1)S(1)}, bf16[2,128,512]{2,1,0:T(8,128)(2,1)S(1)}, u32[]{:S(2)}, u32[]{:S(2)}) %collective-permute-start.4) | collective-permute-done | bytes 262176 | tf_op jit(solution)/shard_map/ppermute | solution.py:145
  41.0 0.0 collective-permute-done.5.refs_4_
  41.0 1.6 %place_z.1.refs_1_ = bf16[4,2,128,512]{3,2,1,0:T(8,128)(2,1)} custom-call(s32[5]{0:T(128)S(1)} %stack.23.refs_0_.at_ref, bf16[2,128,512]{2,1,0:T(8,128)(2,1)S(1)} %bitcast.27, bf16[2,128,512]{2,1,0:T(8,128)(2,1)S(1)} %collective-permute-done.3.refs_2_, bf16[2,128,512]{2,1,0:T(8,128)(2,1)S(1)} %collective-permute-done.4.refs_3_, ...), custom_call_target="tpu_custom_call" | custom-call | flops 1 | bytes 1 | tf_op jit(solution)/shard_map/place_z/pallas_call | solution.py:57
  42.6 0.0 collective-permute-start.6
  42.6 1.7 %all-to-all-done.1.qkv_ref = bf16[8,384,256]{2,1,0:T(8,128)(2,1)S(1)} async-done(((bf16[8,384,256]{2,1,0:T(8,128)(2,1)}), bf16[8,384,256]{2,1,0:T(8,128)(2,1)S(1)}, u32[]{:S(2)}, u32[]{:S(2)}) %all-to-all-start.1) | async-done | bytes 1572896 | tf_op jit(solution)/shard_map/all_to_all | solution.py:430
  44.3 4.2 %attention_forward.1 = (bf16[1024,256]{1,0:T(8,128)(2,1)S(1)}, f32[2,1,1024]{2,1,0:T(1,128)S(1)}) custom-call(bf16[8,384,256]{2,1,0:T(8,128)(2,1)S(1)} %all-to-all-done.1.qkv_ref, f32[2,16,1024]{2,1,0:T(8,128)S(1)} %reshape.86.bias_ref), custom_call_target="tpu_custom_call" | custom-call | flops 8999999488 | bytes 1 | tf_op jit(solution)/shard_map/attention_forward/pallas_call | solution.py:329
  48.6 1.5 %collective-permute-start.2 = (bf16[512,256]{1,0:T(8,128)(2,1)S(1)}, bf16[512,256]{1,0:T(8,128)(2,1)S(1)}, u32[]{:S(2)}, u32[]{:S(2)}) collective-permute-start(bf16[512,256]{1,0:T(8,128)(2,1)S(1)} %constant_dynamic-slice_fusion), channel_id=1, source_target_pairs={{0,4},{4,0},{1,5},{5,1},{2,6},{6,2},{3,7},{7,3},{8,12},{12,8},{9,1... | collective-permute-start | bytes 786440 | tf_op jit(solution)/shard_map/ppermute | solution.py:87
  50.1 1.8 %cot_relay.1 = (bf16[64,2048]{1,0:T(8,128)(2,1)}, bf16[64,2048]{1,0:T(8,128)(2,1)}) custom-call(bf16[128,2048]{1,0:T(8,128)(2,1)S(1)} %copy-done.1, bf16[128,2048]{1,0:T(8,128)(2,1)} %collective-permute-done.1.refs_3_.refs_1_, f32[2,1,1024]{2,1,0:T(1,128)S(1)} %get-tuple-element.24.refs_2_.stat_ref), custom_call_target="tpu_custom_call" | custom-call | flops 1 | bytes 1 | tf_op jit(solution)/shard_map/cot_relay/pallas_call | solution.py:57
  52.0 0.8 collective-permute-start.7
  52.8 2.4 %collective-permute-start.8 = (bf16[64,2048]{1,0:T(8,128)(2,1)}, bf16[64,2048]{1,0:T(8,128)(2,1)}, u32[]{:S(2)}, u32[]{:S(2)}) collective-permute-start(bf16[64,2048]{1,0:T(8,128)(2,1)} %get-tuple-element.26), channel_id=1, source_target_pairs={{0,3},{1,0},{2,1},{3,2},{4,7},{5,4},{6,5},{7,6},{8,11},{9,8},{10,9... | collective-permute-start | bytes 786440 | tf_op jit(solution)/shard_map/ppermute | solution.py:163
  55.2 0.0 collective-permute-done.6.refs_2_
  55.2 1.7 %place_core.1 = bf16[16,128,512]{2,1,0:T(8,128)(2,1)S(1)} custom-call(s32[5]{0:T(128)S(1)} %stack.23.refs_0_.at_ref, bf16[4,2,128,512]{3,2,1,0:T(8,128)(2,1)} %place_z.1.refs_1_, bf16[4,2,128,512]{3,2,1,0:T(8,128)(2,1)} %collective-permute-done.6.refs_2_), custom_call_target="tpu_custom_call" | custom-call | flops 1 | bytes 1 | tf_op jit(solution)/shard_map/place_core/pallas_call | solution.py:57
  56.9 0.0 collective-permute-done.2.refs_2_.refs_7_
  56.9 3.2 %mixed_part.1.refs_8_ = bf16[4,128,2048]{2,1,0:T(8,128)(2,1)} custom-call(s32[5]{0:T(128)S(1)} %stack.23.refs_0_.at_ref, bf16[1024,256]{1,0:T(8,128)(2,1)S(1)} %get-tuple-element.23.refs_1_.refs_6_.o_ref, bf16[512,256]{1,0:T(8,128)(2,1)S(1)} %collective-permute-done.2.refs_2_.refs_7_, bf16[2048,512]{1,0:T(8,128)(2,1)S(1)} %bitcast.21), custom_call_target="tpu_custom_call" | custom-call | flops 1 | bytes 1 | tf_op jit(solution)/shard_map/mixed_part/pallas_call | solution.py:57
  60.1 4.4 %all-to-all-start.2 = ((bf16[4,128,2048]{2,1,0:T(8,128)(2,1)}), bf16[4,128,2048]{2,1,0:T(8,128)(2,1)}, u32[]{:S(2)}, u32[]{:S(2)}) async-start(bf16[4,128,2048]{2,1,0:T(8,128)(2,1)} %mixed_part.1.refs_8_), calls=%async_computation.2 | async-start | bytes 4194304 | tf_op jit(solution)/shard_map/all_to_all | solution.py:439
  64.5 0.0 collective-permute-done.7.refs_4_
  64.5 0.0 collective-permute-done.8.refs_5_
  64.6 0.0 copy-start.6
  64.6 1.0 copy-done.6
  65.6 2.8 %weight_grad.1 = (bf16[4,2,128,512]{3,2,1,0:T(8,128)(2,1)S(1)}, bf16[4,2,128,512]{3,2,1,0:T(8,128)(2,1)S(1)}) custom-call(s32[5]{0:T(128)S(1)} %stack.23.refs_0_.at_ref, bf16[128,2048]{1,0:T(8,128)(2,1)S(1)} %bitcast.30, bf16[128,2048]{1,0:T(8,128)(2,1)S(1)} %copy-done.1, bf16[128,2048]{1,0:T(8,128)(2,1)} %collective-permute-done.1.refs_3_.refs_1_, ...), custom_call_target="tpu_custom_call" | custom-call | flops 1 | bytes 1 | tf_op jit(solution)/shard_map/weight_grad/pallas_call | solution.py:57
  68.4 0.1 collective-permute-start.9
  68.5 2.5 %head_cot.1 = (bf16[512,256]{1,0:T(8,128)(2,1)S(1)}, bf16[512,256]{1,0:T(8,128)(2,1)S(1)}) custom-call(s32[5]{0:T(128)S(1)} %stack.23.refs_0_.at_ref, bf16[128,2048]{1,0:T(8,128)(2,1)S(1)} %bitcast.31, bf16[128,2048]{1,0:T(8,128)(2,1)S(1)} %copy-done.1, bf16[128,2048]{1,0:T(8,128)(2,1)} %collective-permute-done.1.refs_3_.refs_1_, ...), custom_call_target="tpu_custom_call" | custom-call | flops 1 | bytes 1 | tf_op jit(solution)/shard_map/head_cot/pallas_call | solution.py:57
  71.0 1.1 collective-permute-start.13
  72.1 0.0 collective-permute-done.9.refs_2_
  72.1 0.8 add_core.1
  72.9 4.0 %collective-permute-start.10 = (bf16[2,128,512]{2,1,0:T(8,128)(2,1)S(1)}, bf16[2,128,512]{2,1,0:T(8,128)(2,1)S(1)}, u32[]{:S(2)}, u32[]{:S(2)}) collective-permute-start(bf16[2,128,512]{2,1,0:T(8,128)(2,1)S(1)} %get-tuple-element.30), channel_id=1, source_target_pairs={{0,64},{32,96},{64,0},{96,32},{1,65},{33,97},{65,1},{97,33},{2,66}... | collective-permute-start | bytes 786440 | tf_op jit(solution)/shard_map/ppermute | solution.py:283
  76.9 1.0 collective-permute-start.11
  77.9 2.2 %collective-permute-start.12 = (bf16[2,128,512]{2,1,0:T(8,128)(2,1)S(1)}, bf16[2,128,512]{2,1,0:T(8,128)(2,1)S(1)}, u32[]{:S(2)}, u32[]{:S(2)}) collective-permute-start(bf16[2,128,512]{2,1,0:T(8,128)(2,1)S(1)} %get-tuple-element.32.refs_0_), channel_id=1, source_target_pairs={{0,96},{32,0},{64,32},{96,64},{1,97},{33,1},{65,33},{97,65},{2,98}... | collective-permute-start | bytes 786440 | tf_op jit(solution)/shard_map/ppermute | solution.py:283
  80.1 0.0 collective-permute-done.13.recv_ref
  80.1 6.5 %attention_backward.1.refs_5_.refs_2_ = bf16[8,384,256]{2,1,0:T(8,128)(2,1)S(1)} custom-call(s32[5]{0:T(128)S(1)} %stack.23.refs_0_.at_ref, bf16[8,384,256]{2,1,0:T(8,128)(2,1)S(1)} %copy-done.3, f32[2,16,1024]{2,1,0:T(8,128)S(1)} %reshape.86.bias_ref, f32[2,1,1024]{2,1,0:T(1,128)S(1)} %get-tuple-element.24.refs_2_.stat_ref, ...), custom_call_target="tpu_custom_call" | custom-call | flops 1 | bytes 1 | tf_op jit(solution)/shard_map/attention_backward/pallas_call | solution.py:385
  86.7 0.0 collective-permute-done.10.refs_2_
  86.7 2.5 %collective-permute-done.11.refs_3_ = bf16[2,128,512]{2,1,0:T(8,128)(2,1)S(1)} collective-permute-done((bf16[2,128,512]{2,1,0:T(8,128)(2,1)S(1)}, bf16[2,128,512]{2,1,0:T(8,128)(2,1)S(1)}, u32[]{:S(2)}, u32[]{:S(2)}) %collective-permute-start.11) | collective-permute-done | bytes 262176 | tf_op jit(solution)/shard_map/ppermute | solution.py:283
  89.2 0.8 collective-permute-done.12.refs_4_
  90.0 0.7 add_z.1
  90.6 2.8 %collective-permute-start.14 = (bf16[128,512]{1,0:T(8,128)(2,1)S(1)}, bf16[128,512]{1,0:T(8,128)(2,1)S(1)}, u32[]{:S(2)}, u32[]{:S(2)}) collective-permute-start(bf16[128,512]{1,0:T(8,128)(2,1)S(1)} %get-tuple-element.36), channel_id=1, source_target_pairs={{0,16},{16,0},{1,17},{17,1},{2,18},{18,2},{3,19},{19,3},{4,20},{20... | collective-permute-start | bytes 393224 | tf_op jit(solution)/shard_map/ppermute | solution.py:87
  93.4 3.7 %collective-permute-done.14.refs_1_ = bf16[128,512]{1,0:T(8,128)(2,1)S(1)} collective-permute-done((bf16[128,512]{1,0:T(8,128)(2,1)S(1)}, bf16[128,512]{1,0:T(8,128)(2,1)S(1)}, u32[]{:S(2)}, u32[]{:S(2)}) %collective-permute-start.14) | collective-permute-done | bytes 131104 | tf_op jit(solution)/shard_map/ppermute | solution.py:87
  97.2 1.3 %attach.1 = bf16[8,416,256]{2,1,0:T(8,128)(2,1)} custom-call(f32[128,512]{1,0:T(8,128)S(1)} %get-tuple-element.35.refs_0_, bf16[128,512]{1,0:T(8,128)(2,1)S(1)} %collective-permute-done.14.refs_1_, bf16[8,384,256]{2,1,0:T(8,128)(2,1)S(1)} %attention_backward.1.refs_5_.refs_2_), custom_call_target="tpu_custom_call" | custom-call | flops 1 | bytes 1 | tf_op jit(solution)/shard_map/attach/pallas_call | solution.py:57
  98.5 0.0 all-to-all-done.2.refs_0_
  98.5 5.2 %all-to-all-start.3 = ((bf16[8,416,256]{2,1,0:T(8,128)(2,1)}), bf16[8,416,256]{2,1,0:T(8,128)(2,1)S(1)}, u32[]{:S(2)}, u32[]{:S(2)}) async-start(bf16[8,416,256]{2,1,0:T(8,128)(2,1)} %attach.1), calls=%async_computation.3 | async-start | bytes 3407872 | tf_op jit(solution)/shard_map/all_to_all | solution.py:444
  103.7 2.6 %finish_mixed.1 = bf16[128,2048]{1,0:T(8,128)(2,1)} custom-call(bf16[4,128,2048]{2,1,0:T(8,128)(2,1)} %all-to-all-done.2.refs_0_), custom_call_target="tpu_custom_call" | custom-call | flops 1 | bytes 1 | tf_op jit(solution)/shard_map/finish_mixed/pallas_call | solution.py:57
  106.3 17.6 %all-to-all-done.3.refs_0_ = bf16[8,416,256]{2,1,0:T(8,128)(2,1)S(1)} async-done(((bf16[8,416,256]{2,1,0:T(8,128)(2,1)}), bf16[8,416,256]{2,1,0:T(8,128)(2,1)S(1)}, u32[]{:S(2)}, u32[]{:S(2)}) %all-to-all-start.3) | async-done | bytes 1703968 | tf_op jit(solution)/shard_map/all_to_all | solution.py:444
  123.9 1.4 %unpack_heads.1 = (bf16[128,2048]{1,0:T(8,128)(2,1)}, bf16[128,2048]{1,0:T(8,128)(2,1)}, bf16[128,2048]{1,0:T(8,128)(2,1)}, f32[16,2048]{1,0:T(8,128)}) custom-call(bf16[8,416,256]{2,1,0:T(8,128)(2,1)S(1)} %all-to-all-done.3.refs_0_), custom_call_target="tpu_custom_call" | custom-call | flops 1 | bytes 1 | tf_op jit(solution)/shard_map/unpack_heads/pallas_call | solution.py:57
  (19 shorter events, 0.1 us)
Async XLA Ops:
  0.6 19.3 %collective-permute-start = (bf16[128,2048]{1,0:T(8,128)(2,1)}, bf16[128,2048]{1,0:T(8,128)(2,1)S(1)}, u32[]{:S(2)}, u32[]{:S(2)}) collective-permute-start(bf16[128,2048]{1,0:T(8,128)(2,1)} %bitcast.28), channel_id=1, source_target_pairs={{0,1},{1,2},{2,3},{3,0},{4,5},{5,6},{6,7},{7,4},{8,9},{9,10},{10,1... | collective-permute-start | bytes 1572872 | tf_op jit(solution)/shard_map/ppermute | solution.py:152
  2.4 17.6 %collective-permute-start.1 = (bf16[128,2048]{1,0:T(8,128)(2,1)}, bf16[128,2048]{1,0:T(8,128)(2,1)}, u32[]{:S(2)}, u32[]{:S(2)}) collective-permute-start(bf16[128,2048]{1,0:T(8,128)(2,1)} %bitcast.29), channel_id=1, source_target_pairs={{0,3},{1,0},{2,1},{3,2},{4,7},{5,4},{6,5},{7,6},{8,11},{9,8},{10,9... | collective-permute-start | bytes 1572872 | tf_op jit(solution)/shard_map/ppermute | solution.py:152
  3.9 0.8 copy-start.7
  5.5 14.4 %all-to-all-start = ((bf16[16,16,512]{2,1,0:T(8,128)(2,1)}), bf16[16,16,512]{2,1,0:T(8,128)(2,1)S(1)}, u32[]{:S(2)}, u32[]{:S(2)}) async-start(bf16[16,16,512]{2,1,0:T(8,128)(2,1)} %weight_blocks.1), calls=%async_computation | async-start | bytes 524288 | tf_op jit(solution)/shard_map/all_to_all | solution.py:144
  19.9 0.7 copy-start.4
  19.9 0.9 copy-start
  20.8 4.2 %copy-start.8 = (s32[1,2,16,3]{2,1,3,0:T(2,128)S(1)}, s32[1,2,16,3]{2,1,3,0:T(2,128)}, u32[]{:S(2)}) copy-start(s32[1,2,16,3]{2,1,3,0:T(2,128)} %param.12) | copy-start | bytes 1156
  20.8 4.2 %copy-start.9 = (s32[1,2]{1,0:T(1,128)S(1)}, s32[1,2]{1,0:T(1,128)}, u32[]{:S(2)}) copy-start(s32[1,2]{1,0:T(1,128)} %param.13) | copy-start | bytes 28
  20.8 4.4 %copy-start.5 = (bf16[16,16,512]{2,1,0:T(8,128)(2,1)S(1)}, bf16[16,16,512]{2,1,0:T(8,128)(2,1)}, u32[]{:S(2)}) copy-start(bf16[16,16,512]{2,1,0:T(8,128)(2,1)} %copy-done.4) | copy-start | bytes 786436
  20.8 23.5 %all-to-all-start.1 = ((bf16[8,384,256]{2,1,0:T(8,128)(2,1)}), bf16[8,384,256]{2,1,0:T(8,128)(2,1)S(1)}, u32[]{:S(2)}, u32[]{:S(2)}) async-start(bf16[8,384,256]{2,1,0:T(8,128)(2,1)} %hold.1), calls=%async_computation.1 | async-start | bytes 3145728 | tf_op jit(solution)/shard_map/all_to_all | solution.py:430
  25.2 10.4 %collective-permute-start.3 = (bf16[2,128,512]{2,1,0:T(8,128)(2,1)S(1)}, bf16[2,128,512]{2,1,0:T(8,128)(2,1)S(1)}, u32[]{:S(2)}, u32[]{:S(2)}) collective-permute-start(bf16[2,128,512]{2,1,0:T(8,128)(2,1)S(1)} %bitcast.24), channel_id=1, source_target_pairs={{0,32},{32,64},{64,96},{96,0},{1,33},{33,65},{65,97},{97,1},{2,34}... | collective-permute-start | bytes 786440 | tf_op jit(solution)/shard_map/ppermute | solution.py:145
  27.1 13.8 %collective-permute-start.4 = (bf16[2,128,512]{2,1,0:T(8,128)(2,1)S(1)}, bf16[2,128,512]{2,1,0:T(8,128)(2,1)S(1)}, u32[]{:S(2)}, u32[]{:S(2)}) collective-permute-start(bf16[2,128,512]{2,1,0:T(8,128)(2,1)S(1)} %bitcast.25), channel_id=1, source_target_pairs={{0,64},{32,96},{64,0},{96,32},{1,65},{33,97},{65,1},{97,33},{2,66}... | collective-permute-start | bytes 786440 | tf_op jit(solution)/shard_map/ppermute | solution.py:145
  30.7 10.3 %collective-permute-start.5 = (bf16[2,128,512]{2,1,0:T(8,128)(2,1)S(1)}, bf16[2,128,512]{2,1,0:T(8,128)(2,1)S(1)}, u32[]{:S(2)}, u32[]{:S(2)}) collective-permute-start(bf16[2,128,512]{2,1,0:T(8,128)(2,1)S(1)} %bitcast.26), channel_id=1, source_target_pairs={{0,96},{32,0},{64,32},{96,64},{1,97},{33,1},{65,33},{97,65},{2,98}... | collective-permute-start | bytes 786440 | tf_op jit(solution)/shard_map/ppermute | solution.py:145
  42.6 7.6 %copy-start.1 = (bf16[128,2048]{1,0:T(8,128)(2,1)S(1)}, bf16[128,2048]{1,0:T(8,128)(2,1)}, u32[]{:S(2)}) copy-start(bf16[128,2048]{1,0:T(8,128)(2,1)} %copy-done) | copy-start | bytes 1572868
  42.6 12.6 %collective-permute-start.6 = (bf16[4,2,128,512]{3,2,1,0:T(8,128)(2,1)}, bf16[4,2,128,512]{3,2,1,0:T(8,128)(2,1)}, u32[]{:S(2)}, u32[]{:S(2)}) collective-permute-start(bf16[4,2,128,512]{3,2,1,0:T(8,128)(2,1)} %place_z.1.refs_1_), channel_id=1, source_target_pairs={{0,8},{8,0},{1,9},{9,1},{2,10},{10,2},{3,11},{11,3},{4,12},{12,4},... | collective-permute-start | bytes 3145736 | tf_op jit(solution)/shard_map/ppermute | solution.py:87
  44.3 4.2 %copy-start.2 = (bf16[8,384,256]{2,1,0:T(8,128)(2,1)}, bf16[8,384,256]{2,1,0:T(8,128)(2,1)S(1)}, u32[]{:S(2)}) copy-start(bf16[8,384,256]{2,1,0:T(8,128)(2,1)S(1)} %all-to-all-done.1.qkv_ref) | copy-start | bytes 4718596
  48.6 8.3 %collective-permute-start.2 = (bf16[512,256]{1,0:T(8,128)(2,1)S(1)}, bf16[512,256]{1,0:T(8,128)(2,1)S(1)}, u32[]{:S(2)}, u32[]{:S(2)}) collective-permute-start(bf16[512,256]{1,0:T(8,128)(2,1)S(1)} %constant_dynamic-slice_fusion), channel_id=1, source_target_pairs={{0,4},{4,0},{1,5},{5,1},{2,6},{6,2},{3,7},{7,3},{8,12},{12,8},{9,1... | collective-permute-start | bytes 786440 | tf_op jit(solution)/shard_map/ppermute | solution.py:87
  52.0 12.6 %collective-permute-start.7 = (bf16[64,2048]{1,0:T(8,128)(2,1)}, bf16[64,2048]{1,0:T(8,128)(2,1)}, u32[]{:S(2)}, u32[]{:S(2)}) collective-permute-start(bf16[64,2048]{1,0:T(8,128)(2,1)} %get-tuple-element.25), channel_id=1, source_target_pairs={{0,1},{1,2},{2,3},{3,0},{4,5},{5,6},{6,7},{7,4},{8,9},{9,10},{10,1... | collective-permute-start | bytes 786440 | tf_op jit(solution)/shard_map/ppermute | solution.py:163
  52.8 11.7 %collective-permute-start.8 = (bf16[64,2048]{1,0:T(8,128)(2,1)}, bf16[64,2048]{1,0:T(8,128)(2,1)}, u32[]{:S(2)}, u32[]{:S(2)}) collective-permute-start(bf16[64,2048]{1,0:T(8,128)(2,1)} %get-tuple-element.26), channel_id=1, source_target_pairs={{0,3},{1,0},{2,1},{3,2},{4,7},{5,4},{6,5},{7,6},{8,11},{9,8},{10,9... | collective-permute-start | bytes 786440 | tf_op jit(solution)/shard_map/ppermute | solution.py:163
  60.1 38.4 %all-to-all-start.2 = ((bf16[4,128,2048]{2,1,0:T(8,128)(2,1)}), bf16[4,128,2048]{2,1,0:T(8,128)(2,1)}, u32[]{:S(2)}, u32[]{:S(2)}) async-start(bf16[4,128,2048]{2,1,0:T(8,128)(2,1)} %mixed_part.1.refs_8_), calls=%async_computation.2 | async-start | bytes 4194304 | tf_op jit(solution)/shard_map/all_to_all | solution.py:439
  64.6 1.0 copy-start.6
  68.4 3.7 %collective-permute-start.9 = (bf16[4,2,128,512]{3,2,1,0:T(8,128)(2,1)S(1)}, bf16[4,2,128,512]{3,2,1,0:T(8,128)(2,1)S(1)}, u32[]{:S(2)}, u32[]{:S(2)}) collective-permute-start(bf16[4,2,128,512]{3,2,1,0:T(8,128)(2,1)S(1)} %get-tuple-element.28.refs_7_), channel_id=1, source_target_pairs={{0,8},{8,0},{1,9},{9,1},{2,10},{10,2},{3,11},{11,3},{4,12},{12,4},... | collective-permute-start | bytes 3145736 | tf_op jit(solution)/shard_map/ppermute | solution.py:87
  71.0 9.1 %copy-start.3 = (bf16[8,384,256]{2,1,0:T(8,128)(2,1)S(1)}, bf16[8,384,256]{2,1,0:T(8,128)(2,1)}, u32[]{:S(2)}) copy-start(bf16[8,384,256]{2,1,0:T(8,128)(2,1)} %copy-done.2) | copy-start | bytes 4718596
  71.0 9.1 %collective-permute-start.13 = (bf16[512,256]{1,0:T(8,128)(2,1)S(1)}, bf16[512,256]{1,0:T(8,128)(2,1)S(1)}, u32[]{:S(2)}, u32[]{:S(2)}) collective-permute-start(bf16[512,256]{1,0:T(8,128)(2,1)S(1)} %get-tuple-element.34), channel_id=1, source_target_pairs={{0,4},{4,0},{1,5},{5,1},{2,6},{6,2},{3,7},{7,3},{8,12},{12,8},{9,1... | collective-permute-start | bytes 786440 | tf_op jit(solution)/shard_map/ppermute | solution.py:87
  72.9 13.8 %collective-permute-start.10 = (bf16[2,128,512]{2,1,0:T(8,128)(2,1)S(1)}, bf16[2,128,512]{2,1,0:T(8,128)(2,1)S(1)}, u32[]{:S(2)}, u32[]{:S(2)}) collective-permute-start(bf16[2,128,512]{2,1,0:T(8,128)(2,1)S(1)} %get-tuple-element.30), channel_id=1, source_target_pairs={{0,64},{32,96},{64,0},{96,32},{1,65},{33,97},{65,1},{97,33},{2,66}... | collective-permute-start | bytes 786440 | tf_op jit(solution)/shard_map/ppermute | solution.py:283
  76.9 12.3 %collective-permute-start.11 = (bf16[2,128,512]{2,1,0:T(8,128)(2,1)S(1)}, bf16[2,128,512]{2,1,0:T(8,128)(2,1)S(1)}, u32[]{:S(2)}, u32[]{:S(2)}) collective-permute-start(bf16[2,128,512]{2,1,0:T(8,128)(2,1)S(1)} %get-tuple-element.31), channel_id=1, source_target_pairs={{0,32},{32,64},{64,96},{96,0},{1,33},{33,65},{65,97},{97,1},{2,34}... | collective-permute-start | bytes 786440 | tf_op jit(solution)/shard_map/ppermute | solution.py:283
  77.9 12.1 %collective-permute-start.12 = (bf16[2,128,512]{2,1,0:T(8,128)(2,1)S(1)}, bf16[2,128,512]{2,1,0:T(8,128)(2,1)S(1)}, u32[]{:S(2)}, u32[]{:S(2)}) collective-permute-start(bf16[2,128,512]{2,1,0:T(8,128)(2,1)S(1)} %get-tuple-element.32.refs_0_), channel_id=1, source_target_pairs={{0,96},{32,0},{64,32},{96,64},{1,97},{33,1},{65,33},{97,65},{2,98}... | collective-permute-start | bytes 786440 | tf_op jit(solution)/shard_map/ppermute | solution.py:283
  90.6 6.6 %collective-permute-start.14 = (bf16[128,512]{1,0:T(8,128)(2,1)S(1)}, bf16[128,512]{1,0:T(8,128)(2,1)S(1)}, u32[]{:S(2)}, u32[]{:S(2)}) collective-permute-start(bf16[128,512]{1,0:T(8,128)(2,1)S(1)} %get-tuple-element.36), channel_id=1, source_target_pairs={{0,16},{16,0},{1,17},{17,1},{2,18},{18,2},{3,19},{19,3},{4,20},{20... | collective-permute-start | bytes 393224 | tf_op jit(solution)/shard_map/ppermute | solution.py:87
  98.5 25.4 %all-to-all-start.3 = ((bf16[8,416,256]{2,1,0:T(8,128)(2,1)}), bf16[8,416,256]{2,1,0:T(8,128)(2,1)S(1)}, u32[]{:S(2)}, u32[]{:S(2)}) async-start(bf16[8,416,256]{2,1,0:T(8,128)(2,1)} %attach.1), calls=%async_computation.3 | async-start | bytes 3407872 | tf_op jit(solution)/shard_map/all_to_all | solution.py:444
